TPU v7x, 32 devices: a whole 2x2x4 slice. The times are simulated.
32 devices in a mesh: head: 16 (over z, x, core), ctx: 2 (over y).
Axes of the slice: x: 2, y: 2, z: 4, core: 2. Of those that a mesh axis runs over, the one named last changes fastest.
Arguments:
- queries: bfloat16 [4096, 8192], P('ctx', 'head'), may hold values from -6 to 6
- keys: bfloat16 [128, 512], P(('head', 'ctx')), may hold values from -6 to 6
- values: bfloat16 [128, 512], P(('head', 'ctx')), may hold values from -6 to 6
- outputs: bfloat16 [4096, 8192], P('ctx', 'head'), may hold values from -6 to 6
- dout: bfloat16 [4096, 8192], P(('ctx', 'head')), may hold values from -24 to 24
- lse: float32 [64, 4096], P('head', 'ctx'), may hold values from 6.5 to 8.5
Outputs:
- dq: bfloat16 [4096, 8192], P('ctx', 'head')
- dk: bfloat16 [128, 512], P(('head', 'ctx'))
- dv: bfloat16 [128, 512], P(('head', 'ctx'))
All inputs are finite; a program needn't handle non-finite values.
Results may differ from a plain program's by a relative error of at most 0.0052.
Values may be sent and summed in bfloat16 or wider, within the bound.
No kernel may reach another device: no remote copies, remote signals or barrier semaphores. Data moves between devices by JAX's collectives and lax.ppermute only.
A program may use at most 128 MiB of HBM per device.

v0:
```python
import jax
import jax.numpy as jnp
from jax import lax
from jax.sharding import PartitionSpec as P

QUERY_HEADS = 64
KEY_VALUE_HEADS = 4
HEAD_SIZE = 128


def on_device(queries, keys, values, outputs, dout, lse):
    factor = HEAD_SIZE ** (-0.5)
    query_head_index = lax.axis_index("head")
    present_heads = queries.shape[1] // HEAD_SIZE
    key_value_group = query_head_index * present_heads // (QUERY_HEADS // KEY_VALUE_HEADS)
    dout_local = lax.all_to_all(dout, "head", split_axis=1, concat_axis=0, tiled=True)
    full_keys, full_values = (
        lax.all_gather(keys, ("head", "ctx"), axis=0, tiled=True),
        lax.all_gather(values, ("head", "ctx"), axis=0, tiled=True),
    )
    key_group = lax.dynamic_slice_in_dim(full_keys, key_value_group * HEAD_SIZE, HEAD_SIZE, 1)
    value_group = lax.dynamic_slice_in_dim(full_values, key_value_group * HEAD_SIZE, HEAD_SIZE, 1)
    key_total_count = key_group.shape[0]
    query_count = queries.shape[0]
    block_rows = min(query_count, 512)
    dk_sum = jnp.zeros((key_total_count, HEAD_SIZE), jnp.float32)
    dv_sum = jnp.zeros((key_total_count, HEAD_SIZE), jnp.float32)
    dq_heads = []
    for local_head in range(present_heads):
        lower = local_head * HEAD_SIZE
        pieces = []
        for start in range(0, query_count, block_rows):
            q_head = queries[start : start + block_rows, lower : lower + HEAD_SIZE]
            o_head = outputs[start : start + block_rows, lower : lower + HEAD_SIZE]
            d_head = dout_local[start : start + block_rows, lower : lower + HEAD_SIZE]
            l_head = lse[local_head, start : start + block_rows]
            scores = jnp.dot(q_head, key_group.T, preferred_element_type=jnp.float32) * factor
            probs = jnp.exp(scores - l_head[:, None])
            probs_low = probs.astype(jnp.bfloat16)
            dv_sum = dv_sum + jnp.dot(probs_low.T, d_head, preferred_element_type=jnp.float32)
            dprobs = jnp.dot(d_head, value_group.T, preferred_element_type=jnp.float32)
            delta = jnp.sum(d_head.astype(jnp.float32) * o_head.astype(jnp.float32), axis=1)
            dscores = (probs * (dprobs - delta[:, None])).astype(jnp.bfloat16)
            pieces.append(
                (jnp.dot(dscores, key_group, preferred_element_type=jnp.float32) * factor).astype(
                    jnp.bfloat16
                )
            )
            dk_sum = dk_sum + jnp.dot(dscores.T, q_head, preferred_element_type=jnp.float32)
        dq_heads.append(jnp.concatenate(pieces, axis=0))
    dq_local = jnp.concatenate(dq_heads, axis=1)
    empty_buffer = jnp.zeros((key_total_count, KEY_VALUE_HEADS * HEAD_SIZE), jnp.float32)
    padded_k = lax.dynamic_update_slice_in_dim(empty_buffer, dk_sum, key_value_group * HEAD_SIZE, 1)
    padded_v = lax.dynamic_update_slice_in_dim(empty_buffer, dv_sum, key_value_group * HEAD_SIZE, 1)
    dk_local, dv_local = (
        lax.psum_scatter(padded_k, ("head", "ctx"), scatter_dimension=0, tiled=True),
        lax.psum_scatter(padded_v, ("head", "ctx"), scatter_dimension=0, tiled=True),
    )
    return (dq_local, (dk_local * factor).astype(jnp.bfloat16), dv_local.astype(jnp.bfloat16))


def solution(mesh):
    placed = (
        P("ctx", "head"),
        P(("head", "ctx"), None),
        P(("head", "ctx"), None),
        P("ctx", "head"),
        P(("ctx", "head"), None),
        P("head", "ctx"),
    )
    return jax.shard_map(
        on_device,
        mesh=mesh,
        in_specs=placed,
        out_specs=(P("ctx", "head"), P(("head", "ctx"), None), P(("head", "ctx"), None)),
        check_vma=False,
    )
```

profile of v0, /device:TPU:0, one launch (start us, length us, event | category | flops | bytes accessed | tf_op | source)
XLA Modules:
  0.0 357.0 jit_solution(8761453745763745689)
XLA Ops:
  7.2 3.2 copy.10
  10.4 2.6 copy.11
  13.0 7.5 %all-to-all-start = ((bf16[128,16,512]{2,0,1:T(8,128)(2,1)}), bf16[128,16,512]{2,0,1:T(8,128)(2,1)S(1)}, u32[]{:S(2)}, u32[]{:S(2)}) async-start(bf16[128,16,512]{2,0,1:T(8,128)(2,1)} %copy.11), calls=%async_computation | async-start | bytes 4194304 | tf_op jit(solution)/shard_map/all_to_all | solution.py:16
  20.6 97.4 %all-gather = bf16[32,4,512]{2,1,0:T(4,128)(2,1)S(1)} all-gather(bf16[1,4,512]{2,1,0:T(4,128)(2,1)S(1)} %bitcast.105), channel_id=1, replica_groups=mesh['head'=16,'ctx'=2] {'head','ctx'}, dimensions={0}, use_global_device_ids=true | all-gather | bytes 135168 | tf_op jit(solution)/shard_map/all_gather | solution.py:18
  118.0 66.2 %all-gather.1 = bf16[32,4,512]{2,1,0:T(4,128)(2,1)S(1)} all-gather(bf16[1,4,512]{2,1,0:T(4,128)(2,1)S(1)} %bitcast.106), channel_id=1, replica_groups=mesh['head'=16,'ctx'=2] {'head','ctx'}, dimensions={0}, use_global_device_ids=true | all-gather | bytes 135168 | tf_op jit(solution)/shard_map/all_gather | solution.py:19
  184.4 2.0 fusion.47
  186.3 1.8 fusion.44
  188.1 1.8 fusion.41
  190.0 1.8 fusion.38
  191.8 1.8 fusion.35
  193.6 0.9 fusion.32
  194.5 0.9 fusion.29
  195.4 0.9 fusion.26
  196.3 0.9 fusion.23
  197.3 0.9 fusion.20
  198.2 0.9 fusion.17
  199.1 0.9 fusion.14
  200.2 0.2 fusion.8
  200.4 0.2 fusion.5
  200.6 0.2 fusion.2
  200.8 2.2 multiply_reduce_fusion.15
  203.1 1.9 multiply_reduce_fusion.14
  205.6 0.2 fusion.49
  208.8 0.7 copy-done.15
  209.7 0.9 fusion.51
  211.0 0.9 fusion.53
  212.2 0.9 fusion.55
  213.5 0.9 fusion.57
  214.7 0.9 fusion.59
  215.8 0.2 fusion.60
  216.0 0.9 fusion.61
  217.2 0.9 fusion.63
  218.3 0.2 fusion.64
  218.5 0.9 fusion.65
  219.7 0.9 fusion.67
  221.0 0.9 fusion.69
  222.0 0.2 fusion.70
  222.2 0.9 fusion.71
  223.5 0.9 fusion.73
  224.8 0.9 fusion.75
  226.1 0.2 fusion.77
  226.7 0.2 fusion.79
  227.1 0.7 copy-done.14
  227.9 11.3 %maximum_maximum_fusion = bf16[2048,512]{1,0:T(8,128)(2,1)} fusion(bf16[512,128]{1,0:T(8,128)(2,1)S(1)} %fusion.79, bf16[512,128]{1,0:T(8,128)(2,1)S(1)} %fusion.77, bf16[512,128]{1,0:T(8,128)(2,1)S(1)} %copy-done.21, bf16[512,128]{1,0:T(8,128)(2,1)} %fusion.73, bf16[512,128]{1,0:T(8,128)(2,1)} %fusion.71, bf16[512,128]{1,0:T(8,128)(2,1)} %fusion.69, ...), kind=kLoop, calls=%fused_computation | loop fusion | flops 33554432 | bytes 4194304 | tf_op jit(solution)/shard_map/concatenate | solution.py:51
  239.2 39.2 %all-reduce.6 = bf16[128,512]{1,0:T(8,128)(2,1)S(1)} all-reduce(f32[128,512]{1,0:T(8,128)S(1)} %copy-done.16), channel_id=3, replica_groups=mesh['head'=16,'ctx'=2] {'head','ctx'}, use_global_device_ids=true, to_apply=%region_17.18.clone | all-reduce | flops 65536 | bytes 393216
  278.4 0.6 dynamic-slice_convert_fusion
  279.0 69.8 %all-reduce.5.cloned.1.call-done = f32[128,512]{1,0:T(8,128)} async-done(((f32[128,512]{1,0:T(8,128)}), f32[128,512]{1,0:T(8,128)}) %all-reduce.5.cloned.1.call-update) | async-done | bytes 262160
  348.9 1.3 fusion.164
  (102 shorter events, 8.7 us)
Async XLA Ops:
  13.0 7.6 %copy-start.23 = (bf16[4,512]{1,0:T(4,128)(2,1)S(1)}, bf16[4,512]{1,0:T(4,128)(2,1)}, u32[]{:S(2)}) copy-start(bf16[4,512]{1,0:T(4,128)(2,1)} %param.7) | copy-start | bytes 12292
  13.0 105.0 %copy-start.24 = (bf16[4,512]{1,0:T(4,128)(2,1)S(1)}, bf16[4,512]{1,0:T(4,128)(2,1)}, u32[]{:S(2)}) copy-start(bf16[4,512]{1,0:T(4,128)(2,1)} %param.8) | copy-start | bytes 12292
  13.0 171.3 %copy-start.22 = (f32[4,2048]{1,0:T(4,128)S(1)}, f32[4,2048]{1,0:T(4,128)}, u32[]{:S(2)}) copy-start(f32[4,2048]{1,0:T(4,128)} %param.11) | copy-start | bytes 98308
  13.0 187.8 %all-to-all-start = ((bf16[128,16,512]{2,0,1:T(8,128)(2,1)}), bf16[128,16,512]{2,0,1:T(8,128)(2,1)S(1)}, u32[]{:S(2)}, u32[]{:S(2)}) async-start(bf16[128,16,512]{2,0,1:T(8,128)(2,1)} %copy.11), calls=%async_computation | async-start | bytes 4194304 | tf_op jit(solution)/shard_map/all_to_all | solution.py:16
  20.5 328.4 %all-reduce.5.cloned.1.call-start = ((), (), s32[]{:S(2)}) async-start(), calls=%async_computation.1 | async-start | bytes 524288
  184.3 9.3 %copy-start = (bf16[2048,512]{1,0:T(8,128)(2,1)S(1)}, bf16[2048,512]{1,0:T(8,128)(2,1)}, u32[]{:S(2)}) copy-start(bf16[2048,512]{1,0:T(8,128)(2,1)} %param.6) | copy-start | bytes 6291460
  200.8 4.2 %copy-start.13 = (f32[128,512]{1,0:T(8,128)S(1)}, f32[128,512]{1,0:T(8,128)}, u32[]{:S(2)}) copy-start(f32[128,512]{1,0:T(8,128)} %fusion.47) | copy-start | bytes 786436
  200.8 4.6 %copy-start.1 = (bf16[2048,512]{1,0:T(8,128)(2,1)S(1)}, bf16[2048,512]{1,0:T(8,128)(2,1)}, u32[]{:S(2)}) copy-start(bf16[2048,512]{1,0:T(8,128)(2,1)} %param.6) | copy-start | bytes 6291460
  203.0 2.8 copy-start.12
  203.1 3.0 copy-start.11
  203.1 3.2 copy-start.10
  203.1 3.4 copy-start.9
  205.0 1.7 copy-start.8
  205.0 1.9 copy-start.7
  205.2 1.9 copy-start.6
  205.4 1.8 copy-start.5
  205.9 1.6 copy-start.4
  206.1 1.6 copy-start.3
  206.3 1.6 copy-start.2
  208.8 0.7 copy-start.15
  224.6 3.3 copy-start.17
  224.6 3.3 copy-start.18
  224.8 3.1 copy-start.19
  224.8 3.1 copy-start.20
  226.1 1.8 copy-start.21
  227.1 0.7 copy-start.14
  227.9 11.4 %copy-start.16 = (f32[128,512]{1,0:T(8,128)S(1)}, f32[128,512]{1,0:T(8,128)}, u32[]{:S(2)}) copy-start(f32[128,512]{1,0:T(8,128)} %copy-done.15) | copy-start | bytes 786436
Sparse Core Ops, SparseCore 0:
  228.0 120.8 all-reduce.4
where the time goes:
time: 358 us; the launch traced here: 357 us
  blocking collectives  203 us (57%)
  waiting for transfers between devices  69.9 us (20%)
  matrix products  37.2 us (10%)
  other arithmetic  16.7 us (5%)
  between operations  14.9 us (4%)
  local copies, waits for them, and re-layouts  8.05 us (2%)
  starting transfers between devices  7.53 us (2%)
    all_gather x1, blocking collectives, on_device(): lax.all_gather(keys, ('head', 'ctx'), axis=0, tiled=True)  97.4 us
    unnamed x2, waiting for transfers between devices  69.9 us
    all_gather x1, blocking collectives, on_device(): lax.all_gather(values, ('head', 'ctx'), axis=0, tiled=True)  66.2 us
    unnamed x1, blocking collectives  39.2 us
    dot_general x16, matrix products, on_device(): jnp.dot(q_head, key_group.T, preferred_element_type=jnp.float32) * factor  16.4 us
    dot_general x16, matrix products, on_device(): jnp.dot(dscores, key_group, preferred_element_type=jnp.float32) * factor  11.9 us
    concatenate x1, other arithmetic, on_device(): dq_local = jnp.concatenate(dq_heads, axis=1)  11.3 us
    all_to_all x1, starting transfers between devices, on_device(): lax.all_to_all(dout, 'head', split_axis=1, concat_axis=0, tiled=True)  7.49 us
  transfers between devices with their start and end apart: 2, of which 1 were waited for; matrix products, arithmetic and copies ran while one was open for 8% of the time, Pallas kernels for 0%

commit v1 on v0

v1 whole, which is shorter than its diff:
```python
import functools

import jax
import jax.numpy as jnp
from jax import lax
from jax.experimental import pallas as pl
from jax.experimental.pallas import tpu as pltpu
from jax.sharding import PartitionSpec as P

KEY_VALUE_HEADS = 4
HEAD_SIZE = 128
FACTOR = HEAD_SIZE ** (-0.5)
NT = (((1,), (1,)), ((), ()))
TN = (((0,), (0,)), ((), ()))
BATCH = 4
VMEM_LIMIT = 60 * 1024 * 1024
FREE = pl.CostEstimate(flops=0, bytes_accessed=0, transcendentals=0)


def split_kernel(dout_ref, *refs):
    out_refs, (block_ref, in_sems, out_sems) = refs[:-3], refs[-3:]
    width = out_refs[0].shape[1]
    columns = BATCH * width
    me = lax.axis_index("head")
    within = lax.rem(me, BATCH)
    reads, writes = [], []
    groups = list(reversed(range(len(out_refs) // BATCH)))
    for group in groups:
        start = pl.multiple_of((me // BATCH ^ group) * columns, columns)
        reads.append(
            pltpu.make_async_copy(
                dout_ref.at[:, pl.ds(start, columns)], block_ref.at[group], in_sems.at[group]
            )
        )
        reads[-1].start()
    for read, group in zip(reads, groups):
        read.wait()
        for index in range(BATCH):
            distance = group * BATCH + index
            start = pl.multiple_of((within ^ index) * width, width)
            writes.append(
                pltpu.make_async_copy(
                    block_ref.at[group, :, pl.ds(start, width)],
                    out_refs[distance],
                    out_sems.at[distance],
                )
            )
            writes[-1].start()
    for write in writes:
        write.wait()


def split(dout, dests):
    rows, width = dout.shape[0], dout.shape[1] // dests
    groups = dests // BATCH
    return pl.pallas_call(
        split_kernel,
        in_specs=[pl.BlockSpec(memory_space=pl.ANY)],
        out_specs=[pl.BlockSpec(memory_space=pl.ANY)] * dests,
        out_shape=[jax.ShapeDtypeStruct((rows, width), dout.dtype)] * dests,
        scratch_shapes=[
            pltpu.VMEM((groups, rows, BATCH * width), dout.dtype),
            pltpu.SemaphoreType.DMA((groups,)),
            pltpu.SemaphoreType.DMA((dests,)),
        ],
        compiler_params=pltpu.CompilerParams(vmem_limit_bytes=VMEM_LIMIT),
        cost_estimate=FREE,
        name="split",
    )(dout)


def attention_kernel(first, last, pieces, place_ref, *refs):
    d_refs = refs[:pieces]
    q_ref, o_ref, lse_ref, k_ref, v_ref = refs[pieces : pieces + 5]
    refs = refs[pieces + 5 :]
    if not first:
        dk_old, dv_old = refs[1:3]
        refs = refs[3:]
    dq_ref = refs[0]
    if last:
        terms_ref, d_ref, dk_ref, dv_ref = refs[1:]
    else:
        dk_ref, dv_ref, d_ref = refs[1:]
    step = pl.program_id(0)

    @pl.when(step == 0)
    def _():
        if first:
            dk_ref[...] = jnp.zeros_like(dk_ref)
            dv_ref[...] = jnp.zeros_like(dv_ref)
        else:
            dk_ref[...] = dk_old[...]
            dv_ref[...] = dv_old[...]
        rows = d_refs[0].shape[0]
        for index in range(pieces):
            start = (lax.rem(place_ref[0], pieces) ^ index) * rows
            d_ref[pl.ds(pl.multiple_of(start, rows), rows), :] = d_refs[index][...]

    block, width = q_ref.shape
    columns = [slice(start, start + HEAD_SIZE) for start in range(0, width, HEAD_SIZE)]

    def stacked(array):
        return jnp.concatenate([array[:, c] for c in columns], axis=0)

    q, o, k, v = stacked(q_ref), stacked(o_ref), k_ref[...], v_ref[...]
    d = stacked(d_ref[pl.ds(pl.multiple_of(step * block, block), block), :])
    lse = jnp.concatenate([lse_ref[h : h + 1, :] for h in range(len(columns))], axis=1)
    scores = lax.dot_general(k, q, NT, preferred_element_type=jnp.float32) * FACTOR
    probs = jnp.exp(scores - lse)
    product = d.astype(jnp.float32) * o.astype(jnp.float32)
    high = product.astype(jnp.bfloat16)
    low = (product - high.astype(jnp.float32)).astype(jnp.bfloat16)
    minus = jnp.full(v.shape, -1.0, jnp.bfloat16)
    dprobs_less_delta = lax.dot_general(
        jnp.concatenate([v, minus, minus], axis=1),
        jnp.concatenate([d, high, low], axis=1),
        NT,
        preferred_element_type=jnp.float32,
    )
    dscores = (probs * dprobs_less_delta).astype(jnp.bfloat16)
    dq = lax.dot_general(dscores, k, TN, preferred_element_type=jnp.float32) * FACTOR
    for h, c in enumerate(columns):
        dq_ref[:, c] = dq[h * block : (h + 1) * block].astype(jnp.bfloat16)
    dk_ref[...] += jnp.dot(dscores, q, preferred_element_type=jnp.float32)
    dv_ref[...] += jnp.dot(probs.astype(jnp.bfloat16), d, preferred_element_type=jnp.float32)

    if last:

        @pl.when(step == pl.num_programs(0) - 1)
        def _():
            owned = terms_ref.shape[1] // 2
            for owner in range(terms_ref.shape[0]):
                rows = slice(owner * owned, (owner + 1) * owned)
                terms_ref[owner, :owned, :] = dk_ref[rows, :]
                terms_ref[owner, owned:, :] = dv_ref[rows, :]


def attention(start, place, arrived, first, owners, data, carried):
    queries, outputs, lse, k, v = data
    pieces = len(arrived)
    rows, width = arrived[0].shape
    heads = width // HEAD_SIZE
    keys = k.shape[0]
    block, steps = 2 * rows, pieces // 2

    def at(i, place):
        return (place[0] ^ start) // pieces * steps + i

    here = pl.BlockSpec((block, width), lambda i, place: (at(i, place), 0))
    whole = pl.BlockSpec((keys, HEAD_SIZE), lambda i, place: (0, 0))
    in_specs = [pl.BlockSpec((rows, width), lambda i, place: (0, 0))] * pieces + [
        here,
        here,
        pl.BlockSpec((heads, block), lambda i, place: (0, at(i, place))),
        whole,
        whole,
    ]
    operands = [place, *arrived, queries, outputs, lse, k, v]
    aliases = {}
    if not first:
        in_specs += [pl.BlockSpec(memory_space=pl.ANY), whole, whole]
        aliases = {len(operands): 0}
        operands += carried
    out_specs = [here]
    out_shape = [jax.ShapeDtypeStruct(queries.shape, jnp.bfloat16)]
    scratch = [pltpu.VMEM((pieces * rows, width), jnp.bfloat16)]
    if owners:
        terms = (owners, 2 * keys // owners, HEAD_SIZE)
        out_specs += [pl.BlockSpec(terms, lambda i, place: (0, 0, 0))]
        out_shape += [jax.ShapeDtypeStruct(terms, jnp.float32)]
        scratch += [pltpu.VMEM((keys, HEAD_SIZE), jnp.float32)] * 2
    else:
        out_specs += [whole, whole]
        out_shape += [jax.ShapeDtypeStruct((keys, HEAD_SIZE), jnp.float32)] * 2
    return pl.pallas_call(
        functools.partial(attention_kernel, first, owners > 0, pieces),
        grid_spec=pltpu.PrefetchScalarGridSpec(
            num_scalar_prefetch=1,
            grid=(steps,),
            in_specs=in_specs,
            out_specs=out_specs,
            scratch_shapes=scratch,
        ),
        out_shape=out_shape,
        input_output_aliases=aliases,
        compiler_params=pltpu.CompilerParams(vmem_limit_bytes=VMEM_LIMIT),
        cost_estimate=FREE,
        name=f"sources_{start}",
    )(*operands)


def sum_kernel(terms_ref, dk_ref, dv_ref):
    groups = KEY_VALUE_HEADS
    senders = terms_ref.shape[0] // groups
    owned = terms_ref.shape[1] // 2
    for group in range(groups):
        total = terms_ref[group * senders]
        for sender in range(1, senders):
            total = total + terms_ref[group * senders + sender]
        columns = slice(group * HEAD_SIZE, (group + 1) * HEAD_SIZE)
        dk_ref[:, columns] = (total[:owned] * FACTOR).astype(jnp.bfloat16)
        dv_ref[:, columns] = total[owned:].astype(jnp.bfloat16)


def swap(array, axis, size, bits):
    return lax.ppermute(array, axis, [(i, i ^ bits) for i in range(size)])


def after(array, *others):
    return lax.optimization_barrier((array,) + others)[0]


def own_group(keys, values, owners):
    owned = keys.shape[0]
    each = owners // KEY_VALUE_HEADS

    def kernel(k_ref, v_ref, out_ref):
        for group in range(KEY_VALUE_HEADS):
            columns = slice(group * HEAD_SIZE, (group + 1) * HEAD_SIZE)
            both = jnp.concatenate(
                [k_ref[:, columns].astype(jnp.float32), v_ref[:, columns].astype(jnp.float32)],
                axis=0,
            ).astype(keys.dtype)
            for index in range(each):
                out_ref[group * each + index] = both

    mine = pl.pallas_call(
        kernel,
        in_specs=[pl.BlockSpec(memory_space=pltpu.VMEM)] * 2,
        out_shape=jax.ShapeDtypeStruct((owners, 2 * owned, HEAD_SIZE), keys.dtype),
        name="pack_keys",
    )(keys, values)
    got = lax.all_to_all(mine, ("head", "ctx"), split_axis=0, concat_axis=0, tiled=True)
    return got[:, :owned].reshape(-1, HEAD_SIZE), got[:, owned:].reshape(-1, HEAD_SIZE)


def on_device(heads_axis, ctx_axis, queries, keys, values, outputs, dout, lse):
    near = heads_axis // 2
    owners = heads_axis * ctx_axis
    place = lax.axis_index("head").astype(jnp.int32).reshape(1)
    k, v = own_group(keys, values, owners)

    pieces = split(dout, heads_axis)
    arrived = {0: pieces[0]}

    def send(distance, *others):
        piece = after(pieces[distance], *others)
        arrived[distance] = swap(piece, "head", heads_axis, distance)

    data = (queries, outputs, lse, k, v)

    def compute(start, count, carried):
        return attention(
            start,
            place,
            [arrived[distance] for distance in range(start, start + count)],
            start == 0,
            owners if start + count == heads_axis else 0,
            data,
            carried,
        )

    for beside in range(1, near):
        send(beside, *([arrived[beside - 3]] if beside > 3 else []))
    held, carried = list(range(0, near, BATCH)), []
    for distance in range(near, heads_axis):
        gates = [arrived[distance - 3]] if distance >= near + 3 else []
        while held and distance >= heads_axis - (3 if not carried else 0):
            carried = compute(held.pop(0), BATCH, carried)
            gates.append(carried[1])
        if 0 and not carried and distance >= near + 0:
            gates.append(arrived[min(distance - near - 0 + 1, near - 1)])
        send(distance, *gates)
    for start in held + list(range(near, heads_axis - BATCH, BATCH)):
        carried = compute(start, BATCH, carried)
    for start in range(heads_axis - BATCH, heads_axis, 2):
        carried = compute(start, 2, carried)
    dq, terms = carried

    terms = lax.all_to_all(terms, ("head", "ctx"), split_axis=0, concat_axis=0, tiled=True)
    shape = jax.ShapeDtypeStruct(keys.shape, jnp.bfloat16)
    small = pltpu.CompilerParams(vmem_limit_bytes=8 * 1024 * 1024)
    dk, dv = pl.pallas_call(
        sum_kernel, out_shape=[shape, shape], compiler_params=small, name="sum_terms"
    )(terms)
    return dq, dk, dv


def solution(mesh):
    placed = (
        P("ctx", "head"),
        P(("head", "ctx"), None),
        P(("head", "ctx"), None),
        P("ctx", "head"),
        P(("ctx", "head"), None),
        P("head", "ctx"),
    )
    return jax.shard_map(
        functools.partial(on_device, mesh.shape["head"], mesh.shape["ctx"]),
        mesh=mesh,
        in_specs=placed,
        out_specs=(P("ctx", "head"), P(("head", "ctx"), None), P(("head", "ctx"), None)),
        check_vma=False,
    )
```

time: 358 us -> 83 us (0.23)
  blocking collectives: 203 us -> 20.1 us
  waiting for transfers between devices: 69.9 us -> 10.2 us
  matrix products: 37.2 us -> 0 us
  Pallas kernels: 0 us -> 21.1 us
  starting transfers between devices: 7.53 us -> 27.7 us
  other arithmetic: 16.7 us -> 0 us
  between operations: 14.9 us -> 0.85 us
  local copies, waits for them, and re-layouts: 8.05 us -> 2.65 us
    all_gather x2 -> x0, blocking collectives: 164 us -> none  [the longest x1 97.4 us: on_device(): lax.all_gather(keys, ('head', 'ctx'), axis=0, tiled=True)]
    unnamed x2 -> x0, waiting for transfers between devices: 69.9 us -> none
    unnamed x1 -> x0, blocking collectives: 39.2 us -> none
    dot_general x80 -> x0, matrix products: 37.2 us -> none  [the longest x16 16.4 us: on_device(): jnp.dot(q_head, key_group.T, preferred_element_type=jnp.float32) * factor]
    ppermute x0 -> x15, starting transfers between devices: none -> 21.6 us  [swap(): return lax.ppermute(array, axis, [(i, i ^ bits) for i in range(size)])]
    pallas_call x0 -> x8, Pallas kernels: none -> 21.1 us  [the longest x5 16.6 us: attention(): pl.pallas_call(functools.partial(attention_kernel, first, owners > 0, pie...]
    all_to_all x0 -> x1, blocking collectives: none -> 20.1 us  [on_device(): lax.all_to_all(terms, ('head', 'ctx'), split_axis=0, concat_axis=0, tiled...]
    concatenate x1 -> x0, other arithmetic: 11.3 us -> none  [on_device(): dq_local = jnp.concatenate(dq_heads, axis=1)]
  transfers between devices with their start and end apart: 2 -> 16, of which waited for: 1 -> 4; matrix products, arithmetic and copies ran while one was open for 8% -> 1% of each run, Pallas kernels for 0% -> 18%
where the time goes in v1:
time: 83 us; the launch traced here: 82.6 us
  starting transfers between devices  27.7 us (33%)
  Pallas kernels  21.1 us (25%)
  blocking collectives  20.1 us (24%)
  waiting for transfers between devices  10.2 us (12%)
  local copies, waits for them, and re-layouts  2.65 us (3%)
  between operations  0.85 us (1%)
    ppermute x15, starting transfers between devices, swap(): return lax.ppermute(array, axis, [(i, i ^ bits) for i in range(size)])  21.6 us
    all_to_all x1, blocking collectives, on_device(): lax.all_to_all(terms, ('head', 'ctx'), split_axis=0, concat_axis=0, tiled...  20.1 us
    pallas_call x5, Pallas kernels, attention(): pl.pallas_call(functools.partial(attention_kernel, first, owners > 0, pie...  16.6 us
    ppermute x15, waiting for transfers between devices, swap(): return lax.ppermute(array, axis, [(i, i ^ bits) for i in range(size)])  10.2 us
    all_to_all x1, starting transfers between devices, own_group(): lax.all_to_all(mine, ('head', 'ctx'), split_axis=0, concat_axis=0, tiled=...  6.1 us
    pallas_call x1, Pallas kernels, split(): pl.pallas_call(split_kernel, in_specs=[pl.BlockSpec(memory_space=pl.ANY)]...  2.53 us
    unnamed x40, local copies, waits for them, and re-layouts  2.01 us
  transfers between devices with their start and end apart: 16, of which 4 were waited for; matrix products, arithmetic and copies ran while one was open for 1% of the time, Pallas kernels for 18%

profile of v1, /device:TPU:0, one launch (start us, length us, event | category | flops | bytes accessed | tf_op | source)
XLA Modules:
  0.0 82.6 jit_solution(36703913845925186)
XLA Ops:
  0.6 2.5 %split.1 = (bf16[128,512]{1,0:T(8,128)(2,1)}, bf16[128,512]{1,0:T(8,128)(2,1)}, bf16[128,512]{1,0:T(8,128)(2,1)}, bf16[128,512]{1,0:T(8,128)(2,1)}, bf16[128,512...) custom-call(bf16[128,8192]{1,0:T(8,128)(2,1)} %dout_ref.1), custom_call_target="tpu_custom_call" | custom-call | tf_op jit(solution)/shard_map/split/pallas_call | solution.py:56
  3.2 4.1 %collective-permute-start = (bf16[128,512]{1,0:T(8,128)(2,1)}, bf16[128,512]{1,0:T(8,128)(2,1)S(1)}, u32[]{:S(2)}, u32[]{:S(2)}) collective-permute-start(bf16[128,512]{1,0:T(8,128)(2,1)} %get-tuple-element.46), channel_id=1, source_target_pairs={{0,16},{2,18},{4,20},{6,22},{8,24},{10,26},{12,28},{14,30},{16,0},... | collective-permute-start | bytes 393224 | tf_op jit(solution)/shard_map/ppermute | solution.py:206
  7.3 0.0 collective-permute-start.3
  7.3 0.2 collective-permute-start.7
  7.5 1.7 %collective-permute-start.8 = (bf16[128,512]{1,0:T(8,128)(2,1)}, bf16[128,512]{1,0:T(8,128)(2,1)S(1)}, u32[]{:S(2)}, u32[]{:S(2)}) collective-permute-start(bf16[128,512]{1,0:T(8,128)(2,1)} %get-tuple-element.58), channel_id=1, source_target_pairs={{0,4},{2,6},{4,0},{6,2},{8,12},{10,14},{12,8},{14,10},{16,20},{18,... | collective-permute-start | bytes 393224 | tf_op jit(solution)/shard_map/ppermute | solution.py:206
  9.2 0.0 collective-permute-start.9
  9.2 1.3 %pack_keys.1 = bf16[32,8,128]{2,1,0:T(8,128)(2,1)} custom-call(bf16[4,512]{1,0:T(4,128)(2,1)} %k_ref.1, bf16[4,512]{1,0:T(4,128)(2,1)} %v_ref.1), custom_call_target="tpu_custom_call" | custom-call | tf_op jit(solution)/shard_map/pack_keys/pallas_call | solution.py:227
  10.6 6.1 %all-to-all-start = ((bf16[32,8,128]{2,1,0:T(8,128)(2,1)}), bf16[32,8,128]{2,1,0:T(8,128)(2,1)S(1)}, u32[]{:S(2)}, u32[]{:S(2)}) async-start(bf16[32,8,128]{2,1,0:T(8,128)(2,1)} %pack_keys.1), calls=%async_computation | async-start | bytes 131072 | tf_op jit(solution)/shard_map/all_to_all | solution.py:233
  16.7 0.8 collective-permute-done.refs_0_
  17.4 2.9 %collective-permute-start.6 = (bf16[128,512]{1,0:T(8,128)(2,1)}, bf16[128,512]{1,0:T(8,128)(2,1)S(1)}, u32[]{:S(2)}, u32[]{:S(2)}) collective-permute-start(bf16[128,512]{1,0:T(8,128)(2,1)} %get-tuple-element.55), channel_id=1, source_target_pairs={{0,20},{2,22},{4,16},{6,18},{8,28},{10,30},{12,24},{14,26},{16,4},... | collective-permute-start | bytes 393224 | tf_op jit(solution)/shard_map/ppermute | solution.py:206
  20.3 0.0 collective-permute-done.3.refs_1_
  20.3 0.0 collective-permute-start.1
  20.3 0.0 collective-permute-done.7.refs_1_
  20.3 0.0 copy-start.9
  20.4 3.4 %collective-permute-start.4 = (bf16[128,512]{1,0:T(8,128)(2,1)}, bf16[128,512]{1,0:T(8,128)(2,1)S(1)}, u32[]{:S(2)}, u32[]{:S(2)}) collective-permute-start(bf16[128,512]{1,0:T(8,128)(2,1)} %get-tuple-element.52), channel_id=1, source_target_pairs={{0,24},{2,26},{4,28},{6,30},{8,16},{10,18},{12,20},{14,22},{16,8},... | collective-permute-start | bytes 393224 | tf_op jit(solution)/shard_map/ppermute | solution.py:206
  23.7 0.0 collective-permute-done.8.refs_2_
  23.7 1.3 %collective-permute-start.11 = (bf16[128,512]{1,0:T(8,128)(2,1)}, bf16[128,512]{1,0:T(8,128)(2,1)S(1)}, u32[]{:S(2)}, u32[]{:S(2)}) collective-permute-start(bf16[128,512]{1,0:T(8,128)(2,1)} %get-tuple-element.63), channel_id=1, source_target_pairs={{0,8},{2,10},{4,12},{6,14},{8,0},{10,2},{12,4},{14,6},{16,24},{18,... | collective-permute-start | bytes 393224 | tf_op jit(solution)/shard_map/ppermute | solution.py:206
  25.0 0.0 collective-permute-done.9.refs_3_
  25.0 0.5 collective-permute-start.12
  25.5 0.0 all-to-all-done
  25.5 0.6 fusion
  26.2 0.0 copy-done.11
  26.2 3.8 %sources_0.1 = (bf16[2048,512]{1,0:T(8,128)(2,1)}, f32[128,128]{1,0:T(8,128)}, f32[128,128]{1,0:T(8,128)}) custom-call(s32[1]{0:T(128)} %bitcast.place_ref, bf16[128,512]{1,0:T(8,128)(2,1)} %get-tuple-element.56.refs_0_, bf16[128,512]{1,0:T(8,128)(2,1)} %copy-done.9, bf16[128,512]{1,0:T(8,128)(2,1)} %copy-done.10, bf16[128,512]{1,0:T(8,128)(2,1)} %copy-done.11, ...), custom_call_target="tpu_custom_call" | custom-call | tf_op jit(solution)/shard_map/sources_0/pallas_call | solution.py:175
  30.0 4.5 %collective-permute-done.6.refs_2_ = bf16[128,512]{1,0:T(8,128)(2,1)S(1)} collective-permute-done((bf16[128,512]{1,0:T(8,128)(2,1)}, bf16[128,512]{1,0:T(8,128)(2,1)S(1)}, u32[]{:S(2)}, u32[]{:S(2)}) %collective-permute-start.6) | collective-permute-done | bytes 131104 | tf_op jit(solution)/shard_map/ppermute | solution.py:206
  34.5 0.0 collective-permute-start.13
  34.5 3.6 %collective-permute-done.11.refs_0_ = bf16[128,512]{1,0:T(8,128)(2,1)S(1)} collective-permute-done((bf16[128,512]{1,0:T(8,128)(2,1)}, bf16[128,512]{1,0:T(8,128)(2,1)S(1)}, u32[]{:S(2)}, u32[]{:S(2)}) %collective-permute-start.11) | collective-permute-done | bytes 131104 | tf_op jit(solution)/shard_map/ppermute | solution.py:206
  38.2 0.0 collective-permute-start.14
  38.2 0.0 collective-permute-done.1.refs_3_
  38.2 2.1 %collective-permute-start.10 = (bf16[128,512]{1,0:T(8,128)(2,1)S(1)}, bf16[128,512]{1,0:T(8,128)(2,1)S(1)}, u32[]{:S(2)}, u32[]{:S(2)}) collective-permute-start(bf16[128,512]{1,0:T(8,128)(2,1)S(1)} %copy-done.17), channel_id=1, source_target_pairs={{0,26},{2,24},{4,30},{6,28},{8,18},{10,16},{12,22},{14,20},{16,10}... | collective-permute-start | bytes 393224 | tf_op jit(solution)/shard_map/ppermute | solution.py:206
  40.3 0.0 collective-permute-done.4.refs_0_
  40.3 2.1 %collective-permute-start.2 = (bf16[128,512]{1,0:T(8,128)(2,1)S(1)}, bf16[128,512]{1,0:T(8,128)(2,1)S(1)}, u32[]{:S(2)}, u32[]{:S(2)}) collective-permute-start(bf16[128,512]{1,0:T(8,128)(2,1)S(1)} %copy-done.16), channel_id=1, source_target_pairs={{0,28},{2,30},{4,24},{6,26},{8,20},{10,22},{12,16},{14,18},{16,12}... | collective-permute-start | bytes 393224 | tf_op jit(solution)/shard_map/ppermute | solution.py:206
  42.4 0.0 collective-permute-done.12.refs_1_
  42.4 3.3 %collective-permute-start.5 = (bf16[128,512]{1,0:T(8,128)(2,1)S(1)}, bf16[128,512]{1,0:T(8,128)(2,1)S(1)}, u32[]{:S(2)}, u32[]{:S(2)}) collective-permute-start(bf16[128,512]{1,0:T(8,128)(2,1)S(1)} %copy-done.15), channel_id=1, source_target_pairs={{0,30},{2,28},{4,26},{6,24},{8,22},{10,20},{12,18},{14,16},{16,14}... | collective-permute-start | bytes 393224 | tf_op jit(solution)/shard_map/ppermute | solution.py:206
  45.7 0.0 collective-permute-done.13.refs_2_
  45.7 1.4 %collective-permute-done.14.refs_3_ = bf16[128,512]{1,0:T(8,128)(2,1)S(1)} collective-permute-done((bf16[128,512]{1,0:T(8,128)(2,1)S(1)}, bf16[128,512]{1,0:T(8,128)(2,1)S(1)}, u32[]{:S(2)}, u32[]{:S(2)}) %collective-permute-start.14) | collective-permute-done | bytes 131104 | tf_op jit(solution)/shard_map/ppermute | solution.py:206
  47.1 0.6 copy-done.7
  47.7 3.7 %sources_4.1 = (bf16[2048,512]{1,0:T(8,128)(2,1)}, f32[128,128]{1,0:T(8,128)}, f32[128,128]{1,0:T(8,128)}) custom-call(s32[1]{0:T(128)} %bitcast.place_ref, bf16[128,512]{1,0:T(8,128)(2,1)} %copy-done.4, bf16[128,512]{1,0:T(8,128)(2,1)} %copy-done.5, bf16[128,512]{1,0:T(8,128)(2,1)} %copy-done.6, ...), custom_call_target="tpu_custom_call", output_to_operand_aliasing={{0}: (10, {})} | custom-call | tf_op jit(solution)/shard_map/sources_4/pallas_call | solution.py:175
  51.4 3.7 %sources_8.1 = (bf16[2048,512]{1,0:T(8,128)(2,1)}, f32[128,128]{1,0:T(8,128)}, f32[128,128]{1,0:T(8,128)}) custom-call(s32[1]{0:T(128)} %bitcast.place_ref, bf16[128,512]{1,0:T(8,128)(2,1)} %copy-done, bf16[128,512]{1,0:T(8,128)(2,1)} %copy-done.1, bf16[128,512]{1,0:T(8,128)(2,1)} %copy-done.2, ...), custom_call_target="tpu_custom_call", output_to_operand_aliasing={{0}: (10, {})} | custom-call | tf_op jit(solution)/shard_map/sources_8/pallas_call | solution.py:175
  55.2 0.0 collective-permute-done.10.refs_1_
  55.2 0.6 copy-done.14
  55.8 2.7 %sources_12.1 = (bf16[2048,512]{1,0:T(8,128)(2,1)}, f32[128,128]{1,0:T(8,128)}, f32[128,128]{1,0:T(8,128)}) custom-call(s32[1]{0:T(128)} %bitcast.place_ref, bf16[128,512]{1,0:T(8,128)(2,1)} %copy-done.8, bf16[128,512]{1,0:T(8,128)(2,1)} %copy-done.14, bf16[2048,512]{1,0:T(8,128)(2,1)} %refs_2_.3, ...), custom_call_target="tpu_custom_call", output_to_operand_aliasing={{0}: (8, {})} | custom-call | tf_op jit(solution)/shard_map/sources_12/pallas_call | solution.py:175
  58.5 0.0 collective-permute-done.2.refs_0_
  58.5 0.0 collective-permute-done.5.refs_1_
  58.5 0.6 copy-done.12
  59.1 0.0 copy-done.13
  59.2 2.7 %sources_14.1 = (bf16[2048,512]{1,0:T(8,128)(2,1)}, f32[32,8,128]{2,1,0:T(8,128)}) custom-call(s32[1]{0:T(128)} %bitcast.place_ref, bf16[128,512]{1,0:T(8,128)(2,1)} %copy-done.12, bf16[128,512]{1,0:T(8,128)(2,1)} %copy-done.13, bf16[2048,512]{1,0:T(8,128)(2,1)} %refs_2_.3, bf16[2048,512]{1,0:T(8,128)(2,1)} %refs_3_.3, ...), custom_call_target="tpu_custom_call", output_to_operand_aliasing={{0}: (8, {})} | custom-call | tf_op jit(solution)/shard_map/sources_14/pallas_call | solution.py:175
  61.9 20.1 %all_to_all.10.terms_ref = f32[32,8,128]{2,1,0:T(8,128)S(1)} all-to-all(f32[32,8,128]{2,1,0:T(8,128)} %get-tuple-element.82), channel_id=1, replica_groups=mesh['head'=16,'ctx'=2] {'head','ctx'}, dimensions={0} | all-to-all | bytes 262144 | tf_op jit(solution)/shard_map/all_to_all | solution.py:280
  82.0 0.6 sum_terms.1
  (34 shorter events, 0.1 us)
Async XLA Ops:
  3.2 14.3 %collective-permute-start = (bf16[128,512]{1,0:T(8,128)(2,1)}, bf16[128,512]{1,0:T(8,128)(2,1)S(1)}, u32[]{:S(2)}, u32[]{:S(2)}) collective-permute-start(bf16[128,512]{1,0:T(8,128)(2,1)} %get-tuple-element.46), channel_id=1, source_target_pairs={{0,16},{2,18},{4,20},{6,22},{8,24},{10,26},{12,28},{14,30},{16,0},... | collective-permute-start | bytes 393224 | tf_op jit(solution)/shard_map/ppermute | solution.py:206
  7.3 13.1 %collective-permute-start.3 = (bf16[128,512]{1,0:T(8,128)(2,1)}, bf16[128,512]{1,0:T(8,128)(2,1)S(1)}, u32[]{:S(2)}, u32[]{:S(2)}) collective-permute-start(bf16[128,512]{1,0:T(8,128)(2,1)} %get-tuple-element.51), channel_id=1, source_target_pairs={{0,18},{2,16},{4,22},{6,20},{8,26},{10,24},{12,30},{14,28},{16,2},... | collective-permute-start | bytes 393224 | tf_op jit(solution)/shard_map/ppermute | solution.py:206
  7.3 13.1 %collective-permute-start.7 = (bf16[128,512]{1,0:T(8,128)(2,1)}, bf16[128,512]{1,0:T(8,128)(2,1)S(1)}, u32[]{:S(2)}, u32[]{:S(2)}) collective-permute-start(bf16[128,512]{1,0:T(8,128)(2,1)} %get-tuple-element.57), channel_id=1, source_target_pairs={{0,2},{2,0},{4,6},{6,4},{8,10},{10,8},{12,14},{14,12},{16,18},{18,... | collective-permute-start | bytes 393224 | tf_op jit(solution)/shard_map/ppermute | solution.py:206
  7.5 16.2 %collective-permute-start.8 = (bf16[128,512]{1,0:T(8,128)(2,1)}, bf16[128,512]{1,0:T(8,128)(2,1)S(1)}, u32[]{:S(2)}, u32[]{:S(2)}) collective-permute-start(bf16[128,512]{1,0:T(8,128)(2,1)} %get-tuple-element.58), channel_id=1, source_target_pairs={{0,4},{2,6},{4,0},{6,2},{8,12},{10,14},{12,8},{14,10},{16,20},{18,... | collective-permute-start | bytes 393224 | tf_op jit(solution)/shard_map/ppermute | solution.py:206
  9.2 15.8 %collective-permute-start.9 = (bf16[128,512]{1,0:T(8,128)(2,1)}, bf16[128,512]{1,0:T(8,128)(2,1)S(1)}, u32[]{:S(2)}, u32[]{:S(2)}) collective-permute-start(bf16[128,512]{1,0:T(8,128)(2,1)} %get-tuple-element.59), channel_id=1, source_target_pairs={{0,6},{2,4},{4,2},{6,0},{8,14},{10,12},{12,10},{14,8},{16,22},{18,... | collective-permute-start | bytes 393224 | tf_op jit(solution)/shard_map/ppermute | solution.py:206
  10.6 15.0 %all-to-all-start = ((bf16[32,8,128]{2,1,0:T(8,128)(2,1)}), bf16[32,8,128]{2,1,0:T(8,128)(2,1)S(1)}, u32[]{:S(2)}, u32[]{:S(2)}) async-start(bf16[32,8,128]{2,1,0:T(8,128)(2,1)} %pack_keys.1), calls=%async_computation | async-start | bytes 131072 | tf_op jit(solution)/shard_map/all_to_all | solution.py:233
  17.4 12.6 %copy-start = (bf16[128,512]{1,0:T(8,128)(2,1)}, bf16[128,512]{1,0:T(8,128)(2,1)S(1)}, u32[]{:S(2)}) copy-start(bf16[128,512]{1,0:T(8,128)(2,1)S(1)} %collective-permute-done.refs_0_) | copy-start | bytes 393220
  17.4 17.1 %collective-permute-start.6 = (bf16[128,512]{1,0:T(8,128)(2,1)}, bf16[128,512]{1,0:T(8,128)(2,1)S(1)}, u32[]{:S(2)}, u32[]{:S(2)}) collective-permute-start(bf16[128,512]{1,0:T(8,128)(2,1)} %get-tuple-element.55), channel_id=1, source_target_pairs={{0,20},{2,22},{4,16},{6,18},{8,28},{10,30},{12,24},{14,26},{16,4},... | collective-permute-start | bytes 393224 | tf_op jit(solution)/shard_map/ppermute | solution.py:206
  20.3 9.7 %copy-start.1 = (bf16[128,512]{1,0:T(8,128)(2,1)}, bf16[128,512]{1,0:T(8,128)(2,1)S(1)}, u32[]{:S(2)}) copy-start(bf16[128,512]{1,0:T(8,128)(2,1)S(1)} %collective-permute-done.3.refs_1_) | copy-start | bytes 393220
  20.3 17.8 %collective-permute-start.1 = (bf16[128,512]{1,0:T(8,128)(2,1)}, bf16[128,512]{1,0:T(8,128)(2,1)S(1)}, u32[]{:S(2)}, u32[]{:S(2)}) collective-permute-start(bf16[128,512]{1,0:T(8,128)(2,1)} %get-tuple-element.47), channel_id=1, source_target_pairs={{0,22},{2,20},{4,18},{6,16},{8,30},{10,28},{12,26},{14,24},{16,6},... | collective-permute-start | bytes 393224 | tf_op jit(solution)/shard_map/ppermute | solution.py:206
  20.3 5.8 %copy-start.9 = (bf16[128,512]{1,0:T(8,128)(2,1)}, bf16[128,512]{1,0:T(8,128)(2,1)S(1)}, u32[]{:S(2)}) copy-start(bf16[128,512]{1,0:T(8,128)(2,1)S(1)} %collective-permute-done.7.refs_1_) | copy-start | bytes 393220
  20.4 19.9 %collective-permute-start.4 = (bf16[128,512]{1,0:T(8,128)(2,1)}, bf16[128,512]{1,0:T(8,128)(2,1)S(1)}, u32[]{:S(2)}, u32[]{:S(2)}) collective-permute-start(bf16[128,512]{1,0:T(8,128)(2,1)} %get-tuple-element.52), channel_id=1, source_target_pairs={{0,24},{2,26},{4,28},{6,30},{8,16},{10,18},{12,20},{14,22},{16,8},... | collective-permute-start | bytes 393224 | tf_op jit(solution)/shard_map/ppermute | solution.py:206
  23.7 2.5 %copy-start.10 = (bf16[128,512]{1,0:T(8,128)(2,1)}, bf16[128,512]{1,0:T(8,128)(2,1)S(1)}, u32[]{:S(2)}) copy-start(bf16[128,512]{1,0:T(8,128)(2,1)S(1)} %collective-permute-done.8.refs_2_) | copy-start | bytes 393220
  23.7 14.5 %collective-permute-start.11 = (bf16[128,512]{1,0:T(8,128)(2,1)}, bf16[128,512]{1,0:T(8,128)(2,1)S(1)}, u32[]{:S(2)}, u32[]{:S(2)}) collective-permute-start(bf16[128,512]{1,0:T(8,128)(2,1)} %get-tuple-element.63), channel_id=1, source_target_pairs={{0,8},{2,10},{4,12},{6,14},{8,0},{10,2},{12,4},{14,6},{16,24},{18,... | collective-permute-start | bytes 393224 | tf_op jit(solution)/shard_map/ppermute | solution.py:206
  25.0 1.1 %copy-start.11 = (bf16[128,512]{1,0:T(8,128)(2,1)}, bf16[128,512]{1,0:T(8,128)(2,1)S(1)}, u32[]{:S(2)}) copy-start(bf16[128,512]{1,0:T(8,128)(2,1)S(1)} %collective-permute-done.9.refs_3_) | copy-start | bytes 393220
  25.0 17.4 %collective-permute-start.12 = (bf16[128,512]{1,0:T(8,128)(2,1)}, bf16[128,512]{1,0:T(8,128)(2,1)S(1)}, u32[]{:S(2)}, u32[]{:S(2)}) collective-permute-start(bf16[128,512]{1,0:T(8,128)(2,1)} %get-tuple-element.65), channel_id=1, source_target_pairs={{0,10},{2,8},{4,14},{6,12},{8,2},{10,0},{12,6},{14,4},{16,26},{18,... | collective-permute-start | bytes 393224 | tf_op jit(solution)/shard_map/ppermute | solution.py:206
  26.2 8.4 %copy-start.19 = (bf16[128,512]{1,0:T(8,128)(2,1)S(1)}, bf16[128,512]{1,0:T(8,128)(2,1)}, u32[]{:S(2)}) copy-start(bf16[128,512]{1,0:T(8,128)(2,1)} %get-tuple-element.67) | copy-start | bytes 393220
  26.2 12.0 %copy-start.18 = (bf16[128,512]{1,0:T(8,128)(2,1)S(1)}, bf16[128,512]{1,0:T(8,128)(2,1)}, u32[]{:S(2)}) copy-start(bf16[128,512]{1,0:T(8,128)(2,1)} %get-tuple-element.69) | copy-start | bytes 393220
  26.2 12.0 %copy-start.17 = (bf16[128,512]{1,0:T(8,128)(2,1)S(1)}, bf16[128,512]{1,0:T(8,128)(2,1)}, u32[]{:S(2)}) copy-start(bf16[128,512]{1,0:T(8,128)(2,1)} %get-tuple-element.61) | copy-start | bytes 393220
  26.2 14.1 %copy-start.16 = (bf16[128,512]{1,0:T(8,128)(2,1)S(1)}, bf16[128,512]{1,0:T(8,128)(2,1)}, u32[]{:S(2)}) copy-start(bf16[128,512]{1,0:T(8,128)(2,1)} %get-tuple-element.48) | copy-start | bytes 393220
  26.2 16.2 %copy-start.15 = (bf16[128,512]{1,0:T(8,128)(2,1)S(1)}, bf16[128,512]{1,0:T(8,128)(2,1)}, u32[]{:S(2)}) copy-start(bf16[128,512]{1,0:T(8,128)(2,1)} %get-tuple-element.53) | copy-start | bytes 393220
  34.5 16.9 %copy-start.2 = (bf16[128,512]{1,0:T(8,128)(2,1)}, bf16[128,512]{1,0:T(8,128)(2,1)S(1)}, u32[]{:S(2)}) copy-start(bf16[128,512]{1,0:T(8,128)(2,1)S(1)} %collective-permute-done.6.refs_2_) | copy-start | bytes 393220
  34.5 11.2 %collective-permute-start.13 = (bf16[128,512]{1,0:T(8,128)(2,1)S(1)}, bf16[128,512]{1,0:T(8,128)(2,1)S(1)}, u32[]{:S(2)}, u32[]{:S(2)}) collective-permute-start(bf16[128,512]{1,0:T(8,128)(2,1)S(1)} %copy-done.19), channel_id=1, source_target_pairs={{0,12},{2,14},{4,8},{6,10},{8,4},{10,6},{12,0},{14,2},{16,28},{18,... | collective-permute-start | bytes 393224 | tf_op jit(solution)/shard_map/ppermute | solution.py:206
  38.2 8.9 %copy-start.4 = (bf16[128,512]{1,0:T(8,128)(2,1)}, bf16[128,512]{1,0:T(8,128)(2,1)S(1)}, u32[]{:S(2)}) copy-start(bf16[128,512]{1,0:T(8,128)(2,1)S(1)} %collective-permute-done.11.refs_0_) | copy-start | bytes 393220
  38.2 8.9 %collective-permute-start.14 = (bf16[128,512]{1,0:T(8,128)(2,1)S(1)}, bf16[128,512]{1,0:T(8,128)(2,1)S(1)}, u32[]{:S(2)}, u32[]{:S(2)}) collective-permute-start(bf16[128,512]{1,0:T(8,128)(2,1)S(1)} %copy-done.18), channel_id=1, source_target_pairs={{0,14},{2,12},{4,10},{6,8},{8,6},{10,4},{12,2},{14,0},{16,30},{18,... | collective-permute-start | bytes 393224 | tf_op jit(solution)/shard_map/ppermute | solution.py:206
  38.2 13.2 %copy-start.3 = (bf16[128,512]{1,0:T(8,128)(2,1)}, bf16[128,512]{1,0:T(8,128)(2,1)S(1)}, u32[]{:S(2)}) copy-start(bf16[128,512]{1,0:T(8,128)(2,1)S(1)} %collective-permute-done.1.refs_3_) | copy-start | bytes 393220
  38.2 17.0 %collective-permute-start.10 = (bf16[128,512]{1,0:T(8,128)(2,1)S(1)}, bf16[128,512]{1,0:T(8,128)(2,1)S(1)}, u32[]{:S(2)}, u32[]{:S(2)}) collective-permute-start(bf16[128,512]{1,0:T(8,128)(2,1)S(1)} %copy-done.17), channel_id=1, source_target_pairs={{0,26},{2,24},{4,30},{6,28},{8,18},{10,16},{12,22},{14,20},{16,10}... | collective-permute-start | bytes 393224 | tf_op jit(solution)/shard_map/ppermute | solution.py:206
  40.3 14.9 %copy-start.8 = (bf16[128,512]{1,0:T(8,128)(2,1)}, bf16[128,512]{1,0:T(8,128)(2,1)S(1)}, u32[]{:S(2)}) copy-start(bf16[128,512]{1,0:T(8,128)(2,1)S(1)} %collective-permute-done.4.refs_0_) | copy-start | bytes 393220
  40.3 18.2 %collective-permute-start.2 = (bf16[128,512]{1,0:T(8,128)(2,1)S(1)}, bf16[128,512]{1,0:T(8,128)(2,1)S(1)}, u32[]{:S(2)}, u32[]{:S(2)}) collective-permute-start(bf16[128,512]{1,0:T(8,128)(2,1)S(1)} %copy-done.16), channel_id=1, source_target_pairs={{0,28},{2,30},{4,24},{6,26},{8,20},{10,22},{12,16},{14,18},{16,12}... | collective-permute-start | bytes 393224 | tf_op jit(solution)/shard_map/ppermute | solution.py:206
  42.4 4.6 %copy-start.5 = (bf16[128,512]{1,0:T(8,128)(2,1)}, bf16[128,512]{1,0:T(8,128)(2,1)S(1)}, u32[]{:S(2)}) copy-start(bf16[128,512]{1,0:T(8,128)(2,1)S(1)} %collective-permute-done.12.refs_1_) | copy-start | bytes 393220
  42.4 16.1 %collective-permute-start.5 = (bf16[128,512]{1,0:T(8,128)(2,1)S(1)}, bf16[128,512]{1,0:T(8,128)(2,1)S(1)}, u32[]{:S(2)}, u32[]{:S(2)}) collective-permute-start(bf16[128,512]{1,0:T(8,128)(2,1)S(1)} %copy-done.15), channel_id=1, source_target_pairs={{0,30},{2,28},{4,26},{6,24},{8,22},{10,20},{12,18},{14,16},{16,14}... | collective-permute-start | bytes 393224 | tf_op jit(solution)/shard_map/ppermute | solution.py:206
  45.7 1.4 %copy-start.6 = (bf16[128,512]{1,0:T(8,128)(2,1)}, bf16[128,512]{1,0:T(8,128)(2,1)S(1)}, u32[]{:S(2)}) copy-start(bf16[128,512]{1,0:T(8,128)(2,1)S(1)} %collective-permute-done.13.refs_2_) | copy-start | bytes 393220
  47.0 0.6 copy-start.7
  55.2 0.7 copy-start.14
  58.5 0.7 copy-start.12
  58.5 0.7 copy-start.13

commit v2 on v1

--- a/solution.py
+++ b/solution.py
@@ -17,35 +17,44 @@
 FREE = pl.CostEstimate(flops=0, bytes_accessed=0, transcendentals=0)
 
 
-def split_kernel(dout_ref, *refs):
+def batches(heads_axis):
+    near = heads_axis // 2
+    found = [(far, heads_axis - BATCH - far) for far in range(near, heads_axis, BATCH)]
+    return found + [(odd, even) for even, odd in found]
+
+
+def by_place(pair, odd):
+    return pair[0] + odd * (pair[1] - pair[0])
+
+
+def sent_distance(bases, index, odd):
+    return by_place(bases, odd ^ (index % 2)) + index
+
+
+def split_kernel(all_bases, dout_ref, *refs):
     out_refs, (block_ref, in_sems, out_sems) = refs[:-3], refs[-3:]
     width = out_refs[0].shape[1]
     columns = BATCH * width
     me = lax.axis_index("head")
-    within = lax.rem(me, BATCH)
-    reads, writes = [], []
-    groups = list(reversed(range(len(out_refs) // BATCH)))
-    for group in groups:
-        start = pl.multiple_of((me // BATCH ^ group) * columns, columns)
+    reads = []
+    for group in range(block_ref.shape[0]):
         reads.append(
             pltpu.make_async_copy(
-                dout_ref.at[:, pl.ds(start, columns)], block_ref.at[group], in_sems.at[group]
+                dout_ref.at[:, group * columns : (group + 1) * columns],
+                block_ref.at[group],
+                in_sems.at[group],
             )
         )
         reads[-1].start()
-    for read, group in zip(reads, groups):
+    for read in reads:
         read.wait()
-        for index in range(BATCH):
-            distance = group * BATCH + index
-            start = pl.multiple_of((within ^ index) * width, width)
-            writes.append(
-                pltpu.make_async_copy(
-                    block_ref.at[group, :, pl.ds(start, width)],
-                    out_refs[distance],
-                    out_sems.at[distance],
-                )
-            )
-            writes[-1].start()
+    writes = []
+    for place, out_ref in enumerate(out_refs):
+        target = me ^ sent_distance(all_bases[place // BATCH], place % BATCH, lax.rem(me, 2))
+        start = pl.multiple_of(lax.rem(target, BATCH) * width, width)
+        piece = block_ref.at[target // BATCH, :, pl.ds(start, width)]
+        writes.append(pltpu.make_async_copy(piece, out_ref, out_sems.at[place]))
+        writes[-1].start()
     for write in writes:
         write.wait()
 
@@ -54,7 +63,7 @@
     rows, width = dout.shape[0], dout.shape[1] // dests
     groups = dests // BATCH
     return pl.pallas_call(
-        split_kernel,
+        functools.partial(split_kernel, batches(dests)),
         in_specs=[pl.BlockSpec(memory_space=pl.ANY)],
         out_specs=[pl.BlockSpec(memory_space=pl.ANY)] * dests,
         out_shape=[jax.ShapeDtypeStruct((rows, width), dout.dtype)] * dests,
@@ -69,7 +78,8 @@
     )(dout)
 
 
-def attention_kernel(first, last, pieces, place_ref, *refs):
+def attention_kernel(first, last, pairs, place_ref, *refs):
+    pieces = len(pairs)
     d_refs = refs[:pieces]
     q_ref, o_ref, lse_ref, k_ref, v_ref = refs[pieces : pieces + 5]
     refs = refs[pieces + 5 :]
@@ -93,7 +103,8 @@
             dv_ref[...] = dv_old[...]
         rows = d_refs[0].shape[0]
         for index in range(pieces):
-            start = (lax.rem(place_ref[0], pieces) ^ index) * rows
+            distance = by_place(pairs[index], lax.rem(place_ref[0], 2))
+            start = lax.rem(place_ref[0] ^ distance, pieces) * rows
             d_ref[pl.ds(pl.multiple_of(start, rows), rows), :] = d_refs[index][...]
 
     block, width = q_ref.shape
@@ -135,7 +146,7 @@
                 terms_ref[owner, owned:, :] = dv_ref[rows, :]
 
 
-def attention(start, place, arrived, first, owners, data, carried):
+def attention(pairs, place, arrived, first, owners, data, carried):
     queries, outputs, lse, k, v = data
     pieces = len(arrived)
     rows, width = arrived[0].shape
@@ -144,7 +155,7 @@
     block, steps = 2 * rows, pieces // 2
 
     def at(i, place):
-        return (place[0] ^ start) // pieces * steps + i
+        return (place[0] ^ by_place(pairs[0], lax.rem(place[0], 2))) // pieces * steps + i
 
     here = pl.BlockSpec((block, width), lambda i, place: (at(i, place), 0))
     whole = pl.BlockSpec((keys, HEAD_SIZE), lambda i, place: (0, 0))
@@ -173,7 +184,7 @@
         out_specs += [whole, whole]
         out_shape += [jax.ShapeDtypeStruct((keys, HEAD_SIZE), jnp.float32)] * 2
     return pl.pallas_call(
-        functools.partial(attention_kernel, first, owners > 0, pieces),
+        functools.partial(attention_kernel, first, owners > 0, pairs),
         grid_spec=pltpu.PrefetchScalarGridSpec(
             num_scalar_prefetch=1,
             grid=(steps,),
@@ -185,7 +196,7 @@
         input_output_aliases=aliases,
         compiler_params=pltpu.CompilerParams(vmem_limit_bytes=VMEM_LIMIT),
         cost_estimate=FREE,
-        name=f"sources_{start}",
+        name=f"sources_{pairs[0][0]}",
     )(*operands)
 
 
@@ -235,46 +246,50 @@
 
 
 def on_device(heads_axis, ctx_axis, queries, keys, values, outputs, dout, lse):
-    near = heads_axis // 2
     owners = heads_axis * ctx_axis
+    all_bases = batches(heads_axis)
     place = lax.axis_index("head").astype(jnp.int32).reshape(1)
     k, v = own_group(keys, values, owners)
-
     pieces = split(dout, heads_axis)
-    arrived = {0: pieces[0]}
-
-    def send(distance, *others):
-        piece = after(pieces[distance], *others)
-        arrived[distance] = swap(piece, "head", heads_axis, distance)
-
     data = (queries, outputs, lse, k, v)
+    arrived = []
+
+    def send(*gates):
+        batch, index = divmod(len(arrived), BATCH)
+        piece = after(pieces[len(arrived)], *gates)
+        pairs = [
+            (i, i ^ sent_distance(all_bases[batch], index, i % 2)) for i in range(heads_axis)
+        ]
+        arrived.append(lax.ppermute(piece, "head", pairs))
 
     def compute(start, count, carried):
+        pairs = [
+            tuple(base + i % BATCH for base in all_bases[i // BATCH])
+            for i in range(start, start + count)
+        ]
         return attention(
-            start,
+            pairs,
             place,
-            [arrived[distance] for distance in range(start, start + count)],
+            arrived[start : start + count],
             start == 0,
             owners if start + count == heads_axis else 0,
             data,
             carried,
         )
 
-    for beside in range(1, near):
-        send(beside, *([arrived[beside - 3]] if beside > 3 else []))
-    held, carried = list(range(0, near, BATCH)), []
-    for distance in range(near, heads_axis):
-        gates = [arrived[distance - 3]] if distance >= near + 3 else []
-        while held and distance >= heads_axis - (3 if not carried else 0):
-            carried = compute(held.pop(0), BATCH, carried)
+    near = heads_axis // 2
+    carried = []
+    for place_in_order in range(heads_axis):
+        gates = [arrived[place_in_order - 0]] if 0 and place_in_order >= 0 else []
+        if 5 and place_in_order == near + 5:
+            carried = compute(0, near, carried)
+        if 5 and place_in_order >= near + 5:
             gates.append(carried[1])
-        if 0 and not carried and distance >= near + 0:
-            gates.append(arrived[min(distance - near - 0 + 1, near - 1)])
-        send(distance, *gates)
-    for start in held + list(range(near, heads_axis - BATCH, BATCH)):
-        carried = compute(start, BATCH, carried)
-    for start in range(heads_axis - BATCH, heads_axis, 2):
-        carried = compute(start, 2, carried)
+        send(*gates)
+    if not carried:
+        carried = compute(0, near, carried)
+    for start in range(near, heads_axis, 4):
+        carried = compute(start, 4, carried)
     dq, terms = carried
 
     terms = lax.all_to_all(terms, ("head", "ctx"), split_axis=0, concat_axis=0, tiled=True)

time: 83 us -> 74.5 us (0.90)
  starting transfers between devices: 27.7 us -> 38.1 us
  waiting for transfers between devices: 10.2 us -> 0.72 us
  blocking collectives: 20.1 us -> 13.9 us
  Pallas kernels: 21.1 us -> 18.4 us
    ppermute x15 -> x16, starting transfers between devices: 21.6 us -> 32.3 us  [send(): arrived.append(lax.ppermute(piece, 'head', pairs))]
    ppermute x15 -> x16, waiting for transfers between devices: 10.2 us -> 0.72 us  [send(): arrived.append(lax.ppermute(piece, 'head', pairs))]
    all_to_all x1, blocking collectives: 20.1 us -> 13.9 us  [on_device(): lax.all_to_all(terms, ('head', 'ctx'), split_axis=0, concat_axis=0, tiled...]
    pallas_call x6 -> x4, Pallas kernels: 19.1 us -> 16.4 us  [the longest x3 13.4 us: attention(): pl.pallas_call(functools.partial(attention_kernel, first, owners > 0, pai...]
    unnamed x40 -> x38, local copies, waits for them, and re-layouts: 2.01 us -> 1.34 us
  transfers between devices with their start and end apart: 16 -> 17, of which waited for: 4 -> 3; matrix products, arithmetic and copies ran while one was open for 1% -> 1% of each run, Pallas kernels for 18% -> 15%
where the time goes in v2:
time: 74.5 us; the launch traced here: 74 us
  starting transfers between devices  38.1 us (51%)
  Pallas kernels  18.4 us (25%)
  blocking collectives  13.9 us (19%)
  local copies, waits for them, and re-layouts  1.99 us (3%)
  between operations  0.89 us (1%)
    ppermute x16, starting transfers between devices, send(): arrived.append(lax.ppermute(piece, 'head', pairs))  32.3 us
    all_to_all x1, blocking collectives, on_device(): lax.all_to_all(terms, ('head', 'ctx'), split_axis=0, concat_axis=0, tiled...  13.9 us
    pallas_call x3, Pallas kernels, attention(): pl.pallas_call(functools.partial(attention_kernel, first, owners > 0, pai...  13.4 us
    all_to_all x1, starting transfers between devices, own_group(): lax.all_to_all(mine, ('head', 'ctx'), split_axis=0, concat_axis=0, tiled=...  5.78 us
    pallas_call x1, Pallas kernels, split(): pl.pallas_call(functools.partial(split_kernel, batches(dests)), in_specs=...  2.99 us
  transfers between devices with their start and end apart: 17, of which 3 were waited for; matrix products, arithmetic and copies ran while one was open for 1% of the time, Pallas kernels for 15%

profile of v2, /device:TPU:0, one launch (start us, length us, event | category | flops | bytes accessed | tf_op | source)
XLA Modules:
  0.0 74.0 jit_solution(8763722091832241740)
XLA Ops:
  0.6 3.0 %split.1 = (bf16[128,512]{1,0:T(8,128)(2,1)}, bf16[128,512]{1,0:T(8,128)(2,1)}, bf16[128,512]{1,0:T(8,128)(2,1)}, bf16[128,512]{1,0:T(8,128)(2,1)}, bf16[128,512...) custom-call(bf16[128,8192]{1,0:T(8,128)(2,1)} %dout_ref.1), custom_call_target="tpu_custom_call" | custom-call | tf_op jit(solution)/shard_map/split/pallas_call | solution.py:65
  3.6 4.1 %collective-permute-start.1 = (bf16[128,512]{1,0:T(8,128)(2,1)}, bf16[128,512]{1,0:T(8,128)(2,1)S(1)}, u32[]{:S(2)}, u32[]{:S(2)}) collective-permute-start(bf16[128,512]{1,0:T(8,128)(2,1)} %get-tuple-element.34), channel_id=1, source_target_pairs={{0,16},{2,10},{4,20},{6,14},{8,24},{10,2},{12,28},{14,6},{16,0},{1... | collective-permute-start | bytes 393224 | tf_op jit(solution)/shard_map/ppermute | solution.py:263
  7.7 0.0 collective-permute-start.2
  7.7 2.1 %collective-permute-start.3 = (bf16[128,512]{1,0:T(8,128)(2,1)}, bf16[128,512]{1,0:T(8,128)(2,1)S(1)}, u32[]{:S(2)}, u32[]{:S(2)}) collective-permute-start(bf16[128,512]{1,0:T(8,128)(2,1)} %get-tuple-element.36), channel_id=1, source_target_pairs={{0,20},{2,14},{4,16},{6,10},{8,28},{10,6},{12,24},{14,2},{16,4},{1... | collective-permute-start | bytes 393224 | tf_op jit(solution)/shard_map/ppermute | solution.py:263
  9.8 0.5 collective-permute-start.4
  10.3 5.6 %collective-permute-start.5 = (bf16[128,512]{1,0:T(8,128)(2,1)}, bf16[128,512]{1,0:T(8,128)(2,1)S(1)}, u32[]{:S(2)}, u32[]{:S(2)}) collective-permute-start(bf16[128,512]{1,0:T(8,128)(2,1)} %get-tuple-element.38), channel_id=1, source_target_pairs={{0,24},{2,2},{4,28},{6,6},{8,16},{10,10},{12,20},{14,14},{16,8},{1... | collective-permute-start | bytes 393224 | tf_op jit(solution)/shard_map/ppermute | solution.py:263
  15.9 0.0 collective-permute-done.1.refs_0_
  16.0 0.1 collective-permute-start.6
  16.0 1.3 %pack_keys.1 = bf16[32,8,128]{2,1,0:T(8,128)(2,1)} custom-call(bf16[4,512]{1,0:T(4,128)(2,1)} %k_ref.1, bf16[4,512]{1,0:T(4,128)(2,1)} %v_ref.1), custom_call_target="tpu_custom_call" | custom-call | tf_op jit(solution)/shard_map/pack_keys/pallas_call | solution.py:238
  17.4 5.8 %all-to-all-start = ((bf16[32,8,128]{2,1,0:T(8,128)(2,1)}), bf16[32,8,128]{2,1,0:T(8,128)(2,1)S(1)}, u32[]{:S(2)}, u32[]{:S(2)}) async-start(bf16[32,8,128]{2,1,0:T(8,128)(2,1)} %pack_keys.1), calls=%async_computation | async-start | bytes 131072 | tf_op jit(solution)/shard_map/all_to_all | solution.py:244
  23.2 0.0 collective-permute-done.2.refs_1_
  23.2 4.6 %collective-permute-start.7 = (bf16[128,512]{1,0:T(8,128)(2,1)}, bf16[128,512]{1,0:T(8,128)(2,1)S(1)}, u32[]{:S(2)}, u32[]{:S(2)}) collective-permute-start(bf16[128,512]{1,0:T(8,128)(2,1)} %get-tuple-element.40), channel_id=1, source_target_pairs={{0,28},{2,6},{4,24},{6,2},{8,20},{10,14},{12,16},{14,10},{16,12},{... | collective-permute-start | bytes 393224 | tf_op jit(solution)/shard_map/ppermute | solution.py:263
  27.8 0.0 collective-permute-done.3.refs_2_
  27.8 0.0 collective-permute-start.8
  27.8 0.0 collective-permute-done.4.refs_3_
  27.8 0.1 collective-permute-start.12
  27.9 0.0 collective-permute-done.5.refs_4_
  27.9 2.4 %collective-permute-start.13 = (bf16[128,512]{1,0:T(8,128)(2,1)}, bf16[128,512]{1,0:T(8,128)(2,1)S(1)}, u32[]{:S(2)}, u32[]{:S(2)}) collective-permute-start(bf16[128,512]{1,0:T(8,128)(2,1)} %get-tuple-element.49), channel_id=1, source_target_pairs={{0,18},{2,8},{4,22},{6,12},{8,26},{10,0},{12,30},{14,4},{16,2},{18... | collective-permute-start | bytes 393224 | tf_op jit(solution)/shard_map/ppermute | solution.py:263
  30.4 0.0 collective-permute-done.6.refs_5_
  30.4 2.5 %collective-permute-start.14 = (bf16[128,512]{1,0:T(8,128)(2,1)}, bf16[128,512]{1,0:T(8,128)(2,1)S(1)}, u32[]{:S(2)}, u32[]{:S(2)}) collective-permute-start(bf16[128,512]{1,0:T(8,128)(2,1)} %get-tuple-element.50), channel_id=1, source_target_pairs={{0,12},{2,22},{4,8},{6,18},{8,4},{10,30},{12,0},{14,26},{16,28},{1... | collective-permute-start | bytes 393224 | tf_op jit(solution)/shard_map/ppermute | solution.py:263
  32.9 0.0 all-to-all-done
  32.9 0.6 fusion
  33.5 0.0 collective-permute-done.7.refs_6_
  33.5 1.6 %collective-permute-start = (bf16[128,512]{1,0:T(8,128)(2,1)}, bf16[128,512]{1,0:T(8,128)(2,1)S(1)}, u32[]{:S(2)}, u32[]{:S(2)}) collective-permute-start(bf16[128,512]{1,0:T(8,128)(2,1)} %get-tuple-element.32), channel_id=1, source_target_pairs={{0,0},{2,26},{4,4},{6,30},{8,8},{10,18},{12,12},{14,22},{16,16},{1... | collective-permute-start | bytes 393224 | tf_op jit(solution)/shard_map/ppermute | solution.py:263
  35.1 0.2 collective-permute-done.8.refs_7_
  35.3 1.2 %collective-permute-start.15 = (bf16[128,512]{1,0:T(8,128)(2,1)}, bf16[128,512]{1,0:T(8,128)(2,1)S(1)}, u32[]{:S(2)}, u32[]{:S(2)}) collective-permute-start(bf16[128,512]{1,0:T(8,128)(2,1)} %get-tuple-element.51), channel_id=1, source_target_pairs={{0,22},{2,12},{4,18},{6,8},{8,30},{10,4},{12,26},{14,0},{16,6},{18... | collective-permute-start | bytes 393224 | tf_op jit(solution)/shard_map/ppermute | solution.py:263
  36.6 5.9 %sources_8.1 = (bf16[2048,512]{1,0:T(8,128)(2,1)}, f32[128,128]{1,0:T(8,128)}, f32[128,128]{1,0:T(8,128)}) custom-call(s32[1]{0:T(128)} %bitcast.place_ref, bf16[128,512]{1,0:T(8,128)(2,1)} %copy-done.8, bf16[128,512]{1,0:T(8,128)(2,1)} %copy-done.9, bf16[128,512]{1,0:T(8,128)(2,1)} %copy-done.10, bf16[128,512]{1,0:T(8,128)(2,1)} %copy-done.11, ...), custom_call_target="tpu_custom_call" | custom-call | tf_op jit(solution)/shard_map/sources_8/pallas_call | solution.py:186
  42.5 0.0 collective-permute-done.12.refs_0_
  42.5 4.8 %collective-permute-start.9 = (bf16[128,512]{1,0:T(8,128)(2,1)S(1)}, bf16[128,512]{1,0:T(8,128)(2,1)S(1)}, u32[]{:S(2)}, u32[]{:S(2)}) collective-permute-start(bf16[128,512]{1,0:T(8,128)(2,1)S(1)} %copy-done.18), channel_id=1, source_target_pairs={{0,26},{2,0},{4,30},{6,4},{8,18},{10,8},{12,22},{14,12},{16,10},{1... | collective-permute-start | bytes 393224 | tf_op jit(solution)/shard_map/ppermute | solution.py:263
  47.4 0.0 collective-permute-done.13.refs_1_
  47.4 2.2 %collective-permute-start.10 = (bf16[128,512]{1,0:T(8,128)(2,1)S(1)}, bf16[128,512]{1,0:T(8,128)(2,1)S(1)}, u32[]{:S(2)}, u32[]{:S(2)}) collective-permute-start(bf16[128,512]{1,0:T(8,128)(2,1)S(1)} %copy-done.17), channel_id=1, source_target_pairs={{0,4},{2,30},{4,0},{6,26},{8,12},{10,22},{12,8},{14,18},{16,20},{1... | collective-permute-start | bytes 393224 | tf_op jit(solution)/shard_map/ppermute | solution.py:263
  49.6 0.0 collective-permute-done.14.refs_2_
  49.6 0.5 collective-permute-start.11
  50.1 0.0 collective-permute-done.15.refs_3_
  50.1 0.2 copy-done.3
  50.3 0.5 copy-done.5
  50.8 3.7 %sources_4.1 = (bf16[2048,512]{1,0:T(8,128)(2,1)}, f32[128,128]{1,0:T(8,128)}, f32[128,128]{1,0:T(8,128)}) custom-call(s32[1]{0:T(128)} %bitcast.place_ref, bf16[128,512]{1,0:T(8,128)(2,1)} %copy-done, bf16[128,512]{1,0:T(8,128)(2,1)} %copy-done.2, bf16[128,512]{1,0:T(8,128)(2,1)} %copy-done.3, ...), custom_call_target="tpu_custom_call", output_to_operand_aliasing={{0}: (10, {})} | custom-call | tf_op jit(solution)/shard_map/sources_4/pallas_call | solution.py:186
  54.4 0.0 collective-permute-done.refs_0_
  54.5 0.0 collective-permute-done.9.refs_1_
  54.5 0.2 collective-permute-done.10.refs_2_
  54.7 0.3 collective-permute-done.11.refs_3_
  55.0 0.1 copy-done.1
  55.1 0.1 copy-done.4
  55.2 0.2 copy-done.6
  55.3 0.3 copy-done.7
  55.6 3.8 %sources_0.1 = (bf16[2048,512]{1,0:T(8,128)(2,1)}, f32[32,8,128]{2,1,0:T(8,128)}) custom-call(s32[1]{0:T(128)} %bitcast.place_ref, bf16[128,512]{1,0:T(8,128)(2,1)} %copy-done.1, bf16[128,512]{1,0:T(8,128)(2,1)} %copy-done.4, bf16[128,512]{1,0:T(8,128)(2,1)} %copy-done.6, bf16[128,512]{1,0:T(8,128)(2,1)} %copy-done.7, ...), custom_call_target="tpu_custom_call", output_to_operand_aliasing={{0}: (10, {})} | custom-call | tf_op jit(solution)/shard_map/sources_0/pallas_call | solution.py:186
  59.5 13.9 %all_to_all.10.terms_ref = f32[32,8,128]{2,1,0:T(8,128)S(1)} all-to-all(f32[32,8,128]{2,1,0:T(8,128)} %get-tuple-element.58), channel_id=1, replica_groups=mesh['head'=16,'ctx'=2] {'head','ctx'}, dimensions={0} | all-to-all | bytes 262144 | tf_op jit(solution)/shard_map/all_to_all | solution.py:295
  73.4 0.6 sum_terms.1
  (32 shorter events, 0.1 us)
Async XLA Ops:
  3.6 12.3 %collective-permute-start.1 = (bf16[128,512]{1,0:T(8,128)(2,1)}, bf16[128,512]{1,0:T(8,128)(2,1)S(1)}, u32[]{:S(2)}, u32[]{:S(2)}) collective-permute-start(bf16[128,512]{1,0:T(8,128)(2,1)} %get-tuple-element.34), channel_id=1, source_target_pairs={{0,16},{2,10},{4,20},{6,14},{8,24},{10,2},{12,28},{14,6},{16,0},{1... | collective-permute-start | bytes 393224 | tf_op jit(solution)/shard_map/ppermute | solution.py:263
  7.7 15.4 %collective-permute-start.2 = (bf16[128,512]{1,0:T(8,128)(2,1)}, bf16[128,512]{1,0:T(8,128)(2,1)S(1)}, u32[]{:S(2)}, u32[]{:S(2)}) collective-permute-start(bf16[128,512]{1,0:T(8,128)(2,1)} %get-tuple-element.35), channel_id=1, source_target_pairs={{0,10},{2,16},{4,14},{6,20},{8,2},{10,24},{12,6},{14,28},{16,26},{... | collective-permute-start | bytes 393224 | tf_op jit(solution)/shard_map/ppermute | solution.py:263
  7.7 20.0 %collective-permute-start.3 = (bf16[128,512]{1,0:T(8,128)(2,1)}, bf16[128,512]{1,0:T(8,128)(2,1)S(1)}, u32[]{:S(2)}, u32[]{:S(2)}) collective-permute-start(bf16[128,512]{1,0:T(8,128)(2,1)} %get-tuple-element.36), channel_id=1, source_target_pairs={{0,20},{2,14},{4,16},{6,10},{8,28},{10,6},{12,24},{14,2},{16,4},{1... | collective-permute-start | bytes 393224 | tf_op jit(solution)/shard_map/ppermute | solution.py:263
  9.8 17.9 %collective-permute-start.4 = (bf16[128,512]{1,0:T(8,128)(2,1)}, bf16[128,512]{1,0:T(8,128)(2,1)S(1)}, u32[]{:S(2)}, u32[]{:S(2)}) collective-permute-start(bf16[128,512]{1,0:T(8,128)(2,1)} %get-tuple-element.37), channel_id=1, source_target_pairs={{0,14},{2,20},{4,10},{6,16},{8,6},{10,28},{12,2},{14,24},{16,30},{... | collective-permute-start | bytes 393224 | tf_op jit(solution)/shard_map/ppermute | solution.py:263
  10.3 17.6 %collective-permute-start.5 = (bf16[128,512]{1,0:T(8,128)(2,1)}, bf16[128,512]{1,0:T(8,128)(2,1)S(1)}, u32[]{:S(2)}, u32[]{:S(2)}) collective-permute-start(bf16[128,512]{1,0:T(8,128)(2,1)} %get-tuple-element.38), channel_id=1, source_target_pairs={{0,24},{2,2},{4,28},{6,6},{8,16},{10,10},{12,20},{14,14},{16,8},{1... | collective-permute-start | bytes 393224 | tf_op jit(solution)/shard_map/ppermute | solution.py:263
  15.9 20.6 %copy-start.8 = (bf16[128,512]{1,0:T(8,128)(2,1)}, bf16[128,512]{1,0:T(8,128)(2,1)S(1)}, u32[]{:S(2)}) copy-start(bf16[128,512]{1,0:T(8,128)(2,1)S(1)} %collective-permute-done.1.refs_0_) | copy-start | bytes 393220
  16.0 14.4 %collective-permute-start.6 = (bf16[128,512]{1,0:T(8,128)(2,1)}, bf16[128,512]{1,0:T(8,128)(2,1)S(1)}, u32[]{:S(2)}, u32[]{:S(2)}) collective-permute-start(bf16[128,512]{1,0:T(8,128)(2,1)} %get-tuple-element.39), channel_id=1, source_target_pairs={{0,2},{2,24},{4,6},{6,28},{8,10},{10,16},{12,14},{14,20},{16,18},{... | collective-permute-start | bytes 393224 | tf_op jit(solution)/shard_map/ppermute | solution.py:263
  17.4 15.5 %all-to-all-start = ((bf16[32,8,128]{2,1,0:T(8,128)(2,1)}), bf16[32,8,128]{2,1,0:T(8,128)(2,1)S(1)}, u32[]{:S(2)}, u32[]{:S(2)}) async-start(bf16[32,8,128]{2,1,0:T(8,128)(2,1)} %pack_keys.1), calls=%async_computation | async-start | bytes 131072 | tf_op jit(solution)/shard_map/all_to_all | solution.py:244
  23.2 13.3 %copy-start.9 = (bf16[128,512]{1,0:T(8,128)(2,1)}, bf16[128,512]{1,0:T(8,128)(2,1)S(1)}, u32[]{:S(2)}) copy-start(bf16[128,512]{1,0:T(8,128)(2,1)S(1)} %collective-permute-done.2.refs_1_) | copy-start | bytes 393220
  23.2 10.4 %collective-permute-start.7 = (bf16[128,512]{1,0:T(8,128)(2,1)}, bf16[128,512]{1,0:T(8,128)(2,1)S(1)}, u32[]{:S(2)}, u32[]{:S(2)}) collective-permute-start(bf16[128,512]{1,0:T(8,128)(2,1)} %get-tuple-element.40), channel_id=1, source_target_pairs={{0,28},{2,6},{4,24},{6,2},{8,20},{10,14},{12,16},{14,10},{16,12},{... | collective-permute-start | bytes 393224 | tf_op jit(solution)/shard_map/ppermute | solution.py:263
  27.8 8.7 %copy-start.10 = (bf16[128,512]{1,0:T(8,128)(2,1)}, bf16[128,512]{1,0:T(8,128)(2,1)S(1)}, u32[]{:S(2)}) copy-start(bf16[128,512]{1,0:T(8,128)(2,1)S(1)} %collective-permute-done.3.refs_2_) | copy-start | bytes 393220
  27.8 7.5 %collective-permute-start.8 = (bf16[128,512]{1,0:T(8,128)(2,1)}, bf16[128,512]{1,0:T(8,128)(2,1)S(1)}, u32[]{:S(2)}, u32[]{:S(2)}) collective-permute-start(bf16[128,512]{1,0:T(8,128)(2,1)} %get-tuple-element.41), channel_id=1, source_target_pairs={{0,6},{2,28},{4,2},{6,24},{8,14},{10,20},{12,10},{14,16},{16,22},{... | collective-permute-start | bytes 393224 | tf_op jit(solution)/shard_map/ppermute | solution.py:263
  27.8 8.7 %copy-start.11 = (bf16[128,512]{1,0:T(8,128)(2,1)}, bf16[128,512]{1,0:T(8,128)(2,1)S(1)}, u32[]{:S(2)}) copy-start(bf16[128,512]{1,0:T(8,128)(2,1)S(1)} %collective-permute-done.4.refs_3_) | copy-start | bytes 393220
  27.8 14.7 %collective-permute-start.12 = (bf16[128,512]{1,0:T(8,128)(2,1)}, bf16[128,512]{1,0:T(8,128)(2,1)S(1)}, u32[]{:S(2)}, u32[]{:S(2)}) collective-permute-start(bf16[128,512]{1,0:T(8,128)(2,1)} %get-tuple-element.48), channel_id=1, source_target_pairs={{0,8},{2,18},{4,12},{6,22},{8,0},{10,26},{12,4},{14,30},{16,24},{1... | collective-permute-start | bytes 393224 | tf_op jit(solution)/shard_map/ppermute | solution.py:263
  27.9 8.6 %copy-start.12 = (bf16[128,512]{1,0:T(8,128)(2,1)}, bf16[128,512]{1,0:T(8,128)(2,1)S(1)}, u32[]{:S(2)}) copy-start(bf16[128,512]{1,0:T(8,128)(2,1)S(1)} %collective-permute-done.5.refs_4_) | copy-start | bytes 393220
  27.9 19.5 %collective-permute-start.13 = (bf16[128,512]{1,0:T(8,128)(2,1)}, bf16[128,512]{1,0:T(8,128)(2,1)S(1)}, u32[]{:S(2)}, u32[]{:S(2)}) collective-permute-start(bf16[128,512]{1,0:T(8,128)(2,1)} %get-tuple-element.49), channel_id=1, source_target_pairs={{0,18},{2,8},{4,22},{6,12},{8,26},{10,0},{12,30},{14,4},{16,2},{18... | collective-permute-start | bytes 393224 | tf_op jit(solution)/shard_map/ppermute | solution.py:263
  30.4 6.2 %copy-start.13 = (bf16[128,512]{1,0:T(8,128)(2,1)}, bf16[128,512]{1,0:T(8,128)(2,1)S(1)}, u32[]{:S(2)}) copy-start(bf16[128,512]{1,0:T(8,128)(2,1)S(1)} %collective-permute-done.6.refs_5_) | copy-start | bytes 393220
  30.4 19.3 %collective-permute-start.14 = (bf16[128,512]{1,0:T(8,128)(2,1)}, bf16[128,512]{1,0:T(8,128)(2,1)S(1)}, u32[]{:S(2)}, u32[]{:S(2)}) collective-permute-start(bf16[128,512]{1,0:T(8,128)(2,1)} %get-tuple-element.50), channel_id=1, source_target_pairs={{0,12},{2,22},{4,8},{6,18},{8,4},{10,30},{12,0},{14,26},{16,28},{1... | collective-permute-start | bytes 393224 | tf_op jit(solution)/shard_map/ppermute | solution.py:263
  33.5 3.0 %copy-start.14 = (bf16[128,512]{1,0:T(8,128)(2,1)}, bf16[128,512]{1,0:T(8,128)(2,1)S(1)}, u32[]{:S(2)}) copy-start(bf16[128,512]{1,0:T(8,128)(2,1)S(1)} %collective-permute-done.7.refs_6_) | copy-start | bytes 393220
  33.5 20.9 %collective-permute-start = (bf16[128,512]{1,0:T(8,128)(2,1)}, bf16[128,512]{1,0:T(8,128)(2,1)S(1)}, u32[]{:S(2)}, u32[]{:S(2)}) collective-permute-start(bf16[128,512]{1,0:T(8,128)(2,1)} %get-tuple-element.32), channel_id=1, source_target_pairs={{0,0},{2,26},{4,4},{6,30},{8,8},{10,18},{12,12},{14,22},{16,16},{1... | collective-permute-start | bytes 393224 | tf_op jit(solution)/shard_map/ppermute | solution.py:263
  35.3 1.3 %copy-start.15 = (bf16[128,512]{1,0:T(8,128)(2,1)}, bf16[128,512]{1,0:T(8,128)(2,1)S(1)}, u32[]{:S(2)}) copy-start(bf16[128,512]{1,0:T(8,128)(2,1)S(1)} %collective-permute-done.8.refs_7_) | copy-start | bytes 393220
  35.3 14.8 %collective-permute-start.15 = (bf16[128,512]{1,0:T(8,128)(2,1)}, bf16[128,512]{1,0:T(8,128)(2,1)S(1)}, u32[]{:S(2)}, u32[]{:S(2)}) collective-permute-start(bf16[128,512]{1,0:T(8,128)(2,1)} %get-tuple-element.51), channel_id=1, source_target_pairs={{0,22},{2,12},{4,18},{6,8},{8,30},{10,4},{12,26},{14,0},{16,6},{18... | collective-permute-start | bytes 393224 | tf_op jit(solution)/shard_map/ppermute | solution.py:263
  36.6 6.0 %copy-start.18 = (bf16[128,512]{1,0:T(8,128)(2,1)S(1)}, bf16[128,512]{1,0:T(8,128)(2,1)}, u32[]{:S(2)}) copy-start(bf16[128,512]{1,0:T(8,128)(2,1)} %get-tuple-element.43) | copy-start | bytes 393220
  36.6 10.8 %copy-start.17 = (bf16[128,512]{1,0:T(8,128)(2,1)S(1)}, bf16[128,512]{1,0:T(8,128)(2,1)}, u32[]{:S(2)}) copy-start(bf16[128,512]{1,0:T(8,128)(2,1)} %get-tuple-element.45) | copy-start | bytes 393220
  36.6 13.0 %copy-start.16 = (bf16[128,512]{1,0:T(8,128)(2,1)S(1)}, bf16[128,512]{1,0:T(8,128)(2,1)}, u32[]{:S(2)}) copy-start(bf16[128,512]{1,0:T(8,128)(2,1)} %get-tuple-element.47) | copy-start | bytes 393220
  42.5 7.6 %copy-start = (bf16[128,512]{1,0:T(8,128)(2,1)}, bf16[128,512]{1,0:T(8,128)(2,1)S(1)}, u32[]{:S(2)}) copy-start(bf16[128,512]{1,0:T(8,128)(2,1)S(1)} %collective-permute-done.12.refs_0_) | copy-start | bytes 393220
  42.5 11.9 %collective-permute-start.9 = (bf16[128,512]{1,0:T(8,128)(2,1)S(1)}, bf16[128,512]{1,0:T(8,128)(2,1)S(1)}, u32[]{:S(2)}, u32[]{:S(2)}) collective-permute-start(bf16[128,512]{1,0:T(8,128)(2,1)S(1)} %copy-done.18), channel_id=1, source_target_pairs={{0,26},{2,0},{4,30},{6,4},{8,18},{10,8},{12,22},{14,12},{16,10},{1... | collective-permute-start | bytes 393224 | tf_op jit(solution)/shard_map/ppermute | solution.py:263
  47.4 2.7 %copy-start.2 = (bf16[128,512]{1,0:T(8,128)(2,1)}, bf16[128,512]{1,0:T(8,128)(2,1)S(1)}, u32[]{:S(2)}) copy-start(bf16[128,512]{1,0:T(8,128)(2,1)S(1)} %collective-permute-done.13.refs_1_) | copy-start | bytes 393220
  47.4 7.3 %collective-permute-start.10 = (bf16[128,512]{1,0:T(8,128)(2,1)S(1)}, bf16[128,512]{1,0:T(8,128)(2,1)S(1)}, u32[]{:S(2)}, u32[]{:S(2)}) collective-permute-start(bf16[128,512]{1,0:T(8,128)(2,1)S(1)} %copy-done.17), channel_id=1, source_target_pairs={{0,4},{2,30},{4,0},{6,26},{8,12},{10,22},{12,8},{14,18},{16,20},{1... | collective-permute-start | bytes 393224 | tf_op jit(solution)/shard_map/ppermute | solution.py:263
  49.6 0.7 copy-start.3
  49.6 5.4 %collective-permute-start.11 = (bf16[128,512]{1,0:T(8,128)(2,1)S(1)}, bf16[128,512]{1,0:T(8,128)(2,1)S(1)}, u32[]{:S(2)}, u32[]{:S(2)}) collective-permute-start(bf16[128,512]{1,0:T(8,128)(2,1)S(1)} %copy-done.16), channel_id=1, source_target_pairs={{0,30},{2,4},{4,26},{6,0},{8,22},{10,12},{12,18},{14,8},{16,14},{1... | collective-permute-start | bytes 393224 | tf_op jit(solution)/shard_map/ppermute | solution.py:263
  50.1 0.6 copy-start.5
  54.5 0.6 copy-start.1
  54.5 0.7 copy-start.4
  54.7 0.7 copy-start.6
  55.0 0.7 copy-start.7

commit v3 on v2

--- a/solution.py
+++ b/solution.py
@@ -14,6 +14,7 @@
 TN = (((0,), (0,)), ((), ()))
 BATCH = 4
 VMEM_LIMIT = 60 * 1024 * 1024
+SMALL_LIMIT = 24 * 1024 * 1024
 FREE = pl.CostEstimate(flops=0, bytes_accessed=0, transcendentals=0)
 
 
@@ -36,25 +37,29 @@
     width = out_refs[0].shape[1]
     columns = BATCH * width
     me = lax.axis_index("head")
-    reads = []
-    for group in range(block_ref.shape[0]):
-        reads.append(
-            pltpu.make_async_copy(
-                dout_ref.at[:, group * columns : (group + 1) * columns],
-                block_ref.at[group],
-                in_sems.at[group],
-            )
+    mine = me // BATCH
+    half = len(all_bases) // 2
+
+    def read(group):
+        start = pl.multiple_of((mine ^ group) * columns, columns)
+        return pltpu.make_async_copy(
+            dout_ref.at[:, pl.ds(start, columns)], block_ref.at[group], in_sems.at[group]
         )
-        reads[-1].start()
-    for read in reads:
-        read.wait()
+
+    for pair in all_bases[:half]:
+        for base in pair:
+            read(base // BATCH).start()
     writes = []
-    for place, out_ref in enumerate(out_refs):
-        target = me ^ sent_distance(all_bases[place // BATCH], place % BATCH, lax.rem(me, 2))
-        start = pl.multiple_of(lax.rem(target, BATCH) * width, width)
-        piece = block_ref.at[target // BATCH, :, pl.ds(start, width)]
-        writes.append(pltpu.make_async_copy(piece, out_ref, out_sems.at[place]))
-        writes[-1].start()
+    for batch in range(half):
+        for base in all_bases[batch]:
+            read(base // BATCH).wait()
+        for place in (*range(batch * BATCH, (batch + 1) * BATCH),
+                      *range((batch + half) * BATCH, (batch + half + 1) * BATCH)):
+            distance = sent_distance(all_bases[place // BATCH], place % BATCH, lax.rem(me, 2))
+            start = pl.multiple_of(lax.rem(me ^ distance, BATCH) * width, width)
+            piece = block_ref.at[distance // BATCH, :, pl.ds(start, width)]
+            writes.append(pltpu.make_async_copy(piece, out_refs[place], out_sems.at[place]))
+            writes[-1].start()
     for write in writes:
         write.wait()
 
@@ -194,7 +199,9 @@
         ),
         out_shape=out_shape,
         input_output_aliases=aliases,
-        compiler_params=pltpu.CompilerParams(vmem_limit_bytes=VMEM_LIMIT),
+        compiler_params=pltpu.CompilerParams(
+            vmem_limit_bytes=VMEM_LIMIT if first else SMALL_LIMIT
+        ),
         cost_estimate=FREE,
         name=f"sources_{pairs[0][0]}",
     )(*operands)

time: 74.5 us -> 72.4 us (0.972)
  Pallas kernels: 18.4 us -> 15.5 us
  local copies, waits for them, and re-layouts: 1.99 us -> 3.96 us
    pallas_call x3, Pallas kernels: 13.4 us -> 10.8 us  [attention(): pl.pallas_call(functools.partial(attention_kernel, first, owners > 0, pai...]
    unnamed x38 -> x30, local copies, waits for them, and re-layouts: 1.34 us -> 3.32 us
  transfers between devices with their start and end apart: 17 -> 17, of which waited for: 3 -> 1; matrix products, arithmetic and copies ran while one was open for 1% -> 1% of each run, Pallas kernels for 15% -> 13%
where the time goes in v3:
time: 72.4 us; the launch traced here: 71.9 us
  starting transfers between devices  38 us (52%)
  Pallas kernels  15.5 us (21%)
  blocking collectives  13.3 us (18%)
  local copies, waits for them, and re-layouts  3.96 us (5%)
  between operations  0.88 us (1%)
    ppermute x16, starting transfers between devices, send(): arrived.append(lax.ppermute(piece, 'head', pairs))  32.3 us
    all_to_all x1, blocking collectives, on_device(): lax.all_to_all(terms, ('head', 'ctx'), split_axis=0, concat_axis=0, tiled...  13.3 us
    pallas_call x3, Pallas kernels, attention(): pl.pallas_call(functools.partial(attention_kernel, first, owners > 0, pai...  10.8 us
    all_to_all x1, starting transfers between devices, own_group(): lax.all_to_all(mine, ('head', 'ctx'), split_axis=0, concat_axis=0, tiled=...  5.78 us
    unnamed x30, local copies, waits for them, and re-layouts  3.32 us
    pallas_call x1, Pallas kernels, split(): pl.pallas_call(functools.partial(split_kernel, batches(dests)), in_specs=...  2.69 us
  transfers between devices with their start and end apart: 17, of which 1 were waited for; matrix products, arithmetic and copies ran while one was open for 1% of the time, Pallas kernels for 13%

profile of v3, /device:TPU:0, one launch (start us, length us, event | category | flops | bytes accessed | tf_op | source)
XLA Modules:
  0.0 71.9 jit_solution(8046540841657308514)
XLA Ops:
  0.6 2.7 %split.1 = (bf16[128,512]{1,0:T(8,128)(2,1)}, bf16[128,512]{1,0:T(8,128)(2,1)}, bf16[128,512]{1,0:T(8,128)(2,1)}, bf16[128,512]{1,0:T(8,128)(2,1)}, bf16[128,512...) custom-call(bf16[128,8192]{1,0:T(8,128)(2,1)} %dout_ref.1), custom_call_target="tpu_custom_call" | custom-call | tf_op jit(solution)/shard_map/split/pallas_call | solution.py:70
  3.3 4.1 %collective-permute-start.1 = (bf16[128,512]{1,0:T(8,128)(2,1)}, bf16[128,512]{1,0:T(8,128)(2,1)S(1)}, u32[]{:S(2)}, u32[]{:S(2)}) collective-permute-start(bf16[128,512]{1,0:T(8,128)(2,1)} %get-tuple-element.34), channel_id=1, source_target_pairs={{0,16},{2,10},{4,20},{6,14},{8,24},{10,2},{12,28},{14,6},{16,0},{1... | collective-permute-start | bytes 393224 | tf_op jit(solution)/shard_map/ppermute | solution.py:270
  7.4 0.0 collective-permute-start.2
  7.4 2.1 %collective-permute-start.3 = (bf16[128,512]{1,0:T(8,128)(2,1)}, bf16[128,512]{1,0:T(8,128)(2,1)S(1)}, u32[]{:S(2)}, u32[]{:S(2)}) collective-permute-start(bf16[128,512]{1,0:T(8,128)(2,1)} %get-tuple-element.36), channel_id=1, source_target_pairs={{0,20},{2,14},{4,16},{6,10},{8,28},{10,6},{12,24},{14,2},{16,4},{1... | collective-permute-start | bytes 393224 | tf_op jit(solution)/shard_map/ppermute | solution.py:270
  9.5 0.5 collective-permute-start.4
  10.0 5.6 %collective-permute-start.5 = (bf16[128,512]{1,0:T(8,128)(2,1)}, bf16[128,512]{1,0:T(8,128)(2,1)S(1)}, u32[]{:S(2)}, u32[]{:S(2)}) collective-permute-start(bf16[128,512]{1,0:T(8,128)(2,1)} %get-tuple-element.38), channel_id=1, source_target_pairs={{0,24},{2,2},{4,28},{6,6},{8,16},{10,10},{12,20},{14,14},{16,8},{1... | collective-permute-start | bytes 393224 | tf_op jit(solution)/shard_map/ppermute | solution.py:270
  15.6 0.0 collective-permute-done.1.refs_0_
  15.7 0.1 collective-permute-start.6
  15.7 1.3 %pack_keys.1 = bf16[32,8,128]{2,1,0:T(8,128)(2,1)} custom-call(bf16[4,512]{1,0:T(4,128)(2,1)} %k_ref.1, bf16[4,512]{1,0:T(4,128)(2,1)} %v_ref.1), custom_call_target="tpu_custom_call" | custom-call | tf_op jit(solution)/shard_map/pack_keys/pallas_call | solution.py:245
  17.1 5.8 %all-to-all-start = ((bf16[32,8,128]{2,1,0:T(8,128)(2,1)}), bf16[32,8,128]{2,1,0:T(8,128)(2,1)S(1)}, u32[]{:S(2)}, u32[]{:S(2)}) async-start(bf16[32,8,128]{2,1,0:T(8,128)(2,1)} %pack_keys.1), calls=%async_computation | async-start | bytes 131072 | tf_op jit(solution)/shard_map/all_to_all | solution.py:251
  22.9 0.0 collective-permute-done.2.refs_1_
  22.9 4.6 %collective-permute-start.7 = (bf16[128,512]{1,0:T(8,128)(2,1)}, bf16[128,512]{1,0:T(8,128)(2,1)S(1)}, u32[]{:S(2)}, u32[]{:S(2)}) collective-permute-start(bf16[128,512]{1,0:T(8,128)(2,1)} %get-tuple-element.40), channel_id=1, source_target_pairs={{0,28},{2,6},{4,24},{6,2},{8,20},{10,14},{12,16},{14,10},{16,12},{... | collective-permute-start | bytes 393224 | tf_op jit(solution)/shard_map/ppermute | solution.py:270
  27.5 0.0 collective-permute-done.3.refs_2_
  27.5 0.0 collective-permute-start.8
  27.5 0.0 collective-permute-done.4.refs_3_
  27.5 0.1 collective-permute-start.12
  27.6 0.0 collective-permute-done.5.refs_4_
  27.6 2.4 %collective-permute-start.13 = (bf16[128,512]{1,0:T(8,128)(2,1)}, bf16[128,512]{1,0:T(8,128)(2,1)S(1)}, u32[]{:S(2)}, u32[]{:S(2)}) collective-permute-start(bf16[128,512]{1,0:T(8,128)(2,1)} %get-tuple-element.49), channel_id=1, source_target_pairs={{0,18},{2,8},{4,22},{6,12},{8,26},{10,0},{12,30},{14,4},{16,2},{18... | collective-permute-start | bytes 393224 | tf_op jit(solution)/shard_map/ppermute | solution.py:270
  30.0 0.0 collective-permute-done.6.refs_5_
  30.1 2.5 %collective-permute-start.14 = (bf16[128,512]{1,0:T(8,128)(2,1)}, bf16[128,512]{1,0:T(8,128)(2,1)S(1)}, u32[]{:S(2)}, u32[]{:S(2)}) collective-permute-start(bf16[128,512]{1,0:T(8,128)(2,1)} %get-tuple-element.50), channel_id=1, source_target_pairs={{0,12},{2,22},{4,8},{6,18},{8,4},{10,30},{12,0},{14,26},{16,28},{1... | collective-permute-start | bytes 393224 | tf_op jit(solution)/shard_map/ppermute | solution.py:270
  32.6 0.0 all-to-all-done
  32.6 0.6 fusion
  33.2 0.0 collective-permute-done.7.refs_6_
  33.2 1.6 %collective-permute-start = (bf16[128,512]{1,0:T(8,128)(2,1)}, bf16[128,512]{1,0:T(8,128)(2,1)S(1)}, u32[]{:S(2)}, u32[]{:S(2)}) collective-permute-start(bf16[128,512]{1,0:T(8,128)(2,1)} %get-tuple-element.32), channel_id=1, source_target_pairs={{0,0},{2,26},{4,4},{6,30},{8,8},{10,18},{12,12},{14,22},{16,16},{1... | collective-permute-start | bytes 393224 | tf_op jit(solution)/shard_map/ppermute | solution.py:270
  34.8 0.2 collective-permute-done.8.refs_7_
  35.0 1.2 %collective-permute-start.15 = (bf16[128,512]{1,0:T(8,128)(2,1)}, bf16[128,512]{1,0:T(8,128)(2,1)S(1)}, u32[]{:S(2)}, u32[]{:S(2)}) collective-permute-start(bf16[128,512]{1,0:T(8,128)(2,1)} %get-tuple-element.51), channel_id=1, source_target_pairs={{0,22},{2,12},{4,18},{6,8},{8,30},{10,4},{12,26},{14,0},{16,6},{18... | collective-permute-start | bytes 393224 | tf_op jit(solution)/shard_map/ppermute | solution.py:270
  36.2 0.0 copy-start
  36.3 0.0 copy-start.4
  36.3 6.0 %sources_8.1 = (bf16[2048,512]{1,0:T(8,128)(2,1)}, f32[128,128]{1,0:T(8,128)}, f32[128,128]{1,0:T(8,128)}) custom-call(s32[1]{0:T(128)} %bitcast.place_ref, bf16[128,512]{1,0:T(8,128)(2,1)} %copy-done.7, bf16[128,512]{1,0:T(8,128)(2,1)} %copy-done.8, bf16[128,512]{1,0:T(8,128)(2,1)} %copy-done.9, bf16[128,512]{1,0:T(8,128)(2,1)} %copy-done.10, ...), custom_call_target="tpu_custom_call" | custom-call | tf_op jit(solution)/shard_map/sources_8/pallas_call | solution.py:191
  42.3 0.0 collective-permute-done.12.refs_0_
  42.3 4.9 %collective-permute-start.9 = (bf16[128,512]{1,0:T(8,128)(2,1)}, bf16[128,512]{1,0:T(8,128)(2,1)S(1)}, u32[]{:S(2)}, u32[]{:S(2)}) collective-permute-start(bf16[128,512]{1,0:T(8,128)(2,1)} %get-tuple-element.43), channel_id=1, source_target_pairs={{0,26},{2,0},{4,30},{6,4},{8,18},{10,8},{12,22},{14,12},{16,10},{1... | collective-permute-start | bytes 393224 | tf_op jit(solution)/shard_map/ppermute | solution.py:270
  47.1 0.0 collective-permute-done.13.refs_1_
  47.1 2.1 %collective-permute-start.10 = (bf16[128,512]{1,0:T(8,128)(2,1)}, bf16[128,512]{1,0:T(8,128)(2,1)S(1)}, u32[]{:S(2)}, u32[]{:S(2)}) collective-permute-start(bf16[128,512]{1,0:T(8,128)(2,1)} %get-tuple-element.45), channel_id=1, source_target_pairs={{0,4},{2,30},{4,0},{6,26},{8,12},{10,22},{12,8},{14,18},{16,20},{1... | collective-permute-start | bytes 393224 | tf_op jit(solution)/shard_map/ppermute | solution.py:270
  49.3 0.0 collective-permute-done.14.refs_2_
  49.3 0.5 collective-permute-start.11
  49.8 0.0 collective-permute-done.15.refs_3_
  49.8 0.0 copy-start.1
  49.8 1.6 %copy-done.1 = bf16[2048,512]{1,0:T(8,128)(2,1)S(1)} copy-done((bf16[2048,512]{1,0:T(8,128)(2,1)S(1)}, bf16[2048,512]{1,0:T(8,128)(2,1)}, u32[]{:S(2)}) %copy-start.1) | copy-done | bytes 2097176
  51.4 0.8 %copy-done.5 = f32[128,128]{1,0:T(8,128)S(1)} copy-done((f32[128,128]{1,0:T(8,128)S(1)}, f32[128,128]{1,0:T(8,128)}, u32[]{:S(2)}) %copy-start.5) | copy-done | bytes 65560
  52.3 0.8 %copy-done.6 = f32[128,128]{1,0:T(8,128)S(1)} copy-done((f32[128,128]{1,0:T(8,128)S(1)}, f32[128,128]{1,0:T(8,128)}, u32[]{:S(2)}) %copy-start.6) | copy-done | bytes 65560
  53.1 2.3 %sources_4.1 = (bf16[2048,512]{1,0:T(8,128)(2,1)}, f32[128,128]{1,0:T(8,128)S(1)}, f32[128,128]{1,0:T(8,128)S(1)}) custom-call(s32[1]{0:T(128)} %bitcast.place_ref, bf16[128,512]{1,0:T(8,128)(2,1)S(1)} %collective-permute-done.12.refs_0_, bf16[128,512]{1,0:T(8,128)(2,1)S(1)} %collective-permute-done.13.refs_1_, ...), custom_call_target="tpu_custom_call", output_to_operand_aliasing={{0}: (10, {})} | custom-call | tf_op jit(solution)/shard_map/sources_4/pallas_call | solution.py:191
  55.4 0.0 collective-permute-done.refs_0_
  55.4 0.0 collective-permute-done.9.refs_1_
  55.4 0.0 collective-permute-done.10.refs_2_
  55.5 0.0 collective-permute-done.11.refs_3_
  55.5 2.5 %sources_0.1 = (bf16[2048,512]{1,0:T(8,128)(2,1)}, f32[32,8,128]{2,1,0:T(8,128)S(1)}) custom-call(s32[1]{0:T(128)} %bitcast.place_ref, bf16[128,512]{1,0:T(8,128)(2,1)S(1)} %collective-permute-done.refs_0_, bf16[128,512]{1,0:T(8,128)(2,1)S(1)} %collective-permute-done.9.refs_1_, ...), custom_call_target="tpu_custom_call", output_to_operand_aliasing={{0}: (10, {})} | custom-call | tf_op jit(solution)/shard_map/sources_0/pallas_call | solution.py:191
  58.0 13.3 %all_to_all.10.terms_ref = f32[32,8,128]{2,1,0:T(8,128)S(1)} all-to-all(f32[32,8,128]{2,1,0:T(8,128)S(1)} %get-tuple-element.58), channel_id=1, replica_groups=mesh['head'=16,'ctx'=2] {'head','ctx'}, dimensions={0} | all-to-all | bytes 262144 | tf_op jit(solution)/shard_map/all_to_all | solution.py:302
  71.3 0.6 sum_terms.1
  (24 shorter events, 0.0 us)
Async XLA Ops:
  3.3 12.3 %collective-permute-start.1 = (bf16[128,512]{1,0:T(8,128)(2,1)}, bf16[128,512]{1,0:T(8,128)(2,1)S(1)}, u32[]{:S(2)}, u32[]{:S(2)}) collective-permute-start(bf16[128,512]{1,0:T(8,128)(2,1)} %get-tuple-element.34), channel_id=1, source_target_pairs={{0,16},{2,10},{4,20},{6,14},{8,24},{10,2},{12,28},{14,6},{16,0},{1... | collective-permute-start | bytes 393224 | tf_op jit(solution)/shard_map/ppermute | solution.py:270
  7.4 15.4 %collective-permute-start.2 = (bf16[128,512]{1,0:T(8,128)(2,1)}, bf16[128,512]{1,0:T(8,128)(2,1)S(1)}, u32[]{:S(2)}, u32[]{:S(2)}) collective-permute-start(bf16[128,512]{1,0:T(8,128)(2,1)} %get-tuple-element.35), channel_id=1, source_target_pairs={{0,10},{2,16},{4,14},{6,20},{8,2},{10,24},{12,6},{14,28},{16,26},{... | collective-permute-start | bytes 393224 | tf_op jit(solution)/shard_map/ppermute | solution.py:270
  7.4 20.0 %collective-permute-start.3 = (bf16[128,512]{1,0:T(8,128)(2,1)}, bf16[128,512]{1,0:T(8,128)(2,1)S(1)}, u32[]{:S(2)}, u32[]{:S(2)}) collective-permute-start(bf16[128,512]{1,0:T(8,128)(2,1)} %get-tuple-element.36), channel_id=1, source_target_pairs={{0,20},{2,14},{4,16},{6,10},{8,28},{10,6},{12,24},{14,2},{16,4},{1... | collective-permute-start | bytes 393224 | tf_op jit(solution)/shard_map/ppermute | solution.py:270
  9.5 17.9 %collective-permute-start.4 = (bf16[128,512]{1,0:T(8,128)(2,1)}, bf16[128,512]{1,0:T(8,128)(2,1)S(1)}, u32[]{:S(2)}, u32[]{:S(2)}) collective-permute-start(bf16[128,512]{1,0:T(8,128)(2,1)} %get-tuple-element.37), channel_id=1, source_target_pairs={{0,14},{2,20},{4,10},{6,16},{8,6},{10,28},{12,2},{14,24},{16,30},{... | collective-permute-start | bytes 393224 | tf_op jit(solution)/shard_map/ppermute | solution.py:270
  10.0 17.6 %collective-permute-start.5 = (bf16[128,512]{1,0:T(8,128)(2,1)}, bf16[128,512]{1,0:T(8,128)(2,1)S(1)}, u32[]{:S(2)}, u32[]{:S(2)}) collective-permute-start(bf16[128,512]{1,0:T(8,128)(2,1)} %get-tuple-element.38), channel_id=1, source_target_pairs={{0,24},{2,2},{4,28},{6,6},{8,16},{10,10},{12,20},{14,14},{16,8},{1... | collective-permute-start | bytes 393224 | tf_op jit(solution)/shard_map/ppermute | solution.py:270
  15.6 20.5 %copy-start.7 = (bf16[128,512]{1,0:T(8,128)(2,1)}, bf16[128,512]{1,0:T(8,128)(2,1)S(1)}, u32[]{:S(2)}) copy-start(bf16[128,512]{1,0:T(8,128)(2,1)S(1)} %collective-permute-done.1.refs_0_) | copy-start | bytes 393220
  15.7 14.4 %collective-permute-start.6 = (bf16[128,512]{1,0:T(8,128)(2,1)}, bf16[128,512]{1,0:T(8,128)(2,1)S(1)}, u32[]{:S(2)}, u32[]{:S(2)}) collective-permute-start(bf16[128,512]{1,0:T(8,128)(2,1)} %get-tuple-element.39), channel_id=1, source_target_pairs={{0,2},{2,24},{4,6},{6,28},{8,10},{10,16},{12,14},{14,20},{16,18},{... | collective-permute-start | bytes 393224 | tf_op jit(solution)/shard_map/ppermute | solution.py:270
  17.1 15.5 %all-to-all-start = ((bf16[32,8,128]{2,1,0:T(8,128)(2,1)}), bf16[32,8,128]{2,1,0:T(8,128)(2,1)S(1)}, u32[]{:S(2)}, u32[]{:S(2)}) async-start(bf16[32,8,128]{2,1,0:T(8,128)(2,1)} %pack_keys.1), calls=%async_computation | async-start | bytes 131072 | tf_op jit(solution)/shard_map/all_to_all | solution.py:251
  22.9 13.3 %copy-start.8 = (bf16[128,512]{1,0:T(8,128)(2,1)}, bf16[128,512]{1,0:T(8,128)(2,1)S(1)}, u32[]{:S(2)}) copy-start(bf16[128,512]{1,0:T(8,128)(2,1)S(1)} %collective-permute-done.2.refs_1_) | copy-start | bytes 393220
  22.9 10.4 %collective-permute-start.7 = (bf16[128,512]{1,0:T(8,128)(2,1)}, bf16[128,512]{1,0:T(8,128)(2,1)S(1)}, u32[]{:S(2)}, u32[]{:S(2)}) collective-permute-start(bf16[128,512]{1,0:T(8,128)(2,1)} %get-tuple-element.40), channel_id=1, source_target_pairs={{0,28},{2,6},{4,24},{6,2},{8,20},{10,14},{12,16},{14,10},{16,12},{... | collective-permute-start | bytes 393224 | tf_op jit(solution)/shard_map/ppermute | solution.py:270
  27.5 8.7 %copy-start.9 = (bf16[128,512]{1,0:T(8,128)(2,1)}, bf16[128,512]{1,0:T(8,128)(2,1)S(1)}, u32[]{:S(2)}) copy-start(bf16[128,512]{1,0:T(8,128)(2,1)S(1)} %collective-permute-done.3.refs_2_) | copy-start | bytes 393220
  27.5 7.5 %collective-permute-start.8 = (bf16[128,512]{1,0:T(8,128)(2,1)}, bf16[128,512]{1,0:T(8,128)(2,1)S(1)}, u32[]{:S(2)}, u32[]{:S(2)}) collective-permute-start(bf16[128,512]{1,0:T(8,128)(2,1)} %get-tuple-element.41), channel_id=1, source_target_pairs={{0,6},{2,28},{4,2},{6,24},{8,14},{10,20},{12,10},{14,16},{16,22},{... | collective-permute-start | bytes 393224 | tf_op jit(solution)/shard_map/ppermute | solution.py:270
  27.5 8.7 %copy-start.10 = (bf16[128,512]{1,0:T(8,128)(2,1)}, bf16[128,512]{1,0:T(8,128)(2,1)S(1)}, u32[]{:S(2)}) copy-start(bf16[128,512]{1,0:T(8,128)(2,1)S(1)} %collective-permute-done.4.refs_3_) | copy-start | bytes 393220
  27.5 14.8 %collective-permute-start.12 = (bf16[128,512]{1,0:T(8,128)(2,1)}, bf16[128,512]{1,0:T(8,128)(2,1)S(1)}, u32[]{:S(2)}, u32[]{:S(2)}) collective-permute-start(bf16[128,512]{1,0:T(8,128)(2,1)} %get-tuple-element.48), channel_id=1, source_target_pairs={{0,8},{2,18},{4,12},{6,22},{8,0},{10,26},{12,4},{14,30},{16,24},{1... | collective-permute-start | bytes 393224 | tf_op jit(solution)/shard_map/ppermute | solution.py:270
  27.6 8.6 %copy-start.11 = (bf16[128,512]{1,0:T(8,128)(2,1)}, bf16[128,512]{1,0:T(8,128)(2,1)S(1)}, u32[]{:S(2)}) copy-start(bf16[128,512]{1,0:T(8,128)(2,1)S(1)} %collective-permute-done.5.refs_4_) | copy-start | bytes 393220
  27.6 19.5 %collective-permute-start.13 = (bf16[128,512]{1,0:T(8,128)(2,1)}, bf16[128,512]{1,0:T(8,128)(2,1)S(1)}, u32[]{:S(2)}, u32[]{:S(2)}) collective-permute-start(bf16[128,512]{1,0:T(8,128)(2,1)} %get-tuple-element.49), channel_id=1, source_target_pairs={{0,18},{2,8},{4,22},{6,12},{8,26},{10,0},{12,30},{14,4},{16,2},{18... | collective-permute-start | bytes 393224 | tf_op jit(solution)/shard_map/ppermute | solution.py:270
  30.0 6.2 %copy-start.12 = (bf16[128,512]{1,0:T(8,128)(2,1)}, bf16[128,512]{1,0:T(8,128)(2,1)S(1)}, u32[]{:S(2)}) copy-start(bf16[128,512]{1,0:T(8,128)(2,1)S(1)} %collective-permute-done.6.refs_5_) | copy-start | bytes 393220
  30.1 19.2 %collective-permute-start.14 = (bf16[128,512]{1,0:T(8,128)(2,1)}, bf16[128,512]{1,0:T(8,128)(2,1)S(1)}, u32[]{:S(2)}, u32[]{:S(2)}) collective-permute-start(bf16[128,512]{1,0:T(8,128)(2,1)} %get-tuple-element.50), channel_id=1, source_target_pairs={{0,12},{2,22},{4,8},{6,18},{8,4},{10,30},{12,0},{14,26},{16,28},{1... | collective-permute-start | bytes 393224 | tf_op jit(solution)/shard_map/ppermute | solution.py:270
  33.2 3.0 %copy-start.13 = (bf16[128,512]{1,0:T(8,128)(2,1)}, bf16[128,512]{1,0:T(8,128)(2,1)S(1)}, u32[]{:S(2)}) copy-start(bf16[128,512]{1,0:T(8,128)(2,1)S(1)} %collective-permute-done.7.refs_6_) | copy-start | bytes 393220
  33.2 22.2 %collective-permute-start = (bf16[128,512]{1,0:T(8,128)(2,1)}, bf16[128,512]{1,0:T(8,128)(2,1)S(1)}, u32[]{:S(2)}, u32[]{:S(2)}) collective-permute-start(bf16[128,512]{1,0:T(8,128)(2,1)} %get-tuple-element.32), channel_id=1, source_target_pairs={{0,0},{2,26},{4,4},{6,30},{8,8},{10,18},{12,12},{14,22},{16,16},{1... | collective-permute-start | bytes 393224 | tf_op jit(solution)/shard_map/ppermute | solution.py:270
  35.0 1.2 %copy-start.14 = (bf16[128,512]{1,0:T(8,128)(2,1)}, bf16[128,512]{1,0:T(8,128)(2,1)S(1)}, u32[]{:S(2)}) copy-start(bf16[128,512]{1,0:T(8,128)(2,1)S(1)} %collective-permute-done.8.refs_7_) | copy-start | bytes 393220
  35.0 14.8 %collective-permute-start.15 = (bf16[128,512]{1,0:T(8,128)(2,1)}, bf16[128,512]{1,0:T(8,128)(2,1)S(1)}, u32[]{:S(2)}, u32[]{:S(2)}) collective-permute-start(bf16[128,512]{1,0:T(8,128)(2,1)} %get-tuple-element.51), channel_id=1, source_target_pairs={{0,22},{2,12},{4,18},{6,8},{8,30},{10,4},{12,26},{14,0},{16,6},{18... | collective-permute-start | bytes 393224 | tf_op jit(solution)/shard_map/ppermute | solution.py:270
  36.2 13.6 %copy-start = (bf16[2048,512]{1,0:T(8,128)(2,1)S(1)}, bf16[2048,512]{1,0:T(8,128)(2,1)}, u32[]{:S(2)}) copy-start(bf16[2048,512]{1,0:T(8,128)(2,1)} %refs_4_.3) | copy-start | bytes 6291460
  36.3 13.5 %copy-start.2 = (bf16[32,4,128]{2,1,0:T(4,128)(2,1)S(1)}, bf16[32,4,128]{2,1,0:T(4,128)(2,1)}, u32[]{:S(2)}) copy-start(bf16[32,4,128]{2,1,0:T(4,128)(2,1)} %get-tuple-element.61) | copy-start | bytes 98308
  36.3 13.5 %copy-start.3 = (bf16[32,4,128]{2,1,0:T(4,128)(2,1)S(1)}, bf16[32,4,128]{2,1,0:T(4,128)(2,1)}, u32[]{:S(2)}) copy-start(bf16[32,4,128]{2,1,0:T(4,128)(2,1)} %get-tuple-element.62) | copy-start | bytes 98308
  36.3 13.5 %copy-start.4 = (f32[4,2048]{1,0:T(4,128)S(1)}, f32[4,2048]{1,0:T(4,128)}, u32[]{:S(2)}) copy-start(f32[4,2048]{1,0:T(4,128)} %refs_6_.3) | copy-start | bytes 98308
  42.3 13.2 %collective-permute-start.9 = (bf16[128,512]{1,0:T(8,128)(2,1)}, bf16[128,512]{1,0:T(8,128)(2,1)S(1)}, u32[]{:S(2)}, u32[]{:S(2)}) collective-permute-start(bf16[128,512]{1,0:T(8,128)(2,1)} %get-tuple-element.43), channel_id=1, source_target_pairs={{0,26},{2,0},{4,30},{6,4},{8,18},{10,8},{12,22},{14,12},{16,10},{1... | collective-permute-start | bytes 393224 | tf_op jit(solution)/shard_map/ppermute | solution.py:270
  47.1 8.3 %collective-permute-start.10 = (bf16[128,512]{1,0:T(8,128)(2,1)}, bf16[128,512]{1,0:T(8,128)(2,1)S(1)}, u32[]{:S(2)}, u32[]{:S(2)}) collective-permute-start(bf16[128,512]{1,0:T(8,128)(2,1)} %get-tuple-element.45), channel_id=1, source_target_pairs={{0,4},{2,30},{4,0},{6,26},{8,12},{10,22},{12,8},{14,18},{16,20},{1... | collective-permute-start | bytes 393224 | tf_op jit(solution)/shard_map/ppermute | solution.py:270
  49.3 6.2 %collective-permute-start.11 = (bf16[128,512]{1,0:T(8,128)(2,1)}, bf16[128,512]{1,0:T(8,128)(2,1)S(1)}, u32[]{:S(2)}, u32[]{:S(2)}) collective-permute-start(bf16[128,512]{1,0:T(8,128)(2,1)} %get-tuple-element.47), channel_id=1, source_target_pairs={{0,30},{2,4},{4,26},{6,0},{8,22},{10,12},{12,18},{14,8},{16,14},{1... | collective-permute-start | bytes 393224 | tf_op jit(solution)/shard_map/ppermute | solution.py:270
  49.8 1.6 %copy-start.1 = (bf16[2048,512]{1,0:T(8,128)(2,1)S(1)}, bf16[2048,512]{1,0:T(8,128)(2,1)}, u32[]{:S(2)}) copy-start(bf16[2048,512]{1,0:T(8,128)(2,1)} %refs_5_.3) | copy-start | bytes 6291460
  51.4 0.8 %copy-start.5 = (f32[128,128]{1,0:T(8,128)S(1)}, f32[128,128]{1,0:T(8,128)}, u32[]{:S(2)}) copy-start(f32[128,128]{1,0:T(8,128)} %get-tuple-element.42.refs_10_) | copy-start | bytes 196612
  52.3 0.8 %copy-start.6 = (f32[128,128]{1,0:T(8,128)S(1)}, f32[128,128]{1,0:T(8,128)}, u32[]{:S(2)}) copy-start(f32[128,128]{1,0:T(8,128)} %get-tuple-element.53.refs_11_) | copy-start | bytes 196612

commit v4 on v3

--- a/solution.py
+++ b/solution.py
@@ -32,13 +32,12 @@
     return by_place(bases, odd ^ (index % 2)) + index
 
 
-def split_kernel(all_bases, dout_ref, *refs):
-    out_refs, (block_ref, in_sems, out_sems) = refs[:-3], refs[-3:]
+def split_kernel(all_bases, places, tokens, dout_ref, *refs):
+    out_refs, (block_ref, in_sems, out_sems) = refs[tokens:-3], refs[-3:]
     width = out_refs[0].shape[1]
     columns = BATCH * width
     me = lax.axis_index("head")
     mine = me // BATCH
-    half = len(all_bases) // 2
 
     def read(group):
         start = pl.multiple_of((mine ^ group) * columns, columns)
@@ -46,41 +45,45 @@
             dout_ref.at[:, pl.ds(start, columns)], block_ref.at[group], in_sems.at[group]
         )
 
-    for pair in all_bases[:half]:
-        for base in pair:
-            read(base // BATCH).start()
+    needs = [sorted(base // BATCH for base in all_bases[place // BATCH]) for place in places]
+    started, there = [], []
+    for need in needs:
+        for group in need:
+            if group not in started:
+                started.append(group)
+                read(group).start()
     writes = []
-    for batch in range(half):
-        for base in all_bases[batch]:
-            read(base // BATCH).wait()
-        for place in (*range(batch * BATCH, (batch + 1) * BATCH),
-                      *range((batch + half) * BATCH, (batch + half + 1) * BATCH)):
-            distance = sent_distance(all_bases[place // BATCH], place % BATCH, lax.rem(me, 2))
-            start = pl.multiple_of(lax.rem(me ^ distance, BATCH) * width, width)
-            piece = block_ref.at[distance // BATCH, :, pl.ds(start, width)]
-            writes.append(pltpu.make_async_copy(piece, out_refs[place], out_sems.at[place]))
-            writes[-1].start()
+    for place, need, out_ref in zip(places, needs, out_refs):
+        for group in need:
+            if group not in there:
+                there.append(group)
+                read(group).wait()
+        distance = sent_distance(all_bases[place // BATCH], place % BATCH, lax.rem(me, 2))
+        start = pl.multiple_of(lax.rem(me ^ distance, BATCH) * width, width)
+        piece = block_ref.at[distance // BATCH, :, pl.ds(start, width)]
+        writes.append(pltpu.make_async_copy(piece, out_ref, out_sems.at[len(writes)]))
+        writes[-1].start()
     for write in writes:
         write.wait()
 
 
-def split(dout, dests):
+def split(dout, dests, places, tokens):
     rows, width = dout.shape[0], dout.shape[1] // dests
     groups = dests // BATCH
     return pl.pallas_call(
-        functools.partial(split_kernel, batches(dests)),
-        in_specs=[pl.BlockSpec(memory_space=pl.ANY)],
-        out_specs=[pl.BlockSpec(memory_space=pl.ANY)] * dests,
-        out_shape=[jax.ShapeDtypeStruct((rows, width), dout.dtype)] * dests,
+        functools.partial(split_kernel, batches(dests), places, len(tokens)),
+        in_specs=[pl.BlockSpec(memory_space=pl.ANY)] * (1 + len(tokens)),
+        out_specs=[pl.BlockSpec(memory_space=pl.ANY)] * len(places),
+        out_shape=[jax.ShapeDtypeStruct((rows, width), dout.dtype)] * len(places),
         scratch_shapes=[
             pltpu.VMEM((groups, rows, BATCH * width), dout.dtype),
             pltpu.SemaphoreType.DMA((groups,)),
-            pltpu.SemaphoreType.DMA((dests,)),
+            pltpu.SemaphoreType.DMA((len(places),)),
         ],
         compiler_params=pltpu.CompilerParams(vmem_limit_bytes=VMEM_LIMIT),
         cost_estimate=FREE,
-        name="split",
-    )(dout)
+        name=f"split_{places[0]}",
+    )(dout, *tokens)
 
 
 def attention_kernel(first, last, pairs, place_ref, *refs):
@@ -257,7 +260,8 @@
     all_bases = batches(heads_axis)
     place = lax.axis_index("head").astype(jnp.int32).reshape(1)
     k, v = own_group(keys, values, owners)
-    pieces = split(dout, heads_axis)
+    pieces = list(split(dout, heads_axis, list(range(BATCH)), []))
+    pieces += split(dout, heads_axis, list(range(BATCH, heads_axis)), pieces[:1])
     data = (queries, outputs, lse, k, v)
     arrived = []
 

time: 72.4 us -> 73.4 us (1.014)
  Pallas kernels: 15.5 us -> 17.4 us
  blocking collectives: 13.3 us -> 12.5 us
    pallas_call x1 -> x2, Pallas kernels: 2.69 us -> 4.68 us  [split(): pl.pallas_call(functools.partial(split_kernel, batches(dests), places, le...]
    ppermute x16, starting transfers between devices: 32.3 us -> 31.1 us  [send(): arrived.append(lax.ppermute(piece, 'head', pairs))]
    all_to_all x1, blocking collectives: 13.3 us -> 12.5 us  [on_device(): lax.all_to_all(terms, ('head', 'ctx'), split_axis=0, concat_axis=0, tiled...]
  transfers between devices with their start and end apart: 17 -> 17, of which waited for: 1 -> 2; matrix products, arithmetic and copies ran while one was open for 1% -> 1% of each run, Pallas kernels for 13% -> 17%
where the time goes in v4:
time: 73.4 us; the launch traced here: 72.9 us
  starting transfers between devices  37.4 us (51%)
  Pallas kernels  17.4 us (24%)
  blocking collectives  12.5 us (17%)
  local copies, waits for them, and re-layouts  3.96 us (5%)
  between operations  0.88 us (1%)
    ppermute x16, starting transfers between devices, send(): arrived.append(lax.ppermute(piece, 'head', pairs))  31.1 us
    all_to_all x1, blocking collectives, on_device(): lax.all_to_all(terms, ('head', 'ctx'), split_axis=0, concat_axis=0, tiled...  12.5 us
    pallas_call x3, Pallas kernels, attention(): pl.pallas_call(functools.partial(attention_kernel, first, owners > 0, pai...  10.8 us
    all_to_all x1, starting transfers between devices, own_group(): lax.all_to_all(mine, ('head', 'ctx'), split_axis=0, concat_axis=0, tiled=...  6.33 us
    pallas_call x2, Pallas kernels, split(): pl.pallas_call(functools.partial(split_kernel, batches(dests), places, le...  4.68 us
    unnamed x30, local copies, waits for them, and re-layouts  3.32 us
  transfers between devices with their start and end apart: 17, of which 2 were waited for; matrix products, arithmetic and copies ran while one was open for 1% of the time, Pallas kernels for 17%

profile of v4, /device:TPU:0, one launch (start us, length us, event | category | flops | bytes accessed | tf_op | source)
XLA Modules:
  0.0 72.9 jit_solution(18190200557874563388)
XLA Ops:
  0.6 2.1 %split_0.1 = (bf16[128,512]{1,0:T(8,128)(2,1)}, bf16[128,512]{1,0:T(8,128)(2,1)}, bf16[128,512]{1,0:T(8,128)(2,1)}, bf16[128,512]{1,0:T(8,128)(2,1)}) custom-call(bf16[128,8192]{1,0:T(8,128)(2,1)} %dout_ref.3), custom_call_target="tpu_custom_call" | custom-call | tf_op jit(solution)/shard_map/split_0/pallas_call | solution.py:73
  2.7 5.0 %collective-permute-start.3 = (bf16[128,512]{1,0:T(8,128)(2,1)}, bf16[128,512]{1,0:T(8,128)(2,1)S(1)}, u32[]{:S(2)}, u32[]{:S(2)}) collective-permute-start(bf16[128,512]{1,0:T(8,128)(2,1)} %get-tuple-element.36), channel_id=1, source_target_pairs={{0,20},{2,14},{4,16},{6,10},{8,28},{10,6},{12,24},{14,2},{16,4},{1... | collective-permute-start | bytes 393224 | tf_op jit(solution)/shard_map/ppermute | solution.py:274
  7.7 0.0 collective-permute-start.2
  7.7 1.6 %collective-permute-start.4 = (bf16[128,512]{1,0:T(8,128)(2,1)}, bf16[128,512]{1,0:T(8,128)(2,1)S(1)}, u32[]{:S(2)}, u32[]{:S(2)}) collective-permute-start(bf16[128,512]{1,0:T(8,128)(2,1)} %get-tuple-element.37), channel_id=1, source_target_pairs={{0,14},{2,20},{4,10},{6,16},{8,6},{10,28},{12,2},{14,24},{16,30},{... | collective-permute-start | bytes 393224 | tf_op jit(solution)/shard_map/ppermute | solution.py:274
  9.3 2.6 %collective-permute-start.1 = (bf16[128,512]{1,0:T(8,128)(2,1)}, bf16[128,512]{1,0:T(8,128)(2,1)S(1)}, u32[]{:S(2)}, u32[]{:S(2)}) collective-permute-start(bf16[128,512]{1,0:T(8,128)(2,1)} %get-tuple-element.32.refs_0_), channel_id=1, source_target_pairs={{0,16},{2,10},{4,20},{6,14},{8,24},{10,2},{12,28},{14,6},{16,0},{1... | collective-permute-start | bytes 393224 | tf_op jit(solution)/shard_map/ppermute | solution.py:274
  11.9 2.6 %split_4.1 = (bf16[128,512]{1,0:T(8,128)(2,1)}, bf16[128,512]{1,0:T(8,128)(2,1)}, bf16[128,512]{1,0:T(8,128)(2,1)}, bf16[128,512]{1,0:T(8,128)(2,1)}, bf16[128,5...) custom-call(bf16[128,8192]{1,0:T(8,128)(2,1)} %dout_ref.3, ...), custom_call_target="tpu_custom_call" | custom-call | tf_op jit(solution)/shard_map/split_4/pallas_call | solution.py:73
  14.5 1.9 %collective-permute-start.5 = (bf16[128,512]{1,0:T(8,128)(2,1)}, bf16[128,512]{1,0:T(8,128)(2,1)S(1)}, u32[]{:S(2)}, u32[]{:S(2)}) collective-permute-start(bf16[128,512]{1,0:T(8,128)(2,1)} %get-tuple-element.38), channel_id=1, source_target_pairs={{0,24},{2,2},{4,28},{6,6},{8,16},{10,10},{12,20},{14,14},{16,8},{1... | collective-permute-start | bytes 393224 | tf_op jit(solution)/shard_map/ppermute | solution.py:274
  16.5 0.0 collective-permute-done.3.refs_2_
  16.5 0.1 collective-permute-start.6
  16.6 1.3 %pack_keys.1 = bf16[32,8,128]{2,1,0:T(8,128)(2,1)} custom-call(bf16[4,512]{1,0:T(4,128)(2,1)} %k_ref.1, bf16[4,512]{1,0:T(4,128)(2,1)} %v_ref.1), custom_call_target="tpu_custom_call" | custom-call | tf_op jit(solution)/shard_map/pack_keys/pallas_call | solution.py:248
  17.9 6.3 %all-to-all-start = ((bf16[32,8,128]{2,1,0:T(8,128)(2,1)}), bf16[32,8,128]{2,1,0:T(8,128)(2,1)S(1)}, u32[]{:S(2)}, u32[]{:S(2)}) async-start(bf16[32,8,128]{2,1,0:T(8,128)(2,1)} %pack_keys.1), calls=%async_computation | async-start | bytes 131072 | tf_op jit(solution)/shard_map/all_to_all | solution.py:254
  24.2 0.0 collective-permute-done.2.refs_1_
  24.3 4.6 %collective-permute-start.7 = (bf16[128,512]{1,0:T(8,128)(2,1)}, bf16[128,512]{1,0:T(8,128)(2,1)S(1)}, u32[]{:S(2)}, u32[]{:S(2)}) collective-permute-start(bf16[128,512]{1,0:T(8,128)(2,1)} %get-tuple-element.40), channel_id=1, source_target_pairs={{0,28},{2,6},{4,24},{6,2},{8,20},{10,14},{12,16},{14,10},{16,12},{... | collective-permute-start | bytes 393224 | tf_op jit(solution)/shard_map/ppermute | solution.py:274
  28.9 0.0 collective-permute-done.4.refs_3_
  28.9 0.0 collective-permute-start.8
  28.9 0.0 collective-permute-done.1.refs_0_
  28.9 0.1 collective-permute-start.12
  29.0 0.0 collective-permute-done.5.refs_4_
  29.0 2.4 %collective-permute-start.13 = (bf16[128,512]{1,0:T(8,128)(2,1)}, bf16[128,512]{1,0:T(8,128)(2,1)S(1)}, u32[]{:S(2)}, u32[]{:S(2)}) collective-permute-start(bf16[128,512]{1,0:T(8,128)(2,1)} %get-tuple-element.49), channel_id=1, source_target_pairs={{0,18},{2,8},{4,22},{6,12},{8,26},{10,0},{12,30},{14,4},{16,2},{18... | collective-permute-start | bytes 393224 | tf_op jit(solution)/shard_map/ppermute | solution.py:274
  31.4 0.0 collective-permute-done.6.refs_5_
  31.4 2.5 %collective-permute-start.14 = (bf16[128,512]{1,0:T(8,128)(2,1)}, bf16[128,512]{1,0:T(8,128)(2,1)S(1)}, u32[]{:S(2)}, u32[]{:S(2)}) collective-permute-start(bf16[128,512]{1,0:T(8,128)(2,1)} %get-tuple-element.50), channel_id=1, source_target_pairs={{0,12},{2,22},{4,8},{6,18},{8,4},{10,30},{12,0},{14,26},{16,28},{1... | collective-permute-start | bytes 393224 | tf_op jit(solution)/shard_map/ppermute | solution.py:274
  34.0 0.0 all-to-all-done
  34.0 0.6 fusion
  34.6 0.0 collective-permute-done.7.refs_6_
  34.6 1.6 %collective-permute-start = (bf16[128,512]{1,0:T(8,128)(2,1)}, bf16[128,512]{1,0:T(8,128)(2,1)S(1)}, u32[]{:S(2)}, u32[]{:S(2)}) collective-permute-start(bf16[128,512]{1,0:T(8,128)(2,1)} %get-tuple-element.33), channel_id=1, source_target_pairs={{0,0},{2,26},{4,4},{6,30},{8,8},{10,18},{12,12},{14,22},{16,16},{1... | collective-permute-start | bytes 393224 | tf_op jit(solution)/shard_map/ppermute | solution.py:274
  36.2 0.2 collective-permute-done.8.refs_7_
  36.4 1.2 %collective-permute-start.15 = (bf16[128,512]{1,0:T(8,128)(2,1)}, bf16[128,512]{1,0:T(8,128)(2,1)S(1)}, u32[]{:S(2)}, u32[]{:S(2)}) collective-permute-start(bf16[128,512]{1,0:T(8,128)(2,1)} %get-tuple-element.51), channel_id=1, source_target_pairs={{0,22},{2,12},{4,18},{6,8},{8,30},{10,4},{12,26},{14,0},{16,6},{18... | collective-permute-start | bytes 393224 | tf_op jit(solution)/shard_map/ppermute | solution.py:274
  37.6 0.0 copy-start
  37.7 0.0 copy-start.4
  37.7 6.0 %sources_8.1 = (bf16[2048,512]{1,0:T(8,128)(2,1)}, f32[128,128]{1,0:T(8,128)}, f32[128,128]{1,0:T(8,128)}) custom-call(s32[1]{0:T(128)} %bitcast.place_ref, bf16[128,512]{1,0:T(8,128)(2,1)} %copy-done.10, bf16[128,512]{1,0:T(8,128)(2,1)} %copy-done.8, bf16[128,512]{1,0:T(8,128)(2,1)} %copy-done.7, bf16[128,512]{1,0:T(8,128)(2,1)} %copy-done.9, ...), custom_call_target="tpu_custom_call" | custom-call | tf_op jit(solution)/shard_map/sources_8/pallas_call | solution.py:194
  43.6 0.0 collective-permute-done.12.refs_0_
  43.6 4.9 %collective-permute-start.9 = (bf16[128,512]{1,0:T(8,128)(2,1)}, bf16[128,512]{1,0:T(8,128)(2,1)S(1)}, u32[]{:S(2)}, u32[]{:S(2)}) collective-permute-start(bf16[128,512]{1,0:T(8,128)(2,1)} %get-tuple-element.43), channel_id=1, source_target_pairs={{0,26},{2,0},{4,30},{6,4},{8,18},{10,8},{12,22},{14,12},{16,10},{1... | collective-permute-start | bytes 393224 | tf_op jit(solution)/shard_map/ppermute | solution.py:274
  48.5 0.0 collective-permute-start.10
  48.5 0.0 collective-permute-done.14.refs_2_
  48.5 2.7 %collective-permute-start.11 = (bf16[128,512]{1,0:T(8,128)(2,1)}, bf16[128,512]{1,0:T(8,128)(2,1)S(1)}, u32[]{:S(2)}, u32[]{:S(2)}) collective-permute-start(bf16[128,512]{1,0:T(8,128)(2,1)} %get-tuple-element.47), channel_id=1, source_target_pairs={{0,30},{2,4},{4,26},{6,0},{8,22},{10,12},{12,18},{14,8},{16,14},{1... | collective-permute-start | bytes 393224 | tf_op jit(solution)/shard_map/ppermute | solution.py:274
  51.2 0.0 collective-permute-done.15.refs_3_
  51.2 0.0 copy-start.1
  51.2 1.6 %copy-done.1 = bf16[2048,512]{1,0:T(8,128)(2,1)S(1)} copy-done((bf16[2048,512]{1,0:T(8,128)(2,1)S(1)}, bf16[2048,512]{1,0:T(8,128)(2,1)}, u32[]{:S(2)}) %copy-start.1) | copy-done | bytes 2097176
  52.8 0.8 %copy-done.5 = f32[128,128]{1,0:T(8,128)S(1)} copy-done((f32[128,128]{1,0:T(8,128)S(1)}, f32[128,128]{1,0:T(8,128)}, u32[]{:S(2)}) %copy-start.5) | copy-done | bytes 65560
  53.6 0.8 %copy-done.6 = f32[128,128]{1,0:T(8,128)S(1)} copy-done((f32[128,128]{1,0:T(8,128)S(1)}, f32[128,128]{1,0:T(8,128)}, u32[]{:S(2)}) %copy-start.6) | copy-done | bytes 65560
  54.5 2.3 %sources_4.1 = (bf16[2048,512]{1,0:T(8,128)(2,1)}, f32[128,128]{1,0:T(8,128)S(1)}, f32[128,128]{1,0:T(8,128)S(1)}) custom-call(s32[1]{0:T(128)} %bitcast.place_ref, bf16[128,512]{1,0:T(8,128)(2,1)S(1)} %collective-permute-done.12.refs_0_, bf16[128,512]{1,0:T(8,128)(2,1)S(1)} %collective-permute-done.13.refs_1_, ...), custom_call_target="tpu_custom_call", output_to_operand_aliasing={{0}: (10, {})} | custom-call | tf_op jit(solution)/shard_map/sources_4/pallas_call | solution.py:194
  56.8 0.0 collective-permute-done.refs_0_
  56.8 0.0 collective-permute-done.9.refs_1_
  56.8 0.5 collective-permute-done.10.refs_2_
  57.3 0.0 collective-permute-done.11.refs_3_
  57.3 2.4 %sources_0.1 = (bf16[2048,512]{1,0:T(8,128)(2,1)}, f32[32,8,128]{2,1,0:T(8,128)S(1)}) custom-call(s32[1]{0:T(128)} %bitcast.place_ref, bf16[128,512]{1,0:T(8,128)(2,1)S(1)} %collective-permute-done.refs_0_, bf16[128,512]{1,0:T(8,128)(2,1)S(1)} %collective-permute-done.9.refs_1_, ...), custom_call_target="tpu_custom_call", output_to_operand_aliasing={{0}: (10, {})} | custom-call | tf_op jit(solution)/shard_map/sources_0/pallas_call | solution.py:194
  59.8 12.5 %all_to_all.10.terms_ref = f32[32,8,128]{2,1,0:T(8,128)S(1)} all-to-all(f32[32,8,128]{2,1,0:T(8,128)S(1)} %get-tuple-element.58), channel_id=1, replica_groups=mesh['head'=16,'ctx'=2] {'head','ctx'}, dimensions={0} | all-to-all | bytes 262144 | tf_op jit(solution)/shard_map/all_to_all | solution.py:306
  72.2 0.6 sum_terms.1
  (25 shorter events, 0.1 us)
Async XLA Ops:
  2.7 13.8 %collective-permute-start.3 = (bf16[128,512]{1,0:T(8,128)(2,1)}, bf16[128,512]{1,0:T(8,128)(2,1)S(1)}, u32[]{:S(2)}, u32[]{:S(2)}) collective-permute-start(bf16[128,512]{1,0:T(8,128)(2,1)} %get-tuple-element.36), channel_id=1, source_target_pairs={{0,20},{2,14},{4,16},{6,10},{8,28},{10,6},{12,24},{14,2},{16,4},{1... | collective-permute-start | bytes 393224 | tf_op jit(solution)/shard_map/ppermute | solution.py:274
  7.7 16.5 %collective-permute-start.2 = (bf16[128,512]{1,0:T(8,128)(2,1)}, bf16[128,512]{1,0:T(8,128)(2,1)S(1)}, u32[]{:S(2)}, u32[]{:S(2)}) collective-permute-start(bf16[128,512]{1,0:T(8,128)(2,1)} %get-tuple-element.35), channel_id=1, source_target_pairs={{0,10},{2,16},{4,14},{6,20},{8,2},{10,24},{12,6},{14,28},{16,26},{... | collective-permute-start | bytes 393224 | tf_op jit(solution)/shard_map/ppermute | solution.py:274
  7.7 21.1 %collective-permute-start.4 = (bf16[128,512]{1,0:T(8,128)(2,1)}, bf16[128,512]{1,0:T(8,128)(2,1)S(1)}, u32[]{:S(2)}, u32[]{:S(2)}) collective-permute-start(bf16[128,512]{1,0:T(8,128)(2,1)} %get-tuple-element.37), channel_id=1, source_target_pairs={{0,14},{2,20},{4,10},{6,16},{8,6},{10,28},{12,2},{14,24},{16,30},{... | collective-permute-start | bytes 393224 | tf_op jit(solution)/shard_map/ppermute | solution.py:274
  9.3 19.5 %collective-permute-start.1 = (bf16[128,512]{1,0:T(8,128)(2,1)}, bf16[128,512]{1,0:T(8,128)(2,1)S(1)}, u32[]{:S(2)}, u32[]{:S(2)}) collective-permute-start(bf16[128,512]{1,0:T(8,128)(2,1)} %get-tuple-element.32.refs_0_), channel_id=1, source_target_pairs={{0,16},{2,10},{4,20},{6,14},{8,24},{10,2},{12,28},{14,6},{16,0},{1... | collective-permute-start | bytes 393224 | tf_op jit(solution)/shard_map/ppermute | solution.py:274
  14.5 14.4 %collective-permute-start.5 = (bf16[128,512]{1,0:T(8,128)(2,1)}, bf16[128,512]{1,0:T(8,128)(2,1)S(1)}, u32[]{:S(2)}, u32[]{:S(2)}) collective-permute-start(bf16[128,512]{1,0:T(8,128)(2,1)} %get-tuple-element.38), channel_id=1, source_target_pairs={{0,24},{2,2},{4,28},{6,6},{8,16},{10,10},{12,20},{14,14},{16,8},{1... | collective-permute-start | bytes 393224 | tf_op jit(solution)/shard_map/ppermute | solution.py:274
  16.5 21.1 %copy-start.7 = (bf16[128,512]{1,0:T(8,128)(2,1)}, bf16[128,512]{1,0:T(8,128)(2,1)S(1)}, u32[]{:S(2)}) copy-start(bf16[128,512]{1,0:T(8,128)(2,1)S(1)} %collective-permute-done.3.refs_2_) | copy-start | bytes 393220
  16.5 14.9 %collective-permute-start.6 = (bf16[128,512]{1,0:T(8,128)(2,1)}, bf16[128,512]{1,0:T(8,128)(2,1)S(1)}, u32[]{:S(2)}, u32[]{:S(2)}) collective-permute-start(bf16[128,512]{1,0:T(8,128)(2,1)} %get-tuple-element.39), channel_id=1, source_target_pairs={{0,2},{2,24},{4,6},{6,28},{8,10},{10,16},{12,14},{14,20},{16,18},{... | collective-permute-start | bytes 393224 | tf_op jit(solution)/shard_map/ppermute | solution.py:274
  17.9 16.1 %all-to-all-start = ((bf16[32,8,128]{2,1,0:T(8,128)(2,1)}), bf16[32,8,128]{2,1,0:T(8,128)(2,1)S(1)}, u32[]{:S(2)}, u32[]{:S(2)}) async-start(bf16[32,8,128]{2,1,0:T(8,128)(2,1)} %pack_keys.1), calls=%async_computation | async-start | bytes 131072 | tf_op jit(solution)/shard_map/all_to_all | solution.py:254
  24.2 13.3 %copy-start.8 = (bf16[128,512]{1,0:T(8,128)(2,1)}, bf16[128,512]{1,0:T(8,128)(2,1)S(1)}, u32[]{:S(2)}) copy-start(bf16[128,512]{1,0:T(8,128)(2,1)S(1)} %collective-permute-done.2.refs_1_) | copy-start | bytes 393220
  24.3 10.4 %collective-permute-start.7 = (bf16[128,512]{1,0:T(8,128)(2,1)}, bf16[128,512]{1,0:T(8,128)(2,1)S(1)}, u32[]{:S(2)}, u32[]{:S(2)}) collective-permute-start(bf16[128,512]{1,0:T(8,128)(2,1)} %get-tuple-element.40), channel_id=1, source_target_pairs={{0,28},{2,6},{4,24},{6,2},{8,20},{10,14},{12,16},{14,10},{16,12},{... | collective-permute-start | bytes 393224 | tf_op jit(solution)/shard_map/ppermute | solution.py:274
  28.9 8.7 %copy-start.9 = (bf16[128,512]{1,0:T(8,128)(2,1)}, bf16[128,512]{1,0:T(8,128)(2,1)S(1)}, u32[]{:S(2)}) copy-start(bf16[128,512]{1,0:T(8,128)(2,1)S(1)} %collective-permute-done.4.refs_3_) | copy-start | bytes 393220
  28.9 7.5 %collective-permute-start.8 = (bf16[128,512]{1,0:T(8,128)(2,1)}, bf16[128,512]{1,0:T(8,128)(2,1)S(1)}, u32[]{:S(2)}, u32[]{:S(2)}) collective-permute-start(bf16[128,512]{1,0:T(8,128)(2,1)} %get-tuple-element.41), channel_id=1, source_target_pairs={{0,6},{2,28},{4,2},{6,24},{8,14},{10,20},{12,10},{14,16},{16,22},{... | collective-permute-start | bytes 393224 | tf_op jit(solution)/shard_map/ppermute | solution.py:274
  28.9 8.7 %copy-start.10 = (bf16[128,512]{1,0:T(8,128)(2,1)}, bf16[128,512]{1,0:T(8,128)(2,1)S(1)}, u32[]{:S(2)}) copy-start(bf16[128,512]{1,0:T(8,128)(2,1)S(1)} %collective-permute-done.1.refs_0_) | copy-start | bytes 393220
  28.9 14.8 %collective-permute-start.12 = (bf16[128,512]{1,0:T(8,128)(2,1)}, bf16[128,512]{1,0:T(8,128)(2,1)S(1)}, u32[]{:S(2)}, u32[]{:S(2)}) collective-permute-start(bf16[128,512]{1,0:T(8,128)(2,1)} %get-tuple-element.48), channel_id=1, source_target_pairs={{0,8},{2,18},{4,12},{6,22},{8,0},{10,26},{12,4},{14,30},{16,24},{1... | collective-permute-start | bytes 393224 | tf_op jit(solution)/shard_map/ppermute | solution.py:274
  29.0 8.6 %copy-start.11 = (bf16[128,512]{1,0:T(8,128)(2,1)}, bf16[128,512]{1,0:T(8,128)(2,1)S(1)}, u32[]{:S(2)}) copy-start(bf16[128,512]{1,0:T(8,128)(2,1)S(1)} %collective-permute-done.5.refs_4_) | copy-start | bytes 393220
  29.0 19.5 %collective-permute-start.13 = (bf16[128,512]{1,0:T(8,128)(2,1)}, bf16[128,512]{1,0:T(8,128)(2,1)S(1)}, u32[]{:S(2)}, u32[]{:S(2)}) collective-permute-start(bf16[128,512]{1,0:T(8,128)(2,1)} %get-tuple-element.49), channel_id=1, source_target_pairs={{0,18},{2,8},{4,22},{6,12},{8,26},{10,0},{12,30},{14,4},{16,2},{18... | collective-permute-start | bytes 393224 | tf_op jit(solution)/shard_map/ppermute | solution.py:274
  31.4 6.2 %copy-start.12 = (bf16[128,512]{1,0:T(8,128)(2,1)}, bf16[128,512]{1,0:T(8,128)(2,1)S(1)}, u32[]{:S(2)}) copy-start(bf16[128,512]{1,0:T(8,128)(2,1)S(1)} %collective-permute-done.6.refs_5_) | copy-start | bytes 393220
  31.4 17.1 %collective-permute-start.14 = (bf16[128,512]{1,0:T(8,128)(2,1)}, bf16[128,512]{1,0:T(8,128)(2,1)S(1)}, u32[]{:S(2)}, u32[]{:S(2)}) collective-permute-start(bf16[128,512]{1,0:T(8,128)(2,1)} %get-tuple-element.50), channel_id=1, source_target_pairs={{0,12},{2,22},{4,8},{6,18},{8,4},{10,30},{12,0},{14,26},{16,28},{1... | collective-permute-start | bytes 393224 | tf_op jit(solution)/shard_map/ppermute | solution.py:274
  34.6 3.0 %copy-start.13 = (bf16[128,512]{1,0:T(8,128)(2,1)}, bf16[128,512]{1,0:T(8,128)(2,1)S(1)}, u32[]{:S(2)}) copy-start(bf16[128,512]{1,0:T(8,128)(2,1)S(1)} %collective-permute-done.7.refs_6_) | copy-start | bytes 393220
  34.6 22.2 %collective-permute-start = (bf16[128,512]{1,0:T(8,128)(2,1)}, bf16[128,512]{1,0:T(8,128)(2,1)S(1)}, u32[]{:S(2)}, u32[]{:S(2)}) collective-permute-start(bf16[128,512]{1,0:T(8,128)(2,1)} %get-tuple-element.33), channel_id=1, source_target_pairs={{0,0},{2,26},{4,4},{6,30},{8,8},{10,18},{12,12},{14,22},{16,16},{1... | collective-permute-start | bytes 393224 | tf_op jit(solution)/shard_map/ppermute | solution.py:274
  36.4 1.3 %copy-start.14 = (bf16[128,512]{1,0:T(8,128)(2,1)}, bf16[128,512]{1,0:T(8,128)(2,1)S(1)}, u32[]{:S(2)}) copy-start(bf16[128,512]{1,0:T(8,128)(2,1)S(1)} %collective-permute-done.8.refs_7_) | copy-start | bytes 393220
  36.4 14.8 %collective-permute-start.15 = (bf16[128,512]{1,0:T(8,128)(2,1)}, bf16[128,512]{1,0:T(8,128)(2,1)S(1)}, u32[]{:S(2)}, u32[]{:S(2)}) collective-permute-start(bf16[128,512]{1,0:T(8,128)(2,1)} %get-tuple-element.51), channel_id=1, source_target_pairs={{0,22},{2,12},{4,18},{6,8},{8,30},{10,4},{12,26},{14,0},{16,6},{18... | collective-permute-start | bytes 393224 | tf_op jit(solution)/shard_map/ppermute | solution.py:274
  37.6 13.6 %copy-start = (bf16[2048,512]{1,0:T(8,128)(2,1)S(1)}, bf16[2048,512]{1,0:T(8,128)(2,1)}, u32[]{:S(2)}) copy-start(bf16[2048,512]{1,0:T(8,128)(2,1)} %refs_4_.3) | copy-start | bytes 6291460
  37.6 13.5 %copy-start.2 = (bf16[32,4,128]{2,1,0:T(4,128)(2,1)S(1)}, bf16[32,4,128]{2,1,0:T(4,128)(2,1)}, u32[]{:S(2)}) copy-start(bf16[32,4,128]{2,1,0:T(4,128)(2,1)} %get-tuple-element.61) | copy-start | bytes 98308
  37.6 13.5 %copy-start.3 = (bf16[32,4,128]{2,1,0:T(4,128)(2,1)S(1)}, bf16[32,4,128]{2,1,0:T(4,128)(2,1)}, u32[]{:S(2)}) copy-start(bf16[32,4,128]{2,1,0:T(4,128)(2,1)} %get-tuple-element.62) | copy-start | bytes 98308
  37.7 13.5 %copy-start.4 = (f32[4,2048]{1,0:T(4,128)S(1)}, f32[4,2048]{1,0:T(4,128)}, u32[]{:S(2)}) copy-start(f32[4,2048]{1,0:T(4,128)} %refs_6_.3) | copy-start | bytes 98308
  43.6 13.2 %collective-permute-start.9 = (bf16[128,512]{1,0:T(8,128)(2,1)}, bf16[128,512]{1,0:T(8,128)(2,1)S(1)}, u32[]{:S(2)}, u32[]{:S(2)}) collective-permute-start(bf16[128,512]{1,0:T(8,128)(2,1)} %get-tuple-element.43), channel_id=1, source_target_pairs={{0,26},{2,0},{4,30},{6,4},{8,18},{10,8},{12,22},{14,12},{16,10},{1... | collective-permute-start | bytes 393224 | tf_op jit(solution)/shard_map/ppermute | solution.py:274
  48.5 8.8 %collective-permute-start.10 = (bf16[128,512]{1,0:T(8,128)(2,1)}, bf16[128,512]{1,0:T(8,128)(2,1)S(1)}, u32[]{:S(2)}, u32[]{:S(2)}) collective-permute-start(bf16[128,512]{1,0:T(8,128)(2,1)} %get-tuple-element.45), channel_id=1, source_target_pairs={{0,4},{2,30},{4,0},{6,26},{8,12},{10,22},{12,8},{14,18},{16,20},{1... | collective-permute-start | bytes 393224 | tf_op jit(solution)/shard_map/ppermute | solution.py:274
  48.5 8.8 %collective-permute-start.11 = (bf16[128,512]{1,0:T(8,128)(2,1)}, bf16[128,512]{1,0:T(8,128)(2,1)S(1)}, u32[]{:S(2)}, u32[]{:S(2)}) collective-permute-start(bf16[128,512]{1,0:T(8,128)(2,1)} %get-tuple-element.47), channel_id=1, source_target_pairs={{0,30},{2,4},{4,26},{6,0},{8,22},{10,12},{12,18},{14,8},{16,14},{1... | collective-permute-start | bytes 393224 | tf_op jit(solution)/shard_map/ppermute | solution.py:274
  51.2 1.6 %copy-start.1 = (bf16[2048,512]{1,0:T(8,128)(2,1)S(1)}, bf16[2048,512]{1,0:T(8,128)(2,1)}, u32[]{:S(2)}) copy-start(bf16[2048,512]{1,0:T(8,128)(2,1)} %refs_5_.3) | copy-start | bytes 6291460
  52.8 0.8 %copy-start.5 = (f32[128,128]{1,0:T(8,128)S(1)}, f32[128,128]{1,0:T(8,128)}, u32[]{:S(2)}) copy-start(f32[128,128]{1,0:T(8,128)} %get-tuple-element.42.refs_10_) | copy-start | bytes 196612
  53.6 0.8 %copy-start.6 = (f32[128,128]{1,0:T(8,128)S(1)}, f32[128,128]{1,0:T(8,128)}, u32[]{:S(2)}) copy-start(f32[128,128]{1,0:T(8,128)} %get-tuple-element.53.refs_11_) | copy-start | bytes 196612

commit v5 on v3

--- a/solution.py
+++ b/solution.py
@@ -285,18 +285,14 @@
         )
 
     near = heads_axis // 2
-    carried = []
     for place_in_order in range(heads_axis):
-        gates = [arrived[place_in_order - 0]] if 0 and place_in_order >= 0 else []
-        if 5 and place_in_order == near + 5:
-            carried = compute(0, near, carried)
-        if 5 and place_in_order >= near + 5:
-            gates.append(carried[1])
+        gates = [arrived[place_in_order - 6]] if 6 and place_in_order >= 6 else []
+        if place_in_order >= near + 4:
+            gates.append(k)
         send(*gates)
-    if not carried:
-        carried = compute(0, near, carried)
-    for start in range(near, heads_axis, 4):
-        carried = compute(start, 4, carried)
+    carried = compute(0, near, [])
+    for start in range(near, heads_axis, BATCH):
+        carried = compute(start, BATCH, carried)
     dq, terms = carried
 
     terms = lax.all_to_all(terms, ("head", "ctx"), split_axis=0, concat_axis=0, tiled=True)

time: 72.4 us -> 79.1 us (1.093)
  starting transfers between devices: 38 us -> 45.8 us
  blocking collectives: 13.3 us -> 11.1 us
  waiting for transfers between devices: 0.24 us -> 1.16 us
    ppermute x16, starting transfers between devices: 32.3 us -> 40 us  [send(): arrived.append(lax.ppermute(piece, 'head', pairs))]
    all_to_all x1, blocking collectives: 13.3 us -> 11.1 us  [on_device(): lax.all_to_all(terms, ('head', 'ctx'), split_axis=0, concat_axis=0, tiled...]
    ppermute x16, waiting for transfers between devices: 0.24 us -> 1.16 us  [send(): arrived.append(lax.ppermute(piece, 'head', pairs))]
    unnamed x30 -> x24, local copies, waits for them, and re-layouts: 3.32 us -> 3.65 us
  transfers between devices with their start and end apart: 17 -> 17, of which waited for: 1 -> 1; matrix products, arithmetic and copies ran while one was open for 1% -> 1% of each run, Pallas kernels for 13% -> 12%
where the time goes in v5:
time: 79.1 us; the launch traced here: 78.6 us
  starting transfers between devices  45.8 us (58%)
  Pallas kernels  15.4 us (19%)
  blocking collectives  11.1 us (14%)
  local copies, waits for them, and re-layouts  4.29 us (5%)
  waiting for transfers between devices  1.16 us (1%)
  between operations  0.83 us (1%)
    ppermute x16, starting transfers between devices, send(): arrived.append(lax.ppermute(piece, 'head', pairs))  40 us
    all_to_all x1, blocking collectives, on_device(): lax.all_to_all(terms, ('head', 'ctx'), split_axis=0, concat_axis=0, tiled...  11.1 us
    pallas_call x3, Pallas kernels, attention(): pl.pallas_call(functools.partial(attention_kernel, first, owners > 0, pai...  10.8 us
    all_to_all x1, starting transfers between devices, own_group(): lax.all_to_all(mine, ('head', 'ctx'), split_axis=0, concat_axis=0, tiled=...  5.77 us
    unnamed x24, local copies, waits for them, and re-layouts  3.65 us
    pallas_call x1, Pallas kernels, split(): pl.pallas_call(functools.partial(split_kernel, batches(dests)), in_specs=...  2.69 us
  transfers between devices with their start and end apart: 17, of which 1 were waited for; matrix products, arithmetic and copies ran while one was open for 1% of the time, Pallas kernels for 12%

profile of v5, /device:TPU:0, one launch (start us, length us, event | category | flops | bytes accessed | tf_op | source)
XLA Modules:
  0.0 78.6 jit_solution(16580938639520583309)
XLA Ops:
  0.6 2.7 %split.1 = (bf16[128,512]{1,0:T(8,128)(2,1)}, bf16[128,512]{1,0:T(8,128)(2,1)}, bf16[128,512]{1,0:T(8,128)(2,1)}, bf16[128,512]{1,0:T(8,128)(2,1)}, bf16[128,512...) custom-call(bf16[128,8192]{1,0:T(8,128)(2,1)} %dout_ref.1), custom_call_target="tpu_custom_call" | custom-call | tf_op jit(solution)/shard_map/split/pallas_call | solution.py:70
  3.3 4.1 %collective-permute-start = (bf16[128,512]{1,0:T(8,128)(2,1)}, bf16[128,512]{1,0:T(8,128)(2,1)S(1)}, u32[]{:S(2)}, u32[]{:S(2)}) collective-permute-start(bf16[128,512]{1,0:T(8,128)(2,1)} %get-tuple-element.41), channel_id=1, source_target_pairs={{0,16},{2,10},{4,20},{6,14},{8,24},{10,2},{12,28},{14,6},{16,0},{1... | collective-permute-start | bytes 393224 | tf_op jit(solution)/shard_map/ppermute | solution.py:270
  7.4 0.0 collective-permute-start.3
  7.4 2.1 %collective-permute-start.6 = (bf16[128,512]{1,0:T(8,128)(2,1)}, bf16[128,512]{1,0:T(8,128)(2,1)S(1)}, u32[]{:S(2)}, u32[]{:S(2)}) collective-permute-start(bf16[128,512]{1,0:T(8,128)(2,1)} %get-tuple-element.51), channel_id=1, source_target_pairs={{0,20},{2,14},{4,16},{6,10},{8,28},{10,6},{12,24},{14,2},{16,4},{1... | collective-permute-start | bytes 393224 | tf_op jit(solution)/shard_map/ppermute | solution.py:270
  9.5 0.5 collective-permute-start.9
  10.0 5.6 %collective-permute-start.12 = (bf16[128,512]{1,0:T(8,128)(2,1)}, bf16[128,512]{1,0:T(8,128)(2,1)}, u32[]{:S(2)}, u32[]{:S(2)}) collective-permute-start(bf16[128,512]{1,0:T(8,128)(2,1)} %get-tuple-element.60), channel_id=1, source_target_pairs={{0,24},{2,2},{4,28},{6,6},{8,16},{10,10},{12,20},{14,14},{16,8},{1... | collective-permute-start | bytes 393224 | tf_op jit(solution)/shard_map/ppermute | solution.py:270
  15.6 0.0 collective-permute-done.refs_0_
  15.7 0.1 collective-permute-start.14
  15.7 1.3 %pack_keys.1 = bf16[32,8,128]{2,1,0:T(8,128)(2,1)} custom-call(bf16[4,512]{1,0:T(4,128)(2,1)} %k_ref.1, bf16[4,512]{1,0:T(4,128)(2,1)} %v_ref.1), custom_call_target="tpu_custom_call" | custom-call | tf_op jit(solution)/shard_map/pack_keys/pallas_call | solution.py:245
  17.1 5.8 %all-to-all-start = ((bf16[32,8,128]{2,1,0:T(8,128)(2,1)}), bf16[32,8,128]{2,1,0:T(8,128)(2,1)S(1)}, u32[]{:S(2)}, u32[]{:S(2)}) async-start(bf16[32,8,128]{2,1,0:T(8,128)(2,1)} %pack_keys.1), calls=%async_computation | async-start | bytes 131072 | tf_op jit(solution)/shard_map/all_to_all | solution.py:251
  22.9 0.0 collective-permute-done.3.refs_1_
  22.9 4.6 %collective-permute-start.1 = (bf16[128,512]{1,0:T(8,128)(2,1)}, bf16[128,512]{1,0:T(8,128)(2,1)S(1)}, u32[]{:S(2)}, u32[]{:S(2)}) collective-permute-start(bf16[128,512]{1,0:T(8,128)(2,1)} %get-tuple-element.42), channel_id=1, source_target_pairs={{0,28},{2,6},{4,24},{6,2},{8,20},{10,14},{12,16},{14,10},{16,12},{... | collective-permute-start | bytes 393224 | tf_op jit(solution)/shard_map/ppermute | solution.py:270
  27.5 0.0 collective-permute-done.6.refs_2_
  27.5 0.0 collective-permute-start.4
  27.5 0.0 collective-permute-done.9.refs_3_
  27.5 0.1 collective-permute-start.7
  27.6 0.0 collective-permute-done.12.refs_4_
  27.6 2.5 %collective-permute-start.10 = (bf16[128,512]{1,0:T(8,128)(2,1)}, bf16[128,512]{1,0:T(8,128)(2,1)S(1)}, u32[]{:S(2)}, u32[]{:S(2)}) collective-permute-start(bf16[128,512]{1,0:T(8,128)(2,1)} %get-tuple-element.57), channel_id=1, source_target_pairs={{0,18},{2,8},{4,22},{6,12},{8,26},{10,0},{12,30},{14,4},{16,2},{18... | collective-permute-start | bytes 393224 | tf_op jit(solution)/shard_map/ppermute | solution.py:270
  30.0 0.0 collective-permute-done.14.refs_5_
  30.0 2.5 %collective-permute-start.13 = (bf16[128,512]{1,0:T(8,128)(2,1)}, bf16[128,512]{1,0:T(8,128)(2,1)S(1)}, u32[]{:S(2)}, u32[]{:S(2)}) collective-permute-start(bf16[128,512]{1,0:T(8,128)(2,1)} %get-tuple-element.61), channel_id=1, source_target_pairs={{0,12},{2,22},{4,8},{6,18},{8,4},{10,30},{12,0},{14,26},{16,28},{1... | collective-permute-start | bytes 393224 | tf_op jit(solution)/shard_map/ppermute | solution.py:270
  32.6 0.0 all-to-all-done
  32.6 0.6 fusion
  33.2 0.0 collective-permute-done.1.refs_6_
  33.2 0.3 collective-permute-start.15
  33.5 0.4 copy-done.10
  33.9 1.1 %collective-permute-done.4.refs_7_ = bf16[128,512]{1,0:T(8,128)(2,1)S(1)} collective-permute-done((bf16[128,512]{1,0:T(8,128)(2,1)}, bf16[128,512]{1,0:T(8,128)(2,1)S(1)}, u32[]{:S(2)}, u32[]{:S(2)}) %collective-permute-start.4) | collective-permute-done | bytes 131104 | tf_op jit(solution)/shard_map/ppermute | solution.py:270
  35.0 1.6 %collective-permute-start.2 = (bf16[128,512]{1,0:T(8,128)(2,1)}, bf16[128,512]{1,0:T(8,128)(2,1)S(1)}, u32[]{:S(2)}, u32[]{:S(2)}) collective-permute-start(bf16[128,512]{1,0:T(8,128)(2,1)} %get-tuple-element.43), channel_id=1, source_target_pairs={{0,0},{2,26},{4,4},{6,30},{8,8},{10,18},{12,12},{14,22},{16,16},{1... | collective-permute-start | bytes 393224 | tf_op jit(solution)/shard_map/ppermute | solution.py:270
  36.5 0.0 collective-permute-done.7.refs_0_
  36.5 6.9 %collective-permute-start.5 = (bf16[128,512]{1,0:T(8,128)(2,1)}, bf16[128,512]{1,0:T(8,128)(2,1)S(1)}, u32[]{:S(2)}, u32[]{:S(2)}) collective-permute-start(bf16[128,512]{1,0:T(8,128)(2,1)} %get-tuple-element.48), channel_id=1, source_target_pairs={{0,26},{2,0},{4,30},{6,4},{8,18},{10,8},{12,22},{14,12},{16,10},{1... | collective-permute-start | bytes 393224 | tf_op jit(solution)/shard_map/ppermute | solution.py:270
  43.5 0.0 collective-permute-done.10.refs_1_
  43.5 2.6 %collective-permute-start.8 = (bf16[128,512]{1,0:T(8,128)(2,1)}, bf16[128,512]{1,0:T(8,128)(2,1)S(1)}, u32[]{:S(2)}, u32[]{:S(2)}) collective-permute-start(bf16[128,512]{1,0:T(8,128)(2,1)} %get-tuple-element.53), channel_id=1, source_target_pairs={{0,4},{2,30},{4,0},{6,26},{8,12},{10,22},{12,8},{14,18},{16,20},{1... | collective-permute-start | bytes 393224 | tf_op jit(solution)/shard_map/ppermute | solution.py:270
  46.1 0.0 collective-permute-done.13.refs_2_
  46.1 6.6 %collective-permute-start.11 = (bf16[128,512]{1,0:T(8,128)(2,1)}, bf16[128,512]{1,0:T(8,128)(2,1)S(1)}, u32[]{:S(2)}, u32[]{:S(2)}) collective-permute-start(bf16[128,512]{1,0:T(8,128)(2,1)} %get-tuple-element.58), channel_id=1, source_target_pairs={{0,30},{2,4},{4,26},{6,0},{8,22},{10,12},{12,18},{14,8},{16,14},{1... | collective-permute-start | bytes 393224 | tf_op jit(solution)/shard_map/ppermute | solution.py:270
  52.7 0.0 copy-start.4
  52.7 5.9 %sources_8.1 = (bf16[2048,512]{1,0:T(8,128)(2,1)}, f32[128,128]{1,0:T(8,128)}, f32[128,128]{1,0:T(8,128)}) custom-call(s32[1]{0:T(128)} %bitcast.place_ref, bf16[128,512]{1,0:T(8,128)(2,1)} %copy-done.7, bf16[128,512]{1,0:T(8,128)(2,1)} %copy-done.8, bf16[128,512]{1,0:T(8,128)(2,1)} %copy-done.9, bf16[128,512]{1,0:T(8,128)(2,1)} %collective-permute-done.9.refs_3_, ...), custom_call_target="tpu_custom_call" | custom-call | tf_op jit(solution)/shard_map/sources_8/pallas_call | solution.py:191
  58.7 0.0 collective-permute-done.15.refs_3_
  58.7 0.0 copy-start.1
  58.8 1.6 %copy-done.1 = bf16[2048,512]{1,0:T(8,128)(2,1)S(1)} copy-done((bf16[2048,512]{1,0:T(8,128)(2,1)S(1)}, bf16[2048,512]{1,0:T(8,128)(2,1)}, u32[]{:S(2)}) %copy-start.1) | copy-done | bytes 2097176
  60.3 0.8 %copy-done.5 = f32[128,128]{1,0:T(8,128)S(1)} copy-done((f32[128,128]{1,0:T(8,128)S(1)}, f32[128,128]{1,0:T(8,128)}, u32[]{:S(2)}) %copy-start.5) | copy-done | bytes 65560
  61.2 0.8 %copy-done.6 = f32[128,128]{1,0:T(8,128)S(1)} copy-done((f32[128,128]{1,0:T(8,128)S(1)}, f32[128,128]{1,0:T(8,128)}, u32[]{:S(2)}) %copy-start.6) | copy-done | bytes 65560
  62.0 2.3 %sources_4.1 = (bf16[2048,512]{1,0:T(8,128)(2,1)}, f32[128,128]{1,0:T(8,128)S(1)}, f32[128,128]{1,0:T(8,128)S(1)}) custom-call(s32[1]{0:T(128)} %bitcast.place_ref, bf16[128,512]{1,0:T(8,128)(2,1)S(1)} %collective-permute-done.7.refs_0_, bf16[128,512]{1,0:T(8,128)(2,1)S(1)} %collective-permute-done.10.refs_1_, ...), custom_call_target="tpu_custom_call", output_to_operand_aliasing={{0}: (10, {})} | custom-call | tf_op jit(solution)/shard_map/sources_4/pallas_call | solution.py:191
  64.4 0.0 collective-permute-done.2.refs_0_
  64.4 0.0 collective-permute-done.5.refs_1_
  64.4 0.0 collective-permute-done.8.refs_2_
  64.4 0.0 collective-permute-done.11.refs_3_
  64.4 2.5 %sources_0.1 = (bf16[2048,512]{1,0:T(8,128)(2,1)}, f32[32,8,128]{2,1,0:T(8,128)S(1)}) custom-call(s32[1]{0:T(128)} %bitcast.place_ref, bf16[128,512]{1,0:T(8,128)(2,1)S(1)} %collective-permute-done.2.refs_0_, bf16[128,512]{1,0:T(8,128)(2,1)S(1)} %collective-permute-done.5.refs_1_, ...), custom_call_target="tpu_custom_call", output_to_operand_aliasing={{0}: (10, {})} | custom-call | tf_op jit(solution)/shard_map/sources_0/pallas_call | solution.py:191
  66.9 11.1 %all_to_all.10.terms_ref = f32[32,8,128]{2,1,0:T(8,128)S(1)} all-to-all(f32[32,8,128]{2,1,0:T(8,128)S(1)} %get-tuple-element.72), channel_id=1, replica_groups=mesh['head'=16,'ctx'=2] {'head','ctx'}, dimensions={0} | all-to-all | bytes 262144 | tf_op jit(solution)/shard_map/all_to_all | solution.py:298
  78.0 0.6 sum_terms.1
  (18 shorter events, 0.0 us)
Async XLA Ops:
  3.3 12.3 %collective-permute-start = (bf16[128,512]{1,0:T(8,128)(2,1)}, bf16[128,512]{1,0:T(8,128)(2,1)S(1)}, u32[]{:S(2)}, u32[]{:S(2)}) collective-permute-start(bf16[128,512]{1,0:T(8,128)(2,1)} %get-tuple-element.41), channel_id=1, source_target_pairs={{0,16},{2,10},{4,20},{6,14},{8,24},{10,2},{12,28},{14,6},{16,0},{1... | collective-permute-start | bytes 393224 | tf_op jit(solution)/shard_map/ppermute | solution.py:270
  7.4 15.4 %collective-permute-start.3 = (bf16[128,512]{1,0:T(8,128)(2,1)}, bf16[128,512]{1,0:T(8,128)(2,1)S(1)}, u32[]{:S(2)}, u32[]{:S(2)}) collective-permute-start(bf16[128,512]{1,0:T(8,128)(2,1)} %get-tuple-element.46), channel_id=1, source_target_pairs={{0,10},{2,16},{4,14},{6,20},{8,2},{10,24},{12,6},{14,28},{16,26},{... | collective-permute-start | bytes 393224 | tf_op jit(solution)/shard_map/ppermute | solution.py:270
  7.4 20.0 %collective-permute-start.6 = (bf16[128,512]{1,0:T(8,128)(2,1)}, bf16[128,512]{1,0:T(8,128)(2,1)S(1)}, u32[]{:S(2)}, u32[]{:S(2)}) collective-permute-start(bf16[128,512]{1,0:T(8,128)(2,1)} %get-tuple-element.51), channel_id=1, source_target_pairs={{0,20},{2,14},{4,16},{6,10},{8,28},{10,6},{12,24},{14,2},{16,4},{1... | collective-permute-start | bytes 393224 | tf_op jit(solution)/shard_map/ppermute | solution.py:270
  9.5 17.9 %collective-permute-start.9 = (bf16[128,512]{1,0:T(8,128)(2,1)}, bf16[128,512]{1,0:T(8,128)(2,1)}, u32[]{:S(2)}, u32[]{:S(2)}) collective-permute-start(bf16[128,512]{1,0:T(8,128)(2,1)} %get-tuple-element.56), channel_id=1, source_target_pairs={{0,14},{2,20},{4,10},{6,16},{8,6},{10,28},{12,2},{14,24},{16,30},{... | collective-permute-start | bytes 393224 | tf_op jit(solution)/shard_map/ppermute | solution.py:270
  10.0 17.6 %collective-permute-start.12 = (bf16[128,512]{1,0:T(8,128)(2,1)}, bf16[128,512]{1,0:T(8,128)(2,1)}, u32[]{:S(2)}, u32[]{:S(2)}) collective-permute-start(bf16[128,512]{1,0:T(8,128)(2,1)} %get-tuple-element.60), channel_id=1, source_target_pairs={{0,24},{2,2},{4,28},{6,6},{8,16},{10,10},{12,20},{14,14},{16,8},{1... | collective-permute-start | bytes 393224 | tf_op jit(solution)/shard_map/ppermute | solution.py:270
  15.7 37.1 %copy-start.7 = (bf16[128,512]{1,0:T(8,128)(2,1)}, bf16[128,512]{1,0:T(8,128)(2,1)S(1)}, u32[]{:S(2)}) copy-start(bf16[128,512]{1,0:T(8,128)(2,1)S(1)} %collective-permute-done.refs_0_) | copy-start | bytes 393220
  15.7 14.4 %collective-permute-start.14 = (bf16[128,512]{1,0:T(8,128)(2,1)}, bf16[128,512]{1,0:T(8,128)(2,1)}, u32[]{:S(2)}, u32[]{:S(2)}) collective-permute-start(bf16[128,512]{1,0:T(8,128)(2,1)} %get-tuple-element.63), channel_id=1, source_target_pairs={{0,2},{2,24},{4,6},{6,28},{8,10},{10,16},{12,14},{14,20},{16,18},{... | collective-permute-start | bytes 393224 | tf_op jit(solution)/shard_map/ppermute | solution.py:270
  17.1 15.5 %all-to-all-start = ((bf16[32,8,128]{2,1,0:T(8,128)(2,1)}), bf16[32,8,128]{2,1,0:T(8,128)(2,1)S(1)}, u32[]{:S(2)}, u32[]{:S(2)}) async-start(bf16[32,8,128]{2,1,0:T(8,128)(2,1)} %pack_keys.1), calls=%async_computation | async-start | bytes 131072 | tf_op jit(solution)/shard_map/all_to_all | solution.py:251
  22.9 29.8 %copy-start.8 = (bf16[128,512]{1,0:T(8,128)(2,1)}, bf16[128,512]{1,0:T(8,128)(2,1)S(1)}, u32[]{:S(2)}) copy-start(bf16[128,512]{1,0:T(8,128)(2,1)S(1)} %collective-permute-done.3.refs_1_) | copy-start | bytes 393220
  22.9 10.3 %collective-permute-start.1 = (bf16[128,512]{1,0:T(8,128)(2,1)}, bf16[128,512]{1,0:T(8,128)(2,1)S(1)}, u32[]{:S(2)}, u32[]{:S(2)}) collective-permute-start(bf16[128,512]{1,0:T(8,128)(2,1)} %get-tuple-element.42), channel_id=1, source_target_pairs={{0,28},{2,6},{4,24},{6,2},{8,20},{10,14},{12,16},{14,10},{16,12},{... | collective-permute-start | bytes 393224 | tf_op jit(solution)/shard_map/ppermute | solution.py:270
  27.5 25.2 %copy-start.9 = (bf16[128,512]{1,0:T(8,128)(2,1)}, bf16[128,512]{1,0:T(8,128)(2,1)S(1)}, u32[]{:S(2)}) copy-start(bf16[128,512]{1,0:T(8,128)(2,1)S(1)} %collective-permute-done.6.refs_2_) | copy-start | bytes 393220
  27.5 7.5 %collective-permute-start.4 = (bf16[128,512]{1,0:T(8,128)(2,1)}, bf16[128,512]{1,0:T(8,128)(2,1)S(1)}, u32[]{:S(2)}, u32[]{:S(2)}) collective-permute-start(bf16[128,512]{1,0:T(8,128)(2,1)} %get-tuple-element.47), channel_id=1, source_target_pairs={{0,6},{2,28},{4,2},{6,24},{8,14},{10,20},{12,10},{14,16},{16,22},{... | collective-permute-start | bytes 393224 | tf_op jit(solution)/shard_map/ppermute | solution.py:270
  27.5 9.0 %collective-permute-start.7 = (bf16[128,512]{1,0:T(8,128)(2,1)}, bf16[128,512]{1,0:T(8,128)(2,1)S(1)}, u32[]{:S(2)}, u32[]{:S(2)}) collective-permute-start(bf16[128,512]{1,0:T(8,128)(2,1)} %get-tuple-element.52), channel_id=1, source_target_pairs={{0,8},{2,18},{4,12},{6,22},{8,0},{10,26},{12,4},{14,30},{16,24},{1... | collective-permute-start | bytes 393224 | tf_op jit(solution)/shard_map/ppermute | solution.py:270
  27.6 15.9 %collective-permute-start.10 = (bf16[128,512]{1,0:T(8,128)(2,1)}, bf16[128,512]{1,0:T(8,128)(2,1)S(1)}, u32[]{:S(2)}, u32[]{:S(2)}) collective-permute-start(bf16[128,512]{1,0:T(8,128)(2,1)} %get-tuple-element.57), channel_id=1, source_target_pairs={{0,18},{2,8},{4,22},{6,12},{8,26},{10,0},{12,30},{14,4},{16,2},{18... | collective-permute-start | bytes 393224 | tf_op jit(solution)/shard_map/ppermute | solution.py:270
  30.0 16.1 %collective-permute-start.13 = (bf16[128,512]{1,0:T(8,128)(2,1)}, bf16[128,512]{1,0:T(8,128)(2,1)S(1)}, u32[]{:S(2)}, u32[]{:S(2)}) collective-permute-start(bf16[128,512]{1,0:T(8,128)(2,1)} %get-tuple-element.61), channel_id=1, source_target_pairs={{0,12},{2,22},{4,8},{6,18},{8,4},{10,30},{12,0},{14,26},{16,28},{1... | collective-permute-start | bytes 393224 | tf_op jit(solution)/shard_map/ppermute | solution.py:270
  33.2 0.7 copy-start.10
  33.2 25.5 %collective-permute-start.15 = (bf16[128,512]{1,0:T(8,128)(2,1)}, bf16[128,512]{1,0:T(8,128)(2,1)S(1)}, u32[]{:S(2)}, u32[]{:S(2)}) collective-permute-start(bf16[128,512]{1,0:T(8,128)(2,1)} %get-tuple-element.64), channel_id=1, source_target_pairs={{0,22},{2,12},{4,18},{6,8},{8,30},{10,4},{12,26},{14,0},{16,6},{18... | collective-permute-start | bytes 393224 | tf_op jit(solution)/shard_map/ppermute | solution.py:270
  35.0 8.5 %copy-start.11 = (bf16[128,512]{1,0:T(8,128)(2,1)}, bf16[128,512]{1,0:T(8,128)(2,1)S(1)}, u32[]{:S(2)}) copy-start(bf16[128,512]{1,0:T(8,128)(2,1)S(1)} %collective-permute-done.4.refs_7_) | copy-start | bytes 393220
  35.0 29.4 %collective-permute-start.2 = (bf16[128,512]{1,0:T(8,128)(2,1)}, bf16[128,512]{1,0:T(8,128)(2,1)S(1)}, u32[]{:S(2)}, u32[]{:S(2)}) collective-permute-start(bf16[128,512]{1,0:T(8,128)(2,1)} %get-tuple-element.43), channel_id=1, source_target_pairs={{0,0},{2,26},{4,4},{6,30},{8,8},{10,18},{12,12},{14,22},{16,16},{1... | collective-permute-start | bytes 393224 | tf_op jit(solution)/shard_map/ppermute | solution.py:270
  36.5 27.8 %collective-permute-start.5 = (bf16[128,512]{1,0:T(8,128)(2,1)}, bf16[128,512]{1,0:T(8,128)(2,1)S(1)}, u32[]{:S(2)}, u32[]{:S(2)}) collective-permute-start(bf16[128,512]{1,0:T(8,128)(2,1)} %get-tuple-element.48), channel_id=1, source_target_pairs={{0,26},{2,0},{4,30},{6,4},{8,18},{10,8},{12,22},{14,12},{16,10},{1... | collective-permute-start | bytes 393224 | tf_op jit(solution)/shard_map/ppermute | solution.py:270
  43.5 20.9 %collective-permute-start.8 = (bf16[128,512]{1,0:T(8,128)(2,1)}, bf16[128,512]{1,0:T(8,128)(2,1)S(1)}, u32[]{:S(2)}, u32[]{:S(2)}) collective-permute-start(bf16[128,512]{1,0:T(8,128)(2,1)} %get-tuple-element.53), channel_id=1, source_target_pairs={{0,4},{2,30},{4,0},{6,26},{8,12},{10,22},{12,8},{14,18},{16,20},{1... | collective-permute-start | bytes 393224 | tf_op jit(solution)/shard_map/ppermute | solution.py:270
  46.1 18.3 %collective-permute-start.11 = (bf16[128,512]{1,0:T(8,128)(2,1)}, bf16[128,512]{1,0:T(8,128)(2,1)S(1)}, u32[]{:S(2)}, u32[]{:S(2)}) collective-permute-start(bf16[128,512]{1,0:T(8,128)(2,1)} %get-tuple-element.58), channel_id=1, source_target_pairs={{0,30},{2,4},{4,26},{6,0},{8,22},{10,12},{12,18},{14,8},{16,14},{1... | collective-permute-start | bytes 393224 | tf_op jit(solution)/shard_map/ppermute | solution.py:270
  52.7 6.0 %copy-start = (bf16[2048,512]{1,0:T(8,128)(2,1)S(1)}, bf16[2048,512]{1,0:T(8,128)(2,1)}, u32[]{:S(2)}) copy-start(bf16[2048,512]{1,0:T(8,128)(2,1)} %refs_4_.3) | copy-start | bytes 6291460
  52.7 6.0 %copy-start.2 = (bf16[32,4,128]{2,1,0:T(4,128)(2,1)S(1)}, bf16[32,4,128]{2,1,0:T(4,128)(2,1)}, u32[]{:S(2)}) copy-start(bf16[32,4,128]{2,1,0:T(4,128)(2,1)} %get-tuple-element.75) | copy-start | bytes 98308
  52.7 6.0 %copy-start.3 = (bf16[32,4,128]{2,1,0:T(4,128)(2,1)S(1)}, bf16[32,4,128]{2,1,0:T(4,128)(2,1)}, u32[]{:S(2)}) copy-start(bf16[32,4,128]{2,1,0:T(4,128)(2,1)} %get-tuple-element.76) | copy-start | bytes 98308
  52.7 6.0 %copy-start.4 = (f32[4,2048]{1,0:T(4,128)S(1)}, f32[4,2048]{1,0:T(4,128)}, u32[]{:S(2)}) copy-start(f32[4,2048]{1,0:T(4,128)} %refs_6_.3) | copy-start | bytes 98308
  58.7 1.6 %copy-start.1 = (bf16[2048,512]{1,0:T(8,128)(2,1)S(1)}, bf16[2048,512]{1,0:T(8,128)(2,1)}, u32[]{:S(2)}) copy-start(bf16[2048,512]{1,0:T(8,128)(2,1)} %refs_5_.3) | copy-start | bytes 6291460
  60.3 0.8 %copy-start.5 = (f32[128,128]{1,0:T(8,128)S(1)}, f32[128,128]{1,0:T(8,128)}, u32[]{:S(2)}) copy-start(f32[128,128]{1,0:T(8,128)} %get-tuple-element.66.refs_10_) | copy-start | bytes 196612
  61.2 0.8 %copy-start.6 = (f32[128,128]{1,0:T(8,128)S(1)}, f32[128,128]{1,0:T(8,128)}, u32[]{:S(2)}) copy-start(f32[128,128]{1,0:T(8,128)} %get-tuple-element.67.refs_11_) | copy-start | bytes 196612

commit v6 on v5

--- a/solution.py
+++ b/solution.py
@@ -284,14 +284,17 @@
             carried,
         )
 
-    near = heads_axis // 2
+    half, carried = heads_axis // 2, []
     for place_in_order in range(heads_axis):
-        gates = [arrived[place_in_order - 6]] if 6 and place_in_order >= 6 else []
-        if place_in_order >= near + 4:
-            gates.append(k)
+        gates = [arrived[place_in_order - 0]] if 0 and place_in_order >= 0 else []
+        if place_in_order == half + 5:
+            carried = compute(0, half // 2, carried)
+        if place_in_order == half + 6:
+            carried = compute(half // 2, half // 2, carried)
+        if carried:
+            gates.append(carried[1])
         send(*gates)
-    carried = compute(0, near, [])
-    for start in range(near, heads_axis, BATCH):
+    for start in range(half, heads_axis, BATCH):
         carried = compute(start, BATCH, carried)
     dq, terms = carried
 

time: 79.1 us -> 73.2 us (0.925)
  starting transfers between devices: 45.8 us -> 35.8 us
  waiting for transfers between devices: 1.16 us -> 4.1 us
  blocking collectives: 11.1 us -> 12.5 us
    ppermute x16, starting transfers between devices: 40 us -> 30.1 us  [send(): arrived.append(lax.ppermute(piece, 'head', pairs))]
    ppermute x16, waiting for transfers between devices: 1.16 us -> 4.09 us  [send(): arrived.append(lax.ppermute(piece, 'head', pairs))]
    all_to_all x1, blocking collectives: 11.1 us -> 12.5 us  [on_device(): lax.all_to_all(terms, ('head', 'ctx'), split_axis=0, concat_axis=0, tiled...]
    unnamed x24 -> x28, local copies, waits for them, and re-layouts: 3.65 us -> 3.31 us
    pallas_call x3 -> x4, Pallas kernels: 10.8 us -> 10.9 us  [attention(): pl.pallas_call(functools.partial(attention_kernel, first, owners > 0, pai...]
  transfers between devices with their start and end apart: 17 -> 17, of which waited for: 1 -> 2; matrix products, arithmetic and copies ran while one was open for 1% -> 1% of each run, Pallas kernels for 12% -> 13%
where the time goes in v6:
time: 73.2 us; the launch traced here: 72.7 us
  starting transfers between devices  35.8 us (49%)
  Pallas kernels  15.5 us (21%)
  blocking collectives  12.5 us (17%)
  waiting for transfers between devices  4.1 us (6%)
  local copies, waits for them, and re-layouts  3.96 us (5%)
  between operations  0.82 us (1%)
    ppermute x16, starting transfers between devices, send(): arrived.append(lax.ppermute(piece, 'head', pairs))  30.1 us
    all_to_all x1, blocking collectives, on_device(): lax.all_to_all(terms, ('head', 'ctx'), split_axis=0, concat_axis=0, tiled...  12.5 us
    pallas_call x4, Pallas kernels, attention(): pl.pallas_call(functools.partial(attention_kernel, first, owners > 0, pai...  10.9 us
    all_to_all x1, starting transfers between devices, own_group(): lax.all_to_all(mine, ('head', 'ctx'), split_axis=0, concat_axis=0, tiled=...  5.78 us
    ppermute x16, waiting for transfers between devices, send(): arrived.append(lax.ppermute(piece, 'head', pairs))  4.09 us
    unnamed x28, local copies, waits for them, and re-layouts  3.31 us
    pallas_call x1, Pallas kernels, split(): pl.pallas_call(functools.partial(split_kernel, batches(dests)), in_specs=...  2.69 us
  transfers between devices with their start and end apart: 17, of which 2 were waited for; matrix products, arithmetic and copies ran while one was open for 1% of the time, Pallas kernels for 13%

profile of v6, /device:TPU:0, one launch (start us, length us, event | category | flops | bytes accessed | tf_op | source)
XLA Modules:
  0.0 72.7 jit_solution(14340156820846967388)
XLA Ops:
  0.6 2.7 %split.1 = (bf16[128,512]{1,0:T(8,128)(2,1)}, bf16[128,512]{1,0:T(8,128)(2,1)}, bf16[128,512]{1,0:T(8,128)(2,1)}, bf16[128,512]{1,0:T(8,128)(2,1)}, bf16[128,512...) custom-call(bf16[128,8192]{1,0:T(8,128)(2,1)} %dout_ref.1), custom_call_target="tpu_custom_call" | custom-call | tf_op jit(solution)/shard_map/split/pallas_call | solution.py:70
  3.3 4.1 %collective-permute-start.1 = (bf16[128,512]{1,0:T(8,128)(2,1)}, bf16[128,512]{1,0:T(8,128)(2,1)S(1)}, u32[]{:S(2)}, u32[]{:S(2)}) collective-permute-start(bf16[128,512]{1,0:T(8,128)(2,1)} %get-tuple-element.37), channel_id=1, source_target_pairs={{0,16},{2,10},{4,20},{6,14},{8,24},{10,2},{12,28},{14,6},{16,0},{1... | collective-permute-start | bytes 393224 | tf_op jit(solution)/shard_map/ppermute | solution.py:270
  7.4 0.0 collective-permute-start.2
  7.4 2.1 %collective-permute-start.3 = (bf16[128,512]{1,0:T(8,128)(2,1)}, bf16[128,512]{1,0:T(8,128)(2,1)S(1)}, u32[]{:S(2)}, u32[]{:S(2)}) collective-permute-start(bf16[128,512]{1,0:T(8,128)(2,1)} %get-tuple-element.39), channel_id=1, source_target_pairs={{0,20},{2,14},{4,16},{6,10},{8,28},{10,6},{12,24},{14,2},{16,4},{1... | collective-permute-start | bytes 393224 | tf_op jit(solution)/shard_map/ppermute | solution.py:270
  9.5 0.5 collective-permute-start.4
  10.0 5.6 %collective-permute-start.6 = (bf16[128,512]{1,0:T(8,128)(2,1)}, bf16[128,512]{1,0:T(8,128)(2,1)S(1)}, u32[]{:S(2)}, u32[]{:S(2)}) collective-permute-start(bf16[128,512]{1,0:T(8,128)(2,1)} %get-tuple-element.44), channel_id=1, source_target_pairs={{0,24},{2,2},{4,28},{6,6},{8,16},{10,10},{12,20},{14,14},{16,8},{1... | collective-permute-start | bytes 393224 | tf_op jit(solution)/shard_map/ppermute | solution.py:270
  15.6 0.0 collective-permute-done.1.refs_0_
  15.7 0.1 collective-permute-start.7
  15.7 1.3 %pack_keys.1 = bf16[32,8,128]{2,1,0:T(8,128)(2,1)} custom-call(bf16[4,512]{1,0:T(4,128)(2,1)} %k_ref.1, bf16[4,512]{1,0:T(4,128)(2,1)} %v_ref.1), custom_call_target="tpu_custom_call" | custom-call | tf_op jit(solution)/shard_map/pack_keys/pallas_call | solution.py:245
  17.1 5.8 %all-to-all-start = ((bf16[32,8,128]{2,1,0:T(8,128)(2,1)}), bf16[32,8,128]{2,1,0:T(8,128)(2,1)S(1)}, u32[]{:S(2)}, u32[]{:S(2)}) async-start(bf16[32,8,128]{2,1,0:T(8,128)(2,1)} %pack_keys.1), calls=%async_computation | async-start | bytes 131072 | tf_op jit(solution)/shard_map/all_to_all | solution.py:251
  22.9 0.0 collective-permute-done.2.refs_1_
  22.9 4.6 %collective-permute-start.8 = (bf16[128,512]{1,0:T(8,128)(2,1)}, bf16[128,512]{1,0:T(8,128)(2,1)S(1)}, u32[]{:S(2)}, u32[]{:S(2)}) collective-permute-start(bf16[128,512]{1,0:T(8,128)(2,1)} %get-tuple-element.46), channel_id=1, source_target_pairs={{0,28},{2,6},{4,24},{6,2},{8,20},{10,14},{12,16},{14,10},{16,12},{... | collective-permute-start | bytes 393224 | tf_op jit(solution)/shard_map/ppermute | solution.py:270
  27.5 0.0 collective-permute-done.3.refs_2_
  27.5 0.0 collective-permute-start.9
  27.5 0.0 collective-permute-done.4.refs_3_
  27.5 0.1 collective-permute-start.12
  27.6 0.0 collective-permute-done.6.refs_0_
  27.6 2.4 %collective-permute-start.13 = (bf16[128,512]{1,0:T(8,128)(2,1)}, bf16[128,512]{1,0:T(8,128)(2,1)S(1)}, u32[]{:S(2)}, u32[]{:S(2)}) collective-permute-start(bf16[128,512]{1,0:T(8,128)(2,1)} %get-tuple-element.55), channel_id=1, source_target_pairs={{0,18},{2,8},{4,22},{6,12},{8,26},{10,0},{12,30},{14,4},{16,2},{18... | collective-permute-start | bytes 393224 | tf_op jit(solution)/shard_map/ppermute | solution.py:270
  30.0 0.0 collective-permute-done.7.refs_1_
  30.0 2.5 %collective-permute-start.14 = (bf16[128,512]{1,0:T(8,128)(2,1)}, bf16[128,512]{1,0:T(8,128)(2,1)S(1)}, u32[]{:S(2)}, u32[]{:S(2)}) collective-permute-start(bf16[128,512]{1,0:T(8,128)(2,1)} %get-tuple-element.56), channel_id=1, source_target_pairs={{0,12},{2,22},{4,8},{6,18},{8,4},{10,30},{12,0},{14,26},{16,28},{1... | collective-permute-start | bytes 393224 | tf_op jit(solution)/shard_map/ppermute | solution.py:270
  32.6 0.0 all-to-all-done
  32.6 0.6 fusion
  33.2 0.0 copy-start
  33.3 0.0 copy-start.4
  33.3 3.8 %sources_8.1 = (bf16[2048,512]{1,0:T(8,128)(2,1)}, f32[128,128]{1,0:T(8,128)}, f32[128,128]{1,0:T(8,128)}) custom-call(s32[1]{0:T(128)} %bitcast.place_ref, bf16[128,512]{1,0:T(8,128)(2,1)} %copy-done.7, bf16[128,512]{1,0:T(8,128)(2,1)} %copy-done.8, bf16[128,512]{1,0:T(8,128)(2,1)} %copy-done.9, bf16[128,512]{1,0:T(8,128)(2,1)} %copy-done.10, ...), custom_call_target="tpu_custom_call" | custom-call | tf_op jit(solution)/shard_map/sources_8/pallas_call | solution.py:191
  37.0 0.0 collective-permute-done.8.refs_2_
  37.0 1.6 %collective-permute-start = (bf16[128,512]{1,0:T(8,128)(2,1)}, bf16[128,512]{1,0:T(8,128)(2,1)S(1)}, u32[]{:S(2)}, u32[]{:S(2)}) collective-permute-start(bf16[128,512]{1,0:T(8,128)(2,1)} %get-tuple-element.35), channel_id=1, source_target_pairs={{0,0},{2,26},{4,4},{6,30},{8,8},{10,18},{12,12},{14,22},{16,16},{1... | collective-permute-start | bytes 393224 | tf_op jit(solution)/shard_map/ppermute | solution.py:270
  38.6 0.0 collective-permute-done.9.refs_3_
  38.6 1.4 %collective-permute-start.15 = (bf16[128,512]{1,0:T(8,128)(2,1)}, bf16[128,512]{1,0:T(8,128)(2,1)S(1)}, u32[]{:S(2)}, u32[]{:S(2)}) collective-permute-start(bf16[128,512]{1,0:T(8,128)(2,1)} %get-tuple-element.57), channel_id=1, source_target_pairs={{0,22},{2,12},{4,18},{6,8},{8,30},{10,4},{12,26},{14,0},{16,6},{18... | collective-permute-start | bytes 393224 | tf_op jit(solution)/shard_map/ppermute | solution.py:270
  40.0 0.0 copy-start.1
  40.0 1.6 %copy-done.1 = bf16[2048,512]{1,0:T(8,128)(2,1)S(1)} copy-done((bf16[2048,512]{1,0:T(8,128)(2,1)S(1)}, bf16[2048,512]{1,0:T(8,128)(2,1)}, u32[]{:S(2)}) %copy-start.1) | copy-done | bytes 2097176
  41.6 0.8 %copy-done.5 = f32[128,128]{1,0:T(8,128)S(1)} copy-done((f32[128,128]{1,0:T(8,128)S(1)}, f32[128,128]{1,0:T(8,128)}, u32[]{:S(2)}) %copy-start.5) | copy-done | bytes 65560
  42.4 0.8 %copy-done.6 = f32[128,128]{1,0:T(8,128)S(1)} copy-done((f32[128,128]{1,0:T(8,128)S(1)}, f32[128,128]{1,0:T(8,128)}, u32[]{:S(2)}) %copy-start.6) | copy-done | bytes 65560
  43.3 2.3 %sources_12.1 = (bf16[2048,512]{1,0:T(8,128)(2,1)}, f32[128,128]{1,0:T(8,128)S(1)}, f32[128,128]{1,0:T(8,128)S(1)}) custom-call(s32[1]{0:T(128)} %bitcast.place_ref, bf16[128,512]{1,0:T(8,128)(2,1)S(1)} %collective-permute-done.6.refs_0_, bf16[128,512]{1,0:T(8,128)(2,1)S(1)} %collective-permute-done.7.refs_1_, ...), custom_call_target="tpu_custom_call", output_to_operand_aliasing={{0}: (10, {})} | custom-call | tf_op jit(solution)/shard_map/sources_12/pallas_call | solution.py:191
  45.6 0.0 collective-permute-done.12.refs_0_
  45.6 2.4 %collective-permute-start.5 = (bf16[128,512]{1,0:T(8,128)(2,1)S(1)}, bf16[128,512]{1,0:T(8,128)(2,1)S(1)}, u32[]{:S(2)}, u32[]{:S(2)}) collective-permute-start(bf16[128,512]{1,0:T(8,128)(2,1)S(1)} %copy-done.13), channel_id=1, source_target_pairs={{0,26},{2,0},{4,30},{6,4},{8,18},{10,8},{12,22},{14,12},{16,10},{1... | collective-permute-start | bytes 393224 | tf_op jit(solution)/shard_map/ppermute | solution.py:270
  48.0 0.0 collective-permute-done.13.refs_1_
  48.0 1.5 %collective-permute-start.10 = (bf16[128,512]{1,0:T(8,128)(2,1)S(1)}, bf16[128,512]{1,0:T(8,128)(2,1)S(1)}, u32[]{:S(2)}, u32[]{:S(2)}) collective-permute-start(bf16[128,512]{1,0:T(8,128)(2,1)S(1)} %copy-done.12), channel_id=1, source_target_pairs={{0,4},{2,30},{4,0},{6,26},{8,12},{10,22},{12,8},{14,18},{16,20},{1... | collective-permute-start | bytes 393224 | tf_op jit(solution)/shard_map/ppermute | solution.py:270
  49.5 0.0 collective-permute-done.14.refs_2_
  49.5 1.3 %collective-permute-start.11 = (bf16[128,512]{1,0:T(8,128)(2,1)S(1)}, bf16[128,512]{1,0:T(8,128)(2,1)S(1)}, u32[]{:S(2)}, u32[]{:S(2)}) collective-permute-start(bf16[128,512]{1,0:T(8,128)(2,1)S(1)} %copy-done.11), channel_id=1, source_target_pairs={{0,30},{2,4},{4,26},{6,0},{8,22},{10,12},{12,18},{14,8},{16,14},{1... | collective-permute-start | bytes 393224 | tf_op jit(solution)/shard_map/ppermute | solution.py:270
  50.8 2.3 %sources_4.1 = (bf16[2048,512]{1,0:T(8,128)(2,1)}, f32[128,128]{1,0:T(8,128)S(1)}, f32[128,128]{1,0:T(8,128)S(1)}) custom-call(s32[1]{0:T(128)} %bitcast.place_ref, bf16[128,512]{1,0:T(8,128)(2,1)S(1)} %collective-permute-done.12.refs_0_, bf16[128,512]{1,0:T(8,128)(2,1)S(1)} %collective-permute-done.13.refs_1_, ...), custom_call_target="tpu_custom_call", output_to_operand_aliasing={{0}: (10, {})} | custom-call | tf_op jit(solution)/shard_map/sources_4/pallas_call | solution.py:191
  53.1 0.0 collective-permute-done.refs_0_
  53.1 0.0 collective-permute-done.5.refs_1_
  53.1 3.0 %collective-permute-done.10.refs_2_ = bf16[128,512]{1,0:T(8,128)(2,1)S(1)} collective-permute-done((bf16[128,512]{1,0:T(8,128)(2,1)S(1)}, bf16[128,512]{1,0:T(8,128)(2,1)S(1)}, u32[]{:S(2)}, u32[]{:S(2)}) %collective-permute-start.10) | collective-permute-done | bytes 131104 | tf_op jit(solution)/shard_map/ppermute | solution.py:270
  56.2 1.0 %collective-permute-done.11.refs_3_ = bf16[128,512]{1,0:T(8,128)(2,1)S(1)} collective-permute-done((bf16[128,512]{1,0:T(8,128)(2,1)S(1)}, bf16[128,512]{1,0:T(8,128)(2,1)S(1)}, u32[]{:S(2)}, u32[]{:S(2)}) %collective-permute-start.11) | collective-permute-done | bytes 131104 | tf_op jit(solution)/shard_map/ppermute | solution.py:270
  57.2 2.4 %sources_0.1 = (bf16[2048,512]{1,0:T(8,128)(2,1)}, f32[32,8,128]{2,1,0:T(8,128)S(1)}) custom-call(s32[1]{0:T(128)} %bitcast.place_ref, bf16[128,512]{1,0:T(8,128)(2,1)S(1)} %collective-permute-done.refs_0_, bf16[128,512]{1,0:T(8,128)(2,1)S(1)} %collective-permute-done.5.refs_1_, ...), custom_call_target="tpu_custom_call", output_to_operand_aliasing={{0}: (10, {})} | custom-call | tf_op jit(solution)/shard_map/sources_0/pallas_call | solution.py:191
  59.6 12.5 %all_to_all.10.terms_ref = f32[32,8,128]{2,1,0:T(8,128)S(1)} all-to-all(f32[32,8,128]{2,1,0:T(8,128)S(1)} %get-tuple-element.64), channel_id=1, replica_groups=mesh['head'=16,'ctx'=2] {'head','ctx'}, dimensions={0} | all-to-all | bytes 262144 | tf_op jit(solution)/shard_map/all_to_all | solution.py:301
  72.1 0.6 sum_terms.1
  (23 shorter events, 0.0 us)
Async XLA Ops:
  3.3 12.3 %collective-permute-start.1 = (bf16[128,512]{1,0:T(8,128)(2,1)}, bf16[128,512]{1,0:T(8,128)(2,1)S(1)}, u32[]{:S(2)}, u32[]{:S(2)}) collective-permute-start(bf16[128,512]{1,0:T(8,128)(2,1)} %get-tuple-element.37), channel_id=1, source_target_pairs={{0,16},{2,10},{4,20},{6,14},{8,24},{10,2},{12,28},{14,6},{16,0},{1... | collective-permute-start | bytes 393224 | tf_op jit(solution)/shard_map/ppermute | solution.py:270
  7.4 15.4 %collective-permute-start.2 = (bf16[128,512]{1,0:T(8,128)(2,1)}, bf16[128,512]{1,0:T(8,128)(2,1)S(1)}, u32[]{:S(2)}, u32[]{:S(2)}) collective-permute-start(bf16[128,512]{1,0:T(8,128)(2,1)} %get-tuple-element.38), channel_id=1, source_target_pairs={{0,10},{2,16},{4,14},{6,20},{8,2},{10,24},{12,6},{14,28},{16,26},{... | collective-permute-start | bytes 393224 | tf_op jit(solution)/shard_map/ppermute | solution.py:270
  7.4 20.0 %collective-permute-start.3 = (bf16[128,512]{1,0:T(8,128)(2,1)}, bf16[128,512]{1,0:T(8,128)(2,1)S(1)}, u32[]{:S(2)}, u32[]{:S(2)}) collective-permute-start(bf16[128,512]{1,0:T(8,128)(2,1)} %get-tuple-element.39), channel_id=1, source_target_pairs={{0,20},{2,14},{4,16},{6,10},{8,28},{10,6},{12,24},{14,2},{16,4},{1... | collective-permute-start | bytes 393224 | tf_op jit(solution)/shard_map/ppermute | solution.py:270
  9.5 17.9 %collective-permute-start.4 = (bf16[128,512]{1,0:T(8,128)(2,1)}, bf16[128,512]{1,0:T(8,128)(2,1)S(1)}, u32[]{:S(2)}, u32[]{:S(2)}) collective-permute-start(bf16[128,512]{1,0:T(8,128)(2,1)} %get-tuple-element.40), channel_id=1, source_target_pairs={{0,14},{2,20},{4,10},{6,16},{8,6},{10,28},{12,2},{14,24},{16,30},{... | collective-permute-start | bytes 393224 | tf_op jit(solution)/shard_map/ppermute | solution.py:270
  10.0 17.6 %collective-permute-start.6 = (bf16[128,512]{1,0:T(8,128)(2,1)}, bf16[128,512]{1,0:T(8,128)(2,1)S(1)}, u32[]{:S(2)}, u32[]{:S(2)}) collective-permute-start(bf16[128,512]{1,0:T(8,128)(2,1)} %get-tuple-element.44), channel_id=1, source_target_pairs={{0,24},{2,2},{4,28},{6,6},{8,16},{10,10},{12,20},{14,14},{16,8},{1... | collective-permute-start | bytes 393224 | tf_op jit(solution)/shard_map/ppermute | solution.py:270
  15.6 17.6 %copy-start.7 = (bf16[128,512]{1,0:T(8,128)(2,1)}, bf16[128,512]{1,0:T(8,128)(2,1)S(1)}, u32[]{:S(2)}) copy-start(bf16[128,512]{1,0:T(8,128)(2,1)S(1)} %collective-permute-done.1.refs_0_) | copy-start | bytes 393220
  15.7 14.4 %collective-permute-start.7 = (bf16[128,512]{1,0:T(8,128)(2,1)}, bf16[128,512]{1,0:T(8,128)(2,1)S(1)}, u32[]{:S(2)}, u32[]{:S(2)}) collective-permute-start(bf16[128,512]{1,0:T(8,128)(2,1)} %get-tuple-element.45), channel_id=1, source_target_pairs={{0,2},{2,24},{4,6},{6,28},{8,10},{10,16},{12,14},{14,20},{16,18},{... | collective-permute-start | bytes 393224 | tf_op jit(solution)/shard_map/ppermute | solution.py:270
  17.1 15.5 %all-to-all-start = ((bf16[32,8,128]{2,1,0:T(8,128)(2,1)}), bf16[32,8,128]{2,1,0:T(8,128)(2,1)S(1)}, u32[]{:S(2)}, u32[]{:S(2)}) async-start(bf16[32,8,128]{2,1,0:T(8,128)(2,1)} %pack_keys.1), calls=%async_computation | async-start | bytes 131072 | tf_op jit(solution)/shard_map/all_to_all | solution.py:251
  22.9 10.4 %copy-start.8 = (bf16[128,512]{1,0:T(8,128)(2,1)}, bf16[128,512]{1,0:T(8,128)(2,1)S(1)}, u32[]{:S(2)}) copy-start(bf16[128,512]{1,0:T(8,128)(2,1)S(1)} %collective-permute-done.2.refs_1_) | copy-start | bytes 393220
  22.9 14.2 %collective-permute-start.8 = (bf16[128,512]{1,0:T(8,128)(2,1)}, bf16[128,512]{1,0:T(8,128)(2,1)S(1)}, u32[]{:S(2)}, u32[]{:S(2)}) collective-permute-start(bf16[128,512]{1,0:T(8,128)(2,1)} %get-tuple-element.46), channel_id=1, source_target_pairs={{0,28},{2,6},{4,24},{6,2},{8,20},{10,14},{12,16},{14,10},{16,12},{... | collective-permute-start | bytes 393224 | tf_op jit(solution)/shard_map/ppermute | solution.py:270
  27.5 5.7 %copy-start.9 = (bf16[128,512]{1,0:T(8,128)(2,1)}, bf16[128,512]{1,0:T(8,128)(2,1)S(1)}, u32[]{:S(2)}) copy-start(bf16[128,512]{1,0:T(8,128)(2,1)S(1)} %collective-permute-done.3.refs_2_) | copy-start | bytes 393220
  27.5 11.1 %collective-permute-start.9 = (bf16[128,512]{1,0:T(8,128)(2,1)}, bf16[128,512]{1,0:T(8,128)(2,1)S(1)}, u32[]{:S(2)}, u32[]{:S(2)}) collective-permute-start(bf16[128,512]{1,0:T(8,128)(2,1)} %get-tuple-element.47), channel_id=1, source_target_pairs={{0,6},{2,28},{4,2},{6,24},{8,14},{10,20},{12,10},{14,16},{16,22},{... | collective-permute-start | bytes 393224 | tf_op jit(solution)/shard_map/ppermute | solution.py:270
  27.5 5.7 %copy-start.10 = (bf16[128,512]{1,0:T(8,128)(2,1)}, bf16[128,512]{1,0:T(8,128)(2,1)S(1)}, u32[]{:S(2)}) copy-start(bf16[128,512]{1,0:T(8,128)(2,1)S(1)} %collective-permute-done.4.refs_3_) | copy-start | bytes 393220
  27.5 18.1 %collective-permute-start.12 = (bf16[128,512]{1,0:T(8,128)(2,1)}, bf16[128,512]{1,0:T(8,128)(2,1)S(1)}, u32[]{:S(2)}, u32[]{:S(2)}) collective-permute-start(bf16[128,512]{1,0:T(8,128)(2,1)} %get-tuple-element.54), channel_id=1, source_target_pairs={{0,8},{2,18},{4,12},{6,22},{8,0},{10,26},{12,4},{14,30},{16,24},{1... | collective-permute-start | bytes 393224 | tf_op jit(solution)/shard_map/ppermute | solution.py:270
  27.6 20.4 %collective-permute-start.13 = (bf16[128,512]{1,0:T(8,128)(2,1)}, bf16[128,512]{1,0:T(8,128)(2,1)S(1)}, u32[]{:S(2)}, u32[]{:S(2)}) collective-permute-start(bf16[128,512]{1,0:T(8,128)(2,1)} %get-tuple-element.55), channel_id=1, source_target_pairs={{0,18},{2,8},{4,22},{6,12},{8,26},{10,0},{12,30},{14,4},{16,2},{18... | collective-permute-start | bytes 393224 | tf_op jit(solution)/shard_map/ppermute | solution.py:270
  30.0 19.4 %collective-permute-start.14 = (bf16[128,512]{1,0:T(8,128)(2,1)}, bf16[128,512]{1,0:T(8,128)(2,1)S(1)}, u32[]{:S(2)}, u32[]{:S(2)}) collective-permute-start(bf16[128,512]{1,0:T(8,128)(2,1)} %get-tuple-element.56), channel_id=1, source_target_pairs={{0,12},{2,22},{4,8},{6,18},{8,4},{10,30},{12,0},{14,26},{16,28},{1... | collective-permute-start | bytes 393224 | tf_op jit(solution)/shard_map/ppermute | solution.py:270
  33.2 6.8 %copy-start = (bf16[2048,512]{1,0:T(8,128)(2,1)S(1)}, bf16[2048,512]{1,0:T(8,128)(2,1)}, u32[]{:S(2)}) copy-start(bf16[2048,512]{1,0:T(8,128)(2,1)} %refs_4_.7) | copy-start | bytes 6291460
  33.2 6.8 %copy-start.2 = (bf16[32,4,128]{2,1,0:T(4,128)(2,1)S(1)}, bf16[32,4,128]{2,1,0:T(4,128)(2,1)}, u32[]{:S(2)}) copy-start(bf16[32,4,128]{2,1,0:T(4,128)(2,1)} %get-tuple-element.67) | copy-start | bytes 98308
  33.3 6.7 %copy-start.3 = (bf16[32,4,128]{2,1,0:T(4,128)(2,1)S(1)}, bf16[32,4,128]{2,1,0:T(4,128)(2,1)}, u32[]{:S(2)}) copy-start(bf16[32,4,128]{2,1,0:T(4,128)(2,1)} %get-tuple-element.68) | copy-start | bytes 98308
  33.3 6.7 %copy-start.4 = (f32[4,2048]{1,0:T(4,128)S(1)}, f32[4,2048]{1,0:T(4,128)}, u32[]{:S(2)}) copy-start(f32[4,2048]{1,0:T(4,128)} %refs_6_.7) | copy-start | bytes 98308
  37.0 16.1 %collective-permute-start = (bf16[128,512]{1,0:T(8,128)(2,1)}, bf16[128,512]{1,0:T(8,128)(2,1)S(1)}, u32[]{:S(2)}, u32[]{:S(2)}) collective-permute-start(bf16[128,512]{1,0:T(8,128)(2,1)} %get-tuple-element.35), channel_id=1, source_target_pairs={{0,0},{2,26},{4,4},{6,30},{8,8},{10,18},{12,12},{14,22},{16,16},{1... | collective-permute-start | bytes 393224 | tf_op jit(solution)/shard_map/ppermute | solution.py:270
  38.6 12.2 %collective-permute-start.15 = (bf16[128,512]{1,0:T(8,128)(2,1)}, bf16[128,512]{1,0:T(8,128)(2,1)S(1)}, u32[]{:S(2)}, u32[]{:S(2)}) collective-permute-start(bf16[128,512]{1,0:T(8,128)(2,1)} %get-tuple-element.57), channel_id=1, source_target_pairs={{0,22},{2,12},{4,18},{6,8},{8,30},{10,4},{12,26},{14,0},{16,6},{18... | collective-permute-start | bytes 393224 | tf_op jit(solution)/shard_map/ppermute | solution.py:270
  40.0 1.6 %copy-start.1 = (bf16[2048,512]{1,0:T(8,128)(2,1)S(1)}, bf16[2048,512]{1,0:T(8,128)(2,1)}, u32[]{:S(2)}) copy-start(bf16[2048,512]{1,0:T(8,128)(2,1)} %refs_5_.7) | copy-start | bytes 6291460
  41.6 0.8 %copy-start.5 = (f32[128,128]{1,0:T(8,128)S(1)}, f32[128,128]{1,0:T(8,128)}, u32[]{:S(2)}) copy-start(f32[128,128]{1,0:T(8,128)} %get-tuple-element.41.refs_10_) | copy-start | bytes 196612
  42.4 0.8 %copy-start.6 = (f32[128,128]{1,0:T(8,128)S(1)}, f32[128,128]{1,0:T(8,128)}, u32[]{:S(2)}) copy-start(f32[128,128]{1,0:T(8,128)} %get-tuple-element.49.refs_11_) | copy-start | bytes 196612
  43.3 2.4 %copy-start.13 = (bf16[128,512]{1,0:T(8,128)(2,1)S(1)}, bf16[128,512]{1,0:T(8,128)(2,1)}, u32[]{:S(2)}) copy-start(bf16[128,512]{1,0:T(8,128)(2,1)} %get-tuple-element.42) | copy-start | bytes 393220
  43.3 4.7 %copy-start.12 = (bf16[128,512]{1,0:T(8,128)(2,1)S(1)}, bf16[128,512]{1,0:T(8,128)(2,1)}, u32[]{:S(2)}) copy-start(bf16[128,512]{1,0:T(8,128)(2,1)} %get-tuple-element.51) | copy-start | bytes 393220
  43.3 6.2 %copy-start.11 = (bf16[128,512]{1,0:T(8,128)(2,1)S(1)}, bf16[128,512]{1,0:T(8,128)(2,1)}, u32[]{:S(2)}) copy-start(bf16[128,512]{1,0:T(8,128)(2,1)} %get-tuple-element.53) | copy-start | bytes 393220
  45.6 7.5 %collective-permute-start.5 = (bf16[128,512]{1,0:T(8,128)(2,1)S(1)}, bf16[128,512]{1,0:T(8,128)(2,1)S(1)}, u32[]{:S(2)}, u32[]{:S(2)}) collective-permute-start(bf16[128,512]{1,0:T(8,128)(2,1)S(1)} %copy-done.13), channel_id=1, source_target_pairs={{0,26},{2,0},{4,30},{6,4},{8,18},{10,8},{12,22},{14,12},{16,10},{1... | collective-permute-start | bytes 393224 | tf_op jit(solution)/shard_map/ppermute | solution.py:270
  48.0 8.2 %collective-permute-start.10 = (bf16[128,512]{1,0:T(8,128)(2,1)S(1)}, bf16[128,512]{1,0:T(8,128)(2,1)S(1)}, u32[]{:S(2)}, u32[]{:S(2)}) collective-permute-start(bf16[128,512]{1,0:T(8,128)(2,1)S(1)} %copy-done.12), channel_id=1, source_target_pairs={{0,4},{2,30},{4,0},{6,26},{8,12},{10,22},{12,8},{14,18},{16,20},{1... | collective-permute-start | bytes 393224 | tf_op jit(solution)/shard_map/ppermute | solution.py:270
  49.5 7.7 %collective-permute-start.11 = (bf16[128,512]{1,0:T(8,128)(2,1)S(1)}, bf16[128,512]{1,0:T(8,128)(2,1)S(1)}, u32[]{:S(2)}, u32[]{:S(2)}) collective-permute-start(bf16[128,512]{1,0:T(8,128)(2,1)S(1)} %copy-done.11), channel_id=1, source_target_pairs={{0,30},{2,4},{4,26},{6,0},{8,22},{10,12},{12,18},{14,8},{16,14},{1... | collective-permute-start | bytes 393224 | tf_op jit(solution)/shard_map/ppermute | solution.py:270

commit v7 on v3

--- a/solution.py
+++ b/solution.py
@@ -200,7 +200,7 @@
         out_shape=out_shape,
         input_output_aliases=aliases,
         compiler_params=pltpu.CompilerParams(
-            vmem_limit_bytes=VMEM_LIMIT if first else SMALL_LIMIT
+            vmem_limit_bytes=SMALL_LIMIT
         ),
         cost_estimate=FREE,
         name=f"sources_{pairs[0][0]}",

time: 72.4 us -> 71.9 us (level)
  waiting for transfers between devices: 0.24 us -> 3.93 us
  local copies, waits for them, and re-layouts: 3.96 us -> 1.64 us
  Pallas kernels: 15.5 us -> 14.7 us
    ppermute x16, waiting for transfers between devices: 0.24 us -> 3.93 us  [send(): arrived.append(lax.ppermute(piece, 'head', pairs))]
    unnamed x30 -> x12, local copies, waits for them, and re-layouts: 3.32 us -> 1.61 us
    pallas_call x3, Pallas kernels: 10.8 us -> 9.93 us  [attention(): pl.pallas_call(functools.partial(attention_kernel, first, owners > 0, pai...]
  transfers between devices with their start and end apart: 17 -> 17, of which waited for: 1 -> 3; matrix products, arithmetic and copies ran while one was open for 1% -> 0% of each run, Pallas kernels for 13% -> 12%
where the time goes in v7:
time: 71.9 us; the launch traced here: 71.6 us
  starting transfers between devices  37.5 us (52%)
  Pallas kernels  14.7 us (20%)
  blocking collectives  13.1 us (18%)
  waiting for transfers between devices  3.93 us (5%)
  local copies, waits for them, and re-layouts  1.64 us (2%)
  between operations  0.76 us (1%)
    ppermute x16, starting transfers between devices, send(): arrived.append(lax.ppermute(piece, 'head', pairs))  31.7 us
    all_to_all x1, blocking collectives, on_device(): lax.all_to_all(terms, ('head', 'ctx'), split_axis=0, concat_axis=0, tiled...  13.1 us
    pallas_call x3, Pallas kernels, attention(): pl.pallas_call(functools.partial(attention_kernel, first, owners > 0, pai...  9.93 us
    all_to_all x1, starting transfers between devices, own_group(): lax.all_to_all(mine, ('head', 'ctx'), split_axis=0, concat_axis=0, tiled=...  5.78 us
    ppermute x16, waiting for transfers between devices, send(): arrived.append(lax.ppermute(piece, 'head', pairs))  3.93 us
    pallas_call x1, Pallas kernels, split(): pl.pallas_call(functools.partial(split_kernel, batches(dests)), in_specs=...  2.84 us
    unnamed x12, local copies, waits for them, and re-layouts  1.61 us
  transfers between devices with their start and end apart: 17, of which 3 were waited for; matrix products, arithmetic and copies ran while one was open for 0% of the time, Pallas kernels for 12%

profile of v7, /device:TPU:0, one launch (start us, length us, event | category | flops | bytes accessed | tf_op | source)
XLA Modules:
  0.0 71.6 jit_solution(13507409111716231552)
XLA Ops:
  0.6 0.0 copy-start.2
  0.6 0.0 copy-start
  0.7 2.8 %split.1 = (bf16[128,512]{1,0:T(8,128)(2,1)}, bf16[128,512]{1,0:T(8,128)(2,1)}, bf16[128,512]{1,0:T(8,128)(2,1)}, bf16[128,512]{1,0:T(8,128)(2,1)}, bf16[128,512...) custom-call(bf16[128,8192]{1,0:T(8,128)(2,1)} %dout_ref.1), custom_call_target="tpu_custom_call" | custom-call | tf_op jit(solution)/shard_map/split/pallas_call | solution.py:70
  3.5 4.1 %collective-permute-start.1 = (bf16[128,512]{1,0:T(8,128)(2,1)}, bf16[128,512]{1,0:T(8,128)(2,1)S(1)}, u32[]{:S(2)}, u32[]{:S(2)}) collective-permute-start(bf16[128,512]{1,0:T(8,128)(2,1)} %get-tuple-element.34), channel_id=1, source_target_pairs={{0,16},{2,10},{4,20},{6,14},{8,24},{10,2},{12,28},{14,6},{16,0},{1... | collective-permute-start | bytes 393224 | tf_op jit(solution)/shard_map/ppermute | solution.py:270
  7.6 0.0 collective-permute-start.2
  7.6 2.1 %collective-permute-start.3 = (bf16[128,512]{1,0:T(8,128)(2,1)}, bf16[128,512]{1,0:T(8,128)(2,1)S(1)}, u32[]{:S(2)}, u32[]{:S(2)}) collective-permute-start(bf16[128,512]{1,0:T(8,128)(2,1)} %get-tuple-element.36), channel_id=1, source_target_pairs={{0,20},{2,14},{4,16},{6,10},{8,28},{10,6},{12,24},{14,2},{16,4},{1... | collective-permute-start | bytes 393224 | tf_op jit(solution)/shard_map/ppermute | solution.py:270
  9.7 0.5 collective-permute-start.4
  10.2 5.6 %collective-permute-start.5 = (bf16[128,512]{1,0:T(8,128)(2,1)}, bf16[128,512]{1,0:T(8,128)(2,1)S(1)}, u32[]{:S(2)}, u32[]{:S(2)}) collective-permute-start(bf16[128,512]{1,0:T(8,128)(2,1)} %get-tuple-element.38), channel_id=1, source_target_pairs={{0,24},{2,2},{4,28},{6,6},{8,16},{10,10},{12,20},{14,14},{16,8},{1... | collective-permute-start | bytes 393224 | tf_op jit(solution)/shard_map/ppermute | solution.py:270
  15.8 0.0 collective-permute-done.1.refs_0_
  15.8 0.1 collective-permute-start.6
  15.9 1.3 %pack_keys.1 = bf16[32,8,128]{2,1,0:T(8,128)(2,1)} custom-call(bf16[4,512]{1,0:T(4,128)(2,1)} %k_ref.1, bf16[4,512]{1,0:T(4,128)(2,1)} %v_ref.1), custom_call_target="tpu_custom_call" | custom-call | tf_op jit(solution)/shard_map/pack_keys/pallas_call | solution.py:245
  17.2 5.8 %all-to-all-start = ((bf16[32,8,128]{2,1,0:T(8,128)(2,1)}), bf16[32,8,128]{2,1,0:T(8,128)(2,1)S(1)}, u32[]{:S(2)}, u32[]{:S(2)}) async-start(bf16[32,8,128]{2,1,0:T(8,128)(2,1)} %pack_keys.1), calls=%async_computation | async-start | bytes 131072 | tf_op jit(solution)/shard_map/all_to_all | solution.py:251
  23.0 0.0 collective-permute-done.2.refs_1_
  23.0 4.6 %collective-permute-start.7 = (bf16[128,512]{1,0:T(8,128)(2,1)}, bf16[128,512]{1,0:T(8,128)(2,1)S(1)}, u32[]{:S(2)}, u32[]{:S(2)}) collective-permute-start(bf16[128,512]{1,0:T(8,128)(2,1)} %get-tuple-element.40), channel_id=1, source_target_pairs={{0,28},{2,6},{4,24},{6,2},{8,20},{10,14},{12,16},{14,10},{16,12},{... | collective-permute-start | bytes 393224 | tf_op jit(solution)/shard_map/ppermute | solution.py:270
  27.6 0.0 collective-permute-done.3.refs_2_
  27.6 0.0 collective-permute-start.8
  27.6 0.0 collective-permute-done.4.refs_3_
  27.6 0.1 collective-permute-start.12
  27.7 0.0 collective-permute-done.5.refs_4_
  27.7 2.5 %collective-permute-start.13 = (bf16[128,512]{1,0:T(8,128)(2,1)}, bf16[128,512]{1,0:T(8,128)(2,1)S(1)}, u32[]{:S(2)}, u32[]{:S(2)}) collective-permute-start(bf16[128,512]{1,0:T(8,128)(2,1)} %get-tuple-element.49), channel_id=1, source_target_pairs={{0,18},{2,8},{4,22},{6,12},{8,26},{10,0},{12,30},{14,4},{16,2},{18... | collective-permute-start | bytes 393224 | tf_op jit(solution)/shard_map/ppermute | solution.py:270
  30.2 0.0 collective-permute-done.6.refs_5_
  30.2 2.5 %collective-permute-start.14 = (bf16[128,512]{1,0:T(8,128)(2,1)}, bf16[128,512]{1,0:T(8,128)(2,1)S(1)}, u32[]{:S(2)}, u32[]{:S(2)}) collective-permute-start(bf16[128,512]{1,0:T(8,128)(2,1)} %get-tuple-element.50), channel_id=1, source_target_pairs={{0,12},{2,22},{4,8},{6,18},{8,4},{10,30},{12,0},{14,26},{16,28},{1... | collective-permute-start | bytes 393224 | tf_op jit(solution)/shard_map/ppermute | solution.py:270
  32.7 0.0 all-to-all-done
  32.7 0.0 collective-permute-done.7.refs_6_
  32.7 1.6 %collective-permute-start = (bf16[128,512]{1,0:T(8,128)(2,1)}, bf16[128,512]{1,0:T(8,128)(2,1)S(1)}, u32[]{:S(2)}, u32[]{:S(2)}) collective-permute-start(bf16[128,512]{1,0:T(8,128)(2,1)} %get-tuple-element.32), channel_id=1, source_target_pairs={{0,0},{2,26},{4,4},{6,30},{8,8},{10,18},{12,12},{14,22},{16,16},{1... | collective-permute-start | bytes 393224 | tf_op jit(solution)/shard_map/ppermute | solution.py:270
  34.3 0.9 %collective-permute-done.8.refs_7_ = bf16[128,512]{1,0:T(8,128)(2,1)} collective-permute-done((bf16[128,512]{1,0:T(8,128)(2,1)}, bf16[128,512]{1,0:T(8,128)(2,1)}, u32[]{:S(2)}, u32[]{:S(2)}) %collective-permute-start.8) | collective-permute-done | bytes 131104 | tf_op jit(solution)/shard_map/ppermute | solution.py:270
  35.2 0.5 collective-permute-start.15
  35.7 0.0 copy-done.2
  35.7 0.0 copy-done
  35.7 1.6 %copy-done.1 = bf16[2048,512]{1,0:T(8,128)(2,1)S(1)} copy-done((bf16[2048,512]{1,0:T(8,128)(2,1)S(1)}, bf16[2048,512]{1,0:T(8,128)(2,1)}, u32[]{:S(2)}) %copy-start.1) | copy-done | bytes 2097176
  37.3 5.1 %sources_8.1 = (bf16[2048,512]{1,0:T(8,128)(2,1)}, f32[128,128]{1,0:T(8,128)S(1)}, f32[128,128]{1,0:T(8,128)S(1)}) custom-call(s32[1]{0:T(128)} %bitcast.place_ref, bf16[128,512]{1,0:T(8,128)(2,1)S(1)} %collective-permute-done.1.refs_0_, bf16[128,512]{1,0:T(8,128)(2,1)S(1)} %collective-permute-done.2.refs_1_, ...), custom_call_target="tpu_custom_call" | custom-call | tf_op jit(solution)/shard_map/sources_8/pallas_call | solution.py:191
  42.4 0.0 collective-permute-done.12.refs_0_
  42.4 0.0 copy-done.5
  42.4 5.4 %collective-permute-start.9 = (bf16[128,512]{1,0:T(8,128)(2,1)S(1)}, bf16[128,512]{1,0:T(8,128)(2,1)S(1)}, u32[]{:S(2)}, u32[]{:S(2)}) collective-permute-start(bf16[128,512]{1,0:T(8,128)(2,1)S(1)} %copy-done.5), channel_id=1, source_target_pairs={{0,26},{2,0},{4,30},{6,4},{8,18},{10,8},{12,22},{14,12},{16,10},{1... | collective-permute-start | bytes 393224 | tf_op jit(solution)/shard_map/ppermute | solution.py:270
  47.8 0.0 collective-permute-done.13.refs_1_
  47.8 0.0 copy-done.4
  47.8 2.2 %collective-permute-start.10 = (bf16[128,512]{1,0:T(8,128)(2,1)S(1)}, bf16[128,512]{1,0:T(8,128)(2,1)S(1)}, u32[]{:S(2)}, u32[]{:S(2)}) collective-permute-start(bf16[128,512]{1,0:T(8,128)(2,1)S(1)} %copy-done.4), channel_id=1, source_target_pairs={{0,4},{2,30},{4,0},{6,26},{8,12},{10,22},{12,8},{14,18},{16,20},{1... | collective-permute-start | bytes 393224 | tf_op jit(solution)/shard_map/ppermute | solution.py:270
  50.1 0.0 collective-permute-done.14.refs_2_
  50.1 0.0 collective-permute-start.11
  50.1 0.0 collective-permute-done.15.refs_3_
  50.1 2.4 %sources_4.1 = (bf16[2048,512]{1,0:T(8,128)(2,1)}, f32[128,128]{1,0:T(8,128)S(1)}, f32[128,128]{1,0:T(8,128)S(1)}) custom-call(s32[1]{0:T(128)} %bitcast.place_ref, bf16[128,512]{1,0:T(8,128)(2,1)S(1)} %collective-permute-done.12.refs_0_, bf16[128,512]{1,0:T(8,128)(2,1)S(1)} %collective-permute-done.13.refs_1_, ...), custom_call_target="tpu_custom_call", output_to_operand_aliasing={{0}: (10, {})} | custom-call | tf_op jit(solution)/shard_map/sources_4/pallas_call | solution.py:191
  52.5 0.0 collective-permute-done.refs_0_
  52.5 0.0 collective-permute-done.9.refs_1_
  52.5 2.5 %collective-permute-done.10.refs_2_ = bf16[128,512]{1,0:T(8,128)(2,1)S(1)} collective-permute-done((bf16[128,512]{1,0:T(8,128)(2,1)S(1)}, bf16[128,512]{1,0:T(8,128)(2,1)S(1)}, u32[]{:S(2)}, u32[]{:S(2)}) %collective-permute-start.10) | collective-permute-done | bytes 131104 | tf_op jit(solution)/shard_map/ppermute | solution.py:270
  55.0 0.5 collective-permute-done.11.refs_3_
  55.5 2.4 %sources_0.1 = (bf16[2048,512]{1,0:T(8,128)(2,1)}, f32[32,8,128]{2,1,0:T(8,128)S(1)}) custom-call(s32[1]{0:T(128)} %bitcast.place_ref, bf16[128,512]{1,0:T(8,128)(2,1)S(1)} %collective-permute-done.refs_0_, bf16[128,512]{1,0:T(8,128)(2,1)S(1)} %collective-permute-done.9.refs_1_, ...), custom_call_target="tpu_custom_call", output_to_operand_aliasing={{0}: (10, {})} | custom-call | tf_op jit(solution)/shard_map/sources_0/pallas_call | solution.py:191
  57.9 13.1 %all_to_all.10.terms_ref = f32[32,8,128]{2,1,0:T(8,128)S(1)} all-to-all(f32[32,8,128]{2,1,0:T(8,128)S(1)} %get-tuple-element.58), channel_id=1, replica_groups=mesh['head'=16,'ctx'=2] {'head','ctx'}, dimensions={0} | all-to-all | bytes 262144 | tf_op jit(solution)/shard_map/all_to_all | solution.py:302
  71.0 0.6 sum_terms.1
  (6 shorter events, 0.0 us)
Async XLA Ops:
  0.6 35.1 %copy-start.2 = (f32[4,2048]{1,0:T(4,128)S(1)}, f32[4,2048]{1,0:T(4,128)}, u32[]{:S(2)}) copy-start(f32[4,2048]{1,0:T(4,128)} %refs_6_.3) | copy-start | bytes 98308
  0.6 35.1 %copy-start = (bf16[2048,512]{1,0:T(8,128)(2,1)S(1)}, bf16[2048,512]{1,0:T(8,128)(2,1)}, u32[]{:S(2)}) copy-start(bf16[2048,512]{1,0:T(8,128)(2,1)} %refs_4_.3) | copy-start | bytes 6291460
  3.5 12.3 %collective-permute-start.1 = (bf16[128,512]{1,0:T(8,128)(2,1)}, bf16[128,512]{1,0:T(8,128)(2,1)S(1)}, u32[]{:S(2)}, u32[]{:S(2)}) collective-permute-start(bf16[128,512]{1,0:T(8,128)(2,1)} %get-tuple-element.34), channel_id=1, source_target_pairs={{0,16},{2,10},{4,20},{6,14},{8,24},{10,2},{12,28},{14,6},{16,0},{1... | collective-permute-start | bytes 393224 | tf_op jit(solution)/shard_map/ppermute | solution.py:270
  7.6 15.4 %collective-permute-start.2 = (bf16[128,512]{1,0:T(8,128)(2,1)}, bf16[128,512]{1,0:T(8,128)(2,1)S(1)}, u32[]{:S(2)}, u32[]{:S(2)}) collective-permute-start(bf16[128,512]{1,0:T(8,128)(2,1)} %get-tuple-element.35), channel_id=1, source_target_pairs={{0,10},{2,16},{4,14},{6,20},{8,2},{10,24},{12,6},{14,28},{16,26},{... | collective-permute-start | bytes 393224 | tf_op jit(solution)/shard_map/ppermute | solution.py:270
  7.6 20.0 %collective-permute-start.3 = (bf16[128,512]{1,0:T(8,128)(2,1)}, bf16[128,512]{1,0:T(8,128)(2,1)S(1)}, u32[]{:S(2)}, u32[]{:S(2)}) collective-permute-start(bf16[128,512]{1,0:T(8,128)(2,1)} %get-tuple-element.36), channel_id=1, source_target_pairs={{0,20},{2,14},{4,16},{6,10},{8,28},{10,6},{12,24},{14,2},{16,4},{1... | collective-permute-start | bytes 393224 | tf_op jit(solution)/shard_map/ppermute | solution.py:270
  9.7 17.9 %collective-permute-start.4 = (bf16[128,512]{1,0:T(8,128)(2,1)}, bf16[128,512]{1,0:T(8,128)(2,1)S(1)}, u32[]{:S(2)}, u32[]{:S(2)}) collective-permute-start(bf16[128,512]{1,0:T(8,128)(2,1)} %get-tuple-element.37), channel_id=1, source_target_pairs={{0,14},{2,20},{4,10},{6,16},{8,6},{10,28},{12,2},{14,24},{16,30},{... | collective-permute-start | bytes 393224 | tf_op jit(solution)/shard_map/ppermute | solution.py:270
  10.2 17.5 %collective-permute-start.5 = (bf16[128,512]{1,0:T(8,128)(2,1)}, bf16[128,512]{1,0:T(8,128)(2,1)S(1)}, u32[]{:S(2)}, u32[]{:S(2)}) collective-permute-start(bf16[128,512]{1,0:T(8,128)(2,1)} %get-tuple-element.38), channel_id=1, source_target_pairs={{0,24},{2,2},{4,28},{6,6},{8,16},{10,10},{12,20},{14,14},{16,8},{1... | collective-permute-start | bytes 393224 | tf_op jit(solution)/shard_map/ppermute | solution.py:270
  15.8 14.4 %collective-permute-start.6 = (bf16[128,512]{1,0:T(8,128)(2,1)}, bf16[128,512]{1,0:T(8,128)(2,1)S(1)}, u32[]{:S(2)}, u32[]{:S(2)}) collective-permute-start(bf16[128,512]{1,0:T(8,128)(2,1)} %get-tuple-element.39), channel_id=1, source_target_pairs={{0,2},{2,24},{4,6},{6,28},{8,10},{10,16},{12,14},{14,20},{16,18},{... | collective-permute-start | bytes 393224 | tf_op jit(solution)/shard_map/ppermute | solution.py:270
  17.2 15.5 %all-to-all-start = ((bf16[32,8,128]{2,1,0:T(8,128)(2,1)}), bf16[32,8,128]{2,1,0:T(8,128)(2,1)S(1)}, u32[]{:S(2)}, u32[]{:S(2)}) async-start(bf16[32,8,128]{2,1,0:T(8,128)(2,1)} %pack_keys.1), calls=%async_computation | async-start | bytes 131072 | tf_op jit(solution)/shard_map/all_to_all | solution.py:251
  23.0 9.7 %collective-permute-start.7 = (bf16[128,512]{1,0:T(8,128)(2,1)}, bf16[128,512]{1,0:T(8,128)(2,1)S(1)}, u32[]{:S(2)}, u32[]{:S(2)}) collective-permute-start(bf16[128,512]{1,0:T(8,128)(2,1)} %get-tuple-element.40), channel_id=1, source_target_pairs={{0,28},{2,6},{4,24},{6,2},{8,20},{10,14},{12,16},{14,10},{16,12},{... | collective-permute-start | bytes 393224 | tf_op jit(solution)/shard_map/ppermute | solution.py:270
  27.6 7.6 %collective-permute-start.8 = (bf16[128,512]{1,0:T(8,128)(2,1)}, bf16[128,512]{1,0:T(8,128)(2,1)}, u32[]{:S(2)}, u32[]{:S(2)}) collective-permute-start(bf16[128,512]{1,0:T(8,128)(2,1)} %get-tuple-element.41), channel_id=1, source_target_pairs={{0,6},{2,28},{4,2},{6,24},{8,14},{10,20},{12,10},{14,16},{16,22},{... | collective-permute-start | bytes 393224 | tf_op jit(solution)/shard_map/ppermute | solution.py:270
  27.6 14.7 %collective-permute-start.12 = (bf16[128,512]{1,0:T(8,128)(2,1)}, bf16[128,512]{1,0:T(8,128)(2,1)S(1)}, u32[]{:S(2)}, u32[]{:S(2)}) collective-permute-start(bf16[128,512]{1,0:T(8,128)(2,1)} %get-tuple-element.48), channel_id=1, source_target_pairs={{0,8},{2,18},{4,12},{6,22},{8,0},{10,26},{12,4},{14,30},{16,24},{1... | collective-permute-start | bytes 393224 | tf_op jit(solution)/shard_map/ppermute | solution.py:270
  27.7 20.1 %collective-permute-start.13 = (bf16[128,512]{1,0:T(8,128)(2,1)}, bf16[128,512]{1,0:T(8,128)(2,1)S(1)}, u32[]{:S(2)}, u32[]{:S(2)}) collective-permute-start(bf16[128,512]{1,0:T(8,128)(2,1)} %get-tuple-element.49), channel_id=1, source_target_pairs={{0,18},{2,8},{4,22},{6,12},{8,26},{10,0},{12,30},{14,4},{16,2},{18... | collective-permute-start | bytes 393224 | tf_op jit(solution)/shard_map/ppermute | solution.py:270
  30.2 19.9 %collective-permute-start.14 = (bf16[128,512]{1,0:T(8,128)(2,1)}, bf16[128,512]{1,0:T(8,128)(2,1)S(1)}, u32[]{:S(2)}, u32[]{:S(2)}) collective-permute-start(bf16[128,512]{1,0:T(8,128)(2,1)} %get-tuple-element.50), channel_id=1, source_target_pairs={{0,12},{2,22},{4,8},{6,18},{8,4},{10,30},{12,0},{14,26},{16,28},{1... | collective-permute-start | bytes 393224 | tf_op jit(solution)/shard_map/ppermute | solution.py:270
  32.7 19.7 %collective-permute-start = (bf16[128,512]{1,0:T(8,128)(2,1)}, bf16[128,512]{1,0:T(8,128)(2,1)S(1)}, u32[]{:S(2)}, u32[]{:S(2)}) collective-permute-start(bf16[128,512]{1,0:T(8,128)(2,1)} %get-tuple-element.32), channel_id=1, source_target_pairs={{0,0},{2,26},{4,4},{6,30},{8,8},{10,18},{12,12},{14,22},{16,16},{1... | collective-permute-start | bytes 393224 | tf_op jit(solution)/shard_map/ppermute | solution.py:270
  35.2 14.8 %collective-permute-start.15 = (bf16[128,512]{1,0:T(8,128)(2,1)}, bf16[128,512]{1,0:T(8,128)(2,1)S(1)}, u32[]{:S(2)}, u32[]{:S(2)}) collective-permute-start(bf16[128,512]{1,0:T(8,128)(2,1)} %get-tuple-element.51), channel_id=1, source_target_pairs={{0,22},{2,12},{4,18},{6,8},{8,30},{10,4},{12,26},{14,0},{16,6},{18... | collective-permute-start | bytes 393224 | tf_op jit(solution)/shard_map/ppermute | solution.py:270
  35.7 1.6 %copy-start.1 = (bf16[2048,512]{1,0:T(8,128)(2,1)S(1)}, bf16[2048,512]{1,0:T(8,128)(2,1)}, u32[]{:S(2)}) copy-start(bf16[2048,512]{1,0:T(8,128)(2,1)} %refs_5_.3) | copy-start | bytes 6291460
  37.3 5.1 %copy-start.5 = (bf16[128,512]{1,0:T(8,128)(2,1)S(1)}, bf16[128,512]{1,0:T(8,128)(2,1)}, u32[]{:S(2)}) copy-start(bf16[128,512]{1,0:T(8,128)(2,1)} %get-tuple-element.43) | copy-start | bytes 393220
  37.3 10.5 %copy-start.4 = (bf16[128,512]{1,0:T(8,128)(2,1)S(1)}, bf16[128,512]{1,0:T(8,128)(2,1)}, u32[]{:S(2)}) copy-start(bf16[128,512]{1,0:T(8,128)(2,1)} %get-tuple-element.45) | copy-start | bytes 393220
  37.3 12.8 %copy-start.3 = (bf16[128,512]{1,0:T(8,128)(2,1)S(1)}, bf16[128,512]{1,0:T(8,128)(2,1)}, u32[]{:S(2)}) copy-start(bf16[128,512]{1,0:T(8,128)(2,1)} %get-tuple-element.47) | copy-start | bytes 393220
  42.4 10.1 %collective-permute-start.9 = (bf16[128,512]{1,0:T(8,128)(2,1)S(1)}, bf16[128,512]{1,0:T(8,128)(2,1)S(1)}, u32[]{:S(2)}, u32[]{:S(2)}) collective-permute-start(bf16[128,512]{1,0:T(8,128)(2,1)S(1)} %copy-done.5), channel_id=1, source_target_pairs={{0,26},{2,0},{4,30},{6,4},{8,18},{10,8},{12,22},{14,12},{16,10},{1... | collective-permute-start | bytes 393224 | tf_op jit(solution)/shard_map/ppermute | solution.py:270
  47.8 7.2 %collective-permute-start.10 = (bf16[128,512]{1,0:T(8,128)(2,1)S(1)}, bf16[128,512]{1,0:T(8,128)(2,1)S(1)}, u32[]{:S(2)}, u32[]{:S(2)}) collective-permute-start(bf16[128,512]{1,0:T(8,128)(2,1)S(1)} %copy-done.4), channel_id=1, source_target_pairs={{0,4},{2,30},{4,0},{6,26},{8,12},{10,22},{12,8},{14,18},{16,20},{1... | collective-permute-start | bytes 393224 | tf_op jit(solution)/shard_map/ppermute | solution.py:270
  50.1 5.4 %collective-permute-start.11 = (bf16[128,512]{1,0:T(8,128)(2,1)S(1)}, bf16[128,512]{1,0:T(8,128)(2,1)S(1)}, u32[]{:S(2)}, u32[]{:S(2)}) collective-permute-start(bf16[128,512]{1,0:T(8,128)(2,1)S(1)} %copy-done.3), channel_id=1, source_target_pairs={{0,30},{2,4},{4,26},{6,0},{8,22},{10,12},{12,18},{14,8},{16,14},{1... | collective-permute-start | bytes 393224 | tf_op jit(solution)/shard_map/ppermute | solution.py:270
